TPU v7x, 32 devices: a whole 2x2x4 slice. The times are simulated.
32 devices in a mesh: leaf: 8 (over y, x, core), path: 4 (over z).
Axes of the slice: x: 2, y: 2, z: 4, core: 2. Of those that a mesh axis runs over, the one named last changes fastest.
Arguments:
- tokens: bfloat16 [8, 2048, 768], P('leaf', 'path'), may hold values from -6 to 6
- encoded: bfloat16 [8, 1024, 768], P('leaf', 'path'), may hold values from -6 to 6
- cotangent: bfloat16 [8, 2048, 768], P('leaf', 'path'), may hold values from -6 to 6
- parent: int32 [8, 16], P('leaf'), may hold values from 0 to 14, as said below
- assignment: int32 [8, 16], P('leaf'), may hold values from 0 to 15, each once within a row
- attn_in: bfloat16 [6, 768, 768], P(None, ('leaf', 'path')), may hold values from -0.21875 to 0.21875
- attn_out: bfloat16 [2, 768, 768], P(None, ('leaf', 'path')), may hold values from -2.5 to 2.5
- ffn_in: bfloat16 [768, 3072], P(('leaf', 'path')), may hold values from -0.21875 to 0.21875
- ffn_out: bfloat16 [3072, 768], P(('leaf', 'path')), may hold values from -0.109375 to 0.109375
- shifts: bfloat16 [10, 768], P(None, ('leaf', 'path')), may hold values from -0.3984375 to 0.3984375
- gains: bfloat16 [3, 768], P(None, ('leaf', 'path')), may hold values from 0.5 to 1.5
- ffn_bias: bfloat16 [3072], P(('leaf', 'path')), may hold values from -0.5 to 0.5
Outputs:
- output: bfloat16 [8, 2048, 768], P('leaf', 'path')
- grad_tokens: float32 [8, 2048, 768], P('leaf', 'path')
- grad_encoded: float32 [8, 1024, 768], P('leaf', 'path')
- grad_attn_in: float32 [6, 768, 768], P(None, ('leaf', 'path'))
- grad_attn_out: float32 [2, 768, 768], P(None, ('leaf', 'path'))
- grad_ffn_in: float32 [768, 3072], P(('leaf', 'path'))
- grad_ffn_out: float32 [3072, 768], P(('leaf', 'path'))
- grad_shifts: float32 [10, 768], P(None, ('leaf', 'path'))
- grad_gains: float32 [3, 768], P(None, ('leaf', 'path'))
- gradient_feedforward_bias: float32 [3072], P(('leaf', 'path'))
Inputs may be any that keep to these rules, and one draw needn't show every extreme that they name: Entry 0 of each tree is 0 (the root); every other block's parent is one of the three blocks before it, or block 0; block 15 continues block 14. `assignment`: each tree's entries are a permutation of 0 to 15.
All inputs are finite; a program needn't handle non-finite values.
Results may differ from a plain program's by a relative error of at most 0.02.
Values may be sent and summed in bfloat16 or wider, within the bound.
A program may use at most 192 MiB of HBM per device.

v0:
```python
import jax
import jax.numpy as jnp
from jax import lax
from jax.sharding import PartitionSpec as P

HEAD = 64
BLK = 128


def layer_norm(values, norm_gain, norm_shift):
    centre = values - jnp.mean(values, axis=-1, keepdims=True)
    spread = jnp.mean(centre * centre, axis=-1, keepdims=True)
    return centre * lax.rsqrt(spread + 1e-05) * norm_gain + norm_shift


def gelu_exact(values):
    return 0.5 * values * (1.0 + jax.scipy.special.erf(values * 0.7071067811865476))


def slot_links(parent, assignment):
    block_count = parent.shape[1]
    blocks = jnp.arange(block_count, dtype=jnp.int32)
    upward = (parent[:, :, None] == blocks[None, None, :]) & (blocks[:, None] != blocks[None, :])[
        None
    ]
    reached_ancestor = upward.astype(jnp.float32)
    for sweep_turn in range(block_count.bit_length()):
        reached_ancestor = jnp.minimum(
            reached_ancestor
            + jnp.einsum(
                "fjd,fdz->fjz", reached_ancestor, reached_ancestor, precision=lax.Precision.HIGHEST
            ),
            1.0,
        )
    placed = (assignment[:, :, None] == blocks[None, None, :]).astype(jnp.float32)
    linked = jnp.einsum("tsa,tab->tsb", placed, reached_ancestor, precision=lax.Precision.HIGHEST)
    return jnp.einsum("tsb,trb->tsr", linked, placed, precision=lax.Precision.HIGHEST)


def visible(linked, first_query, query_count, key_count):
    slot_ids = jnp.arange(linked.shape[1], dtype=jnp.int32)
    query_pos = first_query + jnp.arange(query_count, dtype=jnp.int32)
    key_pos = jnp.arange(key_count, dtype=jnp.int32)
    query_pick = (query_pos[:, None] // BLK == slot_ids[None, :]).astype(jnp.float32)
    key_pick = (key_pos[:, None] // BLK == slot_ids[None, :]).astype(jnp.float32)
    ancestral = jnp.einsum("qa,tab->tqb", query_pick, linked, precision=lax.Precision.HIGHEST)
    ancestral = jnp.einsum("tqb,kb->tqk", ancestral, key_pick, precision=lax.Precision.HIGHEST)
    inside = (query_pos[:, None] // BLK == key_pos[None, :] // BLK) & (
        key_pos[None, :] <= query_pos[:, None]
    )
    return (ancestral > 0.5) | inside[None]


def project(activations, matrix):
    return jnp.einsum("trd,de->tre", activations, matrix, preferred_element_type=jnp.float32)


def project_back(gradients, matrix):
    return jnp.einsum("tre,de->trd", gradients, matrix, preferred_element_type=jnp.float32)


def weight_grad(activations, gradients):
    return jnp.einsum("trd,tre->de", activations, gradients, preferred_element_type=jnp.float32)


def column_sum(gradients):
    return jnp.sum(gradients.astype(jnp.float32), axis=(0, 1))


def split_pair(matrix, offset):
    piece = lax.dynamic_slice_in_dim(matrix, offset, 2 * HEAD, 2)
    return piece.reshape(piece.shape[0], piece.shape[1], 2, HEAD)


def attend_forward(queries, key_rows, value_rows, allowed):
    groups, query_count, feature_count = queries.shape

    def per_pair(pair_index, state_pair):
        merged, log_mass = state_pair
        offset = pair_index * 2 * HEAD
        scores = jnp.einsum(
            "tqhe,tkhe->thqk",
            split_pair(queries, offset),
            split_pair(key_rows, offset),
            preferred_element_type=jnp.float32,
        )
        if allowed is not None:
            scores = jnp.where(allowed[:, None], scores, -1e30)
        row_peak = jnp.max(scores, axis=3, keepdims=True)
        raised = jnp.exp(scores - row_peak)
        row_mass = jnp.sum(raised, axis=3, keepdims=True)
        weights = (raised / row_mass).astype(jnp.bfloat16)
        pair_out = jnp.einsum(
            "thqk,tkhe->tqhe",
            weights,
            split_pair(value_rows, offset),
            preferred_element_type=jnp.float32,
        )
        merged = lax.dynamic_update_slice_in_dim(
            merged, pair_out.reshape(groups, query_count, 2 * HEAD), offset, 2
        )
        log_mass = lax.dynamic_update_slice_in_dim(
            log_mass, (row_peak + jnp.log(row_mass))[..., 0], 2 * pair_index, 1
        )
        return (merged, log_mass)

    initial = (
        jnp.zeros((groups, query_count, feature_count), jnp.float32),
        jnp.zeros((groups, feature_count // HEAD, query_count), jnp.float32),
    )
    return lax.fori_loop(0, feature_count // (2 * HEAD), per_pair, initial)


def attend_back(queries, key_rows, value_rows, allowed, log_mass, grad_mixed):
    groups, query_count, feature_count = queries.shape
    key_count = key_rows.shape[1]

    def per_pair(pair_index, state_pair):
        grad_queries, grad_keys, grad_values, delta_rows = state_pair
        offset = pair_index * 2 * HEAD
        query_pair = split_pair(queries, offset)
        key_pair = split_pair(key_rows, offset)
        grad_pair = split_pair(grad_mixed, offset)
        scores = jnp.einsum(
            "tqhe,tkhe->thqk", query_pair, key_pair, preferred_element_type=jnp.float32
        )
        if allowed is not None:
            scores = jnp.where(allowed[:, None], scores, -1e30)
        probs = jnp.exp(
            scores - lax.dynamic_slice_in_dim(log_mass, 2 * pair_index, 2, 1)[..., None]
        )
        grad_probs = jnp.einsum(
            "tqhe,tkhe->thqk",
            grad_pair,
            split_pair(value_rows, offset),
            preferred_element_type=jnp.float32,
        )
        delta_pair = jnp.sum(probs * grad_probs, axis=3)
        delta_rows = lax.dynamic_update_slice_in_dim(delta_rows, delta_pair, 2 * pair_index, 1)
        grad_scores = (probs * (grad_probs - delta_pair[..., None])).astype(jnp.bfloat16)
        query_term = jnp.einsum(
            "thqk,tkhe->tqhe", grad_scores, key_pair, preferred_element_type=jnp.float32
        )
        grad_queries = lax.dynamic_update_slice_in_dim(
            grad_queries, query_term.reshape(groups, query_count, 2 * HEAD), offset, 2
        )
        key_term = jnp.einsum(
            "thqk,tqhe->tkhe", grad_scores, query_pair, preferred_element_type=jnp.float32
        )
        value_term = jnp.einsum(
            "thqk,tqhe->tkhe",
            probs.astype(jnp.bfloat16),
            grad_pair,
            preferred_element_type=jnp.float32,
        )
        grad_keys = lax.dynamic_update_slice_in_dim(
            grad_keys, key_term.reshape(groups, key_count, 2 * HEAD), offset, 2
        )
        grad_values = lax.dynamic_update_slice_in_dim(
            grad_values, value_term.reshape(groups, key_count, 2 * HEAD), offset, 2
        )
        return (grad_queries, grad_keys, grad_values, delta_rows)

    query_start = jnp.zeros((groups, query_count, feature_count), jnp.float32)
    key_start = jnp.zeros((groups, key_count, feature_count), jnp.float32)
    initial = (
        query_start,
        key_start,
        key_start,
        jnp.zeros((groups, feature_count // HEAD, query_count), jnp.float32),
    )
    return lax.fori_loop(0, feature_count // (2 * HEAD), per_pair, initial)


def body(
    tokens,
    encoded,
    cotangent,
    parent,
    assignment,
    attn_in,
    attn_out,
    ffn_in,
    ffn_out,
    shifts,
    gains,
    ffn_bias,
):
    score_scale = HEAD ** (-0.5)
    gathered = (
        lax.all_gather(attn_in, ("leaf", "path"), axis=1, tiled=True),
        lax.all_gather(attn_out, ("leaf", "path"), axis=1, tiled=True),
        lax.all_gather(shifts, ("leaf", "path"), axis=1, tiled=True),
        lax.all_gather(gains, ("leaf", "path"), axis=1, tiled=True),
        lax.all_gather(ffn_in, ("leaf", "path"), axis=0, tiled=True),
        lax.all_gather(ffn_out, ("leaf", "path"), axis=0, tiled=True),
        lax.all_gather(ffn_bias, ("leaf", "path"), axis=0, tiled=True),
    )
    w_in, w_out, shift_rows, gain_rows, feedforward_up_weight, ffn_w2, ffn_b1 = gathered
    shift_all = shift_rows.astype(jnp.float32)
    gain_all = gain_rows.astype(jnp.float32)
    local_rows = tokens.shape[1]
    tree_rows = local_rows * lax.axis_size("path")
    first_row = lax.axis_index("path") * local_rows
    linked = slot_links(parent, assignment)
    allowed = visible(linked, first_row, local_rows, tree_rows)
    queries = ((project(tokens, w_in[0]) + shift_all[0]) * score_scale).astype(jnp.bfloat16)
    key_rows = project(tokens, w_in[1]).astype(jnp.bfloat16)
    value_rows = (project(tokens, w_in[2]) + shift_all[1]).astype(jnp.bfloat16)
    cross_keys = project(encoded, w_in[4]).astype(jnp.bfloat16)
    cross_values = (project(encoded, w_in[5]) + shift_all[4]).astype(jnp.bfloat16)
    all_keys, all_values, enc_keys, enc_values = (
        lax.all_gather(key_rows, "path", axis=1, tiled=True),
        lax.all_gather(value_rows, "path", axis=1, tiled=True),
        lax.all_gather(cross_keys, "path", axis=1, tiled=True),
        lax.all_gather(cross_values, "path", axis=1, tiled=True),
    )
    attended, self_mass = attend_forward(queries, all_keys, all_values, allowed)
    attended = attended.astype(jnp.bfloat16)
    branch = project(attended, w_out[0]) + shift_all[2]
    first_norm, norm_back_one = jax.vjp(
        layer_norm, tokens.astype(jnp.float32) + branch, gain_all[0], shift_all[7]
    )
    first_low = first_norm.astype(jnp.bfloat16)
    cross_queries = ((project(first_low, w_in[3]) + shift_all[3]) * score_scale).astype(
        jnp.bfloat16
    )
    crossed, cross_mass = attend_forward(cross_queries, enc_keys, enc_values, None)
    crossed = crossed.astype(jnp.bfloat16)
    cross_branch = project(crossed, w_out[1]) + shift_all[5]
    second_norm, norm_back_two = jax.vjp(
        layer_norm, first_norm + cross_branch, gain_all[1], shift_all[8]
    )
    second_low = second_norm.astype(jnp.bfloat16)
    hidden_pre = project(second_low, feedforward_up_weight) + ffn_b1.astype(jnp.float32)
    hidden, gelu_backward_pass = jax.vjp(gelu_exact, hidden_pre)
    hidden_low = hidden.astype(jnp.bfloat16)
    ffn_branch = project(hidden_low, ffn_w2) + shift_all[6]
    result, norm_back_three = jax.vjp(
        layer_norm, second_norm + ffn_branch, gain_all[2], shift_all[9]
    )
    output = result.astype(jnp.bfloat16)
    ffn_w1_back, ffn_w2_back = (
        lax.all_gather(ffn_in, ("leaf", "path"), axis=0, tiled=True),
        lax.all_gather(ffn_out, ("leaf", "path"), axis=0, tiled=True),
    )
    grad_pre3, grad_gain3, gradient_third_shift = norm_back_three(cotangent.astype(jnp.float32))
    grad_ffn_branch = grad_pre3.astype(jnp.bfloat16)
    grad_w2 = weight_grad(hidden_low, grad_ffn_branch)
    gradient_down_bias = column_sum(grad_ffn_branch)
    (grad_hidden_pre,) = gelu_backward_pass(project_back(grad_ffn_branch, ffn_w2_back))
    grad_hidden = grad_hidden_pre.astype(jnp.bfloat16)
    grad_w1 = weight_grad(second_low, grad_hidden)
    grad_b1 = column_sum(grad_hidden)
    grad_ffn_w1, grad_ffn_w2, grad_ffn_b1 = (
        lax.psum_scatter(grad_w1, ("leaf", "path"), scatter_dimension=0, tiled=True),
        lax.psum_scatter(grad_w2, ("leaf", "path"), scatter_dimension=0, tiled=True),
        lax.psum_scatter(grad_b1, ("leaf", "path"), scatter_dimension=0, tiled=True),
    )
    w_in_back, w_out_back = (
        lax.all_gather(attn_in, ("leaf", "path"), axis=1, tiled=True),
        lax.all_gather(attn_out, ("leaf", "path"), axis=1, tiled=True),
    )
    grad_second = grad_pre3 + project_back(grad_hidden, ffn_w1_back)
    grad_pre2, grad_gain2, grad_shift2 = norm_back_two(grad_second)
    grad_cross_branch = grad_pre2.astype(jnp.bfloat16)
    grad_wo2 = weight_grad(crossed, grad_cross_branch)
    grad_co = column_sum(grad_cross_branch)
    grad_crossed = project_back(grad_cross_branch, w_out_back[1]).astype(jnp.bfloat16)
    grad_cq, grad_ck_tree, grad_cv_tree, cross_delta = attend_back(
        cross_queries, enc_keys, enc_values, None, cross_mass, grad_crossed
    )
    grad_ck, grad_cv = (
        lax.psum_scatter(
            grad_ck_tree.astype(jnp.bfloat16), "path", scatter_dimension=1, tiled=True
        ).astype(jnp.float32),
        lax.psum_scatter(
            grad_cv_tree.astype(jnp.bfloat16), "path", scatter_dimension=1, tiled=True
        ).astype(jnp.float32),
    )
    grad_ck = grad_ck.astype(jnp.bfloat16)
    grad_cv = grad_cv.astype(jnp.bfloat16)
    grad_wk2 = weight_grad(encoded, grad_ck)
    grad_wv2 = weight_grad(encoded, grad_cv)
    grad_cv_bias = column_sum(grad_cv)
    grad_encoded = project_back(grad_ck, w_in_back[4]) + project_back(grad_cv, w_in_back[5])
    grad_cq_scaled = grad_cq.astype(jnp.bfloat16) * score_scale
    grad_wq2 = weight_grad(first_low, grad_cq_scaled)
    grad_cq_bias = column_sum(grad_cq_scaled)
    grad_first = grad_pre2 + project_back(grad_cq_scaled, w_in_back[3])
    grad_pre1, grad_gain1, grad_shift1 = norm_back_one(grad_first)
    gradient_branch_sum = grad_pre1.astype(jnp.bfloat16)
    grad_wo = weight_grad(attended, gradient_branch_sum)
    grad_bo = column_sum(gradient_branch_sum)
    grad_attended = project_back(gradient_branch_sum, w_out_back[0]).astype(jnp.bfloat16)
    grad_queries, grad_keys_tree, grad_values_tree, self_delta = attend_back(
        queries, all_keys, all_values, allowed, self_mass, grad_attended
    )
    grad_keys, grad_values = (
        lax.psum_scatter(
            grad_keys_tree.astype(jnp.bfloat16), "path", scatter_dimension=1, tiled=True
        ).astype(jnp.float32),
        lax.psum_scatter(
            grad_values_tree.astype(jnp.bfloat16), "path", scatter_dimension=1, tiled=True
        ).astype(jnp.float32),
    )
    grad_keys = grad_keys.astype(jnp.bfloat16)
    grad_values = grad_values.astype(jnp.bfloat16)
    grad_q_scaled = grad_queries.astype(jnp.bfloat16) * score_scale
    grad_wq = weight_grad(tokens, grad_q_scaled)
    grad_bq = column_sum(grad_q_scaled)
    grad_wk = weight_grad(tokens, grad_keys)
    gradient_value_weight = weight_grad(tokens, grad_values)
    grad_bv = column_sum(grad_values)
    grad_tokens = (
        grad_pre1
        + project_back(grad_q_scaled, w_in_back[0])
        + project_back(grad_keys, w_in_back[1])
        + project_back(grad_values, w_in_back[2])
    )
    stacked_in = jnp.stack([grad_wq, grad_wk, gradient_value_weight, grad_wq2, grad_wk2, grad_wv2])
    stacked_out = jnp.stack([grad_wo, grad_wo2])
    stacked_shifts = jnp.stack(
        [
            grad_bq,
            grad_bv,
            grad_bo,
            grad_cq_bias,
            grad_cv_bias,
            grad_co,
            gradient_down_bias,
            grad_shift1,
            grad_shift2,
            gradient_third_shift,
        ]
    )
    stacked_gains = jnp.stack([grad_gain1, grad_gain2, grad_gain3])
    grad_attn_in, grad_attn_out, grad_shifts, grad_gains = (
        lax.psum_scatter(stacked_in, ("leaf", "path"), scatter_dimension=1, tiled=True),
        lax.psum_scatter(stacked_out, ("leaf", "path"), scatter_dimension=1, tiled=True),
        lax.psum_scatter(stacked_shifts, ("leaf", "path"), scatter_dimension=1, tiled=True),
        lax.psum_scatter(stacked_gains, ("leaf", "path"), scatter_dimension=1, tiled=True),
    )
    return (
        output,
        grad_tokens,
        grad_encoded,
        grad_attn_in,
        grad_attn_out,
        grad_ffn_w1,
        grad_ffn_w2,
        grad_shifts,
        grad_gains,
        grad_ffn_b1,
    )


def solution(mesh):
    placed = (
        P("leaf", "path", None),
        P("leaf", "path", None),
        P("leaf", "path", None),
        P("leaf", None),
        P("leaf", None),
        P(None, ("leaf", "path"), None),
        P(None, ("leaf", "path"), None),
        P(("leaf", "path"), None),
        P(("leaf", "path"), None),
        P(None, ("leaf", "path")),
        P(None, ("leaf", "path")),
        P(("leaf", "path")),
    )
    return jax.shard_map(
        body,
        mesh=mesh,
        in_specs=placed,
        out_specs=(
            P("leaf", "path", None),
            P("leaf", "path", None),
            P("leaf", "path", None),
            P(None, ("leaf", "path"), None),
            P(None, ("leaf", "path"), None),
            P(("leaf", "path"), None),
            P(("leaf", "path"), None),
            P(None, ("leaf", "path")),
            P(None, ("leaf", "path")),
            P(("leaf", "path")),
        ),
        check_vma=False,
    )
```

profile of v0, /device:TPU:0, one launch (start us, length us, event | category | flops | bytes accessed | tf_op | source)
XLA Modules:
  0.0 1566.8 jit_solution(17043161388606391220)
XLA Ops:
  8.0 70.3 %all-gather.5 = bf16[32,24,3]{1,2,0:T(4,128)(2,1)S(1)} all-gather(bf16[1,24,3]{1,2,0:T(4,128)(2,1)} %bitcast.477), channel_id=1, replica_groups=mesh['leaf'=8,'path'=4] {'leaf','path'}, dimensions={0}, use_global_device_ids=true | all-gather | bytes 4752 | tf_op jit(solution)/shard_map/all_gather | solution.py:194
  78.5 64.8 %all-gather.4 = bf16[32,24,10]{1,2,0:T(8,128)(2,1)S(1)} all-gather(bf16[1,24,10]{1,2,0:T(8,128)(2,1)} %bitcast.476), channel_id=1, replica_groups=mesh['leaf'=8,'path'=4] {'leaf','path'}, dimensions={0}, use_global_device_ids=true | all-gather | bytes 15840 | tf_op jit(solution)/shard_map/all_gather | solution.py:193
  158.1 40.9 %all-reduce = bf16[3072]{0:T(1024)(128)(2,1)S(1)} all-reduce(bf16[3072]{0:T(1024)(128)(2,1)S(1)} %dynamic-update-slice), channel_id=1, replica_groups=mesh['leaf'=8,'path'=4] {'leaf','path'}, use_global_device_ids=true, to_apply=%add | all-reduce | flops 3072 | bytes 12288
  208.7 12.2 all-gather.29.cloned.1.call-done
  223.4 61.8 %all-gather.23.cloned.1.call-done = bf16[2048,768]{1,0:T(8,128)(2,1)} async-done(((bf16[512,768]{1,0:T(8,128)(2,1)}), bf16[2048,768]{1,0:T(8,128)(2,1)}) %all-gather.23.cloned.1.call-update) | async-done | bytes 3145744 | tf_op jit(solution)/shard_map/all_gather | solution.py:214
  290.0 59.5 %all-gather.25.cloned.1.call-done = bf16[2048,768]{1,0:T(8,128)(2,1)} async-done(((bf16[512,768]{1,0:T(8,128)(2,1)}), bf16[2048,768]{1,0:T(8,128)(2,1)}) %all-gather.25.cloned.1.call-update) | async-done | bytes 3145744 | tf_op jit(solution)/shard_map/all_gather | solution.py:213
  355.1 56.9 %while.72 = (s32[]{:T(128)}, bf16[1,512,768]{1,2,0:T(8,128)(2,1)}, f32[1,12,512]{2,1,0:T(8,128)S(1)}, bf16[1,2048,768]{1,2,0:T(8,128)(2,1)}, pred[1,512,2048]{2,...) while((s32[]{:T(128)}, bf16[1,512,768]{1,2,0:T(8,128)(2,1)}, ...), condition=%wide.region_3.4_spmd, body=%wide.region_0.3_spmd.sunk | while | flops 555744256 | bytes 32276720 | solution.py:111
  422.2 33.6 %while.73 = (s32[]{:T(128)}, bf16[1,512,768]{1,2,0:T(8,128)(2,1)}, f32[1,12,512]{2,1,0:T(8,128)S(1)}, bf16[1,1024,768]{1,2,0:T(8,128)(2,1)S(1)}, bf16[1,512,768]...) while((s32[]{:T(128)}, bf16[1,512,768]{1,2,0:T(8,128)(2,1)}, ...), condition=%wide.region_9.10_spmd, body=%wide.region_6.9_spmd.sunk | while | flops 274725888 | bytes 14975209 | solution.py:111
  460.4 13.4 all-gather.19.cloned.1.call-done
  473.8 8.4 multiply_convert_fusion.2
  482.2 56.8 %all-gather.21.cloned.1.call-done = bf16[3072,768]{1,0:T(8,128)(2,1)} async-done(((bf16[96,768]{1,0:T(8,128)(2,1)}), bf16[3072,768]{1,0:T(8,128)(2,1)}) %all-gather.21.cloned.1.call-update) | async-done | bytes 4718608 | tf_op jit(solution)/shard_map/all_gather | solution.py:196
  569.1 57.0 %while.74 = (s32[]{:T(128)}, bf16[1,512,768]{1,2,0:T(8,128)(2,1)}, bf16[1,1024,768]{1,2,0:T(8,128)(2,1)}, bf16[1,1024,768]{1,2,0:T(8,128)(2,1)}, bf16[1,1024,768...) while((s32[]{:T(128)}, bf16[1,512,768]{1,2,0:T(8,128)(2,1)}, ...), condition=%wide.region_20.21_spmd, body=%wide.region_18.20_spmd.sunk | while | flops 680524800 | bytes 36598028 | solution.py:172
  640.7 101.9 %while.75 = (s32[]{:T(128)}, bf16[1,512,768]{1,2,0:T(8,128)(2,1)}, bf16[1,2048,768]{1,2,0:T(8,128)(2,1)}, bf16[1,2048,768]{1,2,0:T(8,128)(2,1)}, bf16[1,2048,768...) while((s32[]{:T(128)}, bf16[1,512,768]{1,2,0:T(8,128)(2,1)}, ...), condition=%wide.region_25.26_spmd, body=%wide.region_23.25_spmd.sunk | while | flops 1367342080 | bytes 74608920 | solution.py:172
  748.3 53.5 %reduce-scatter.11.cloned.1.call-done = bf16[1,512,768]{1,2,0:T(8,128)(2,1)} async-done(((bf16[1,2048,768]{1,2,0:T(8,128)(2,1)}), bf16[1,512,768]{1,2,0:T(8,128)(2,1)}) %reduce-scatter.11.cloned.1.call-update) | async-done | bytes 786448 | tf_op jit(solution)/shard_map/reduce_scatter | solution.py:300
  805.5 58.9 %reduce-scatter.13.cloned.1.call-done = bf16[1,512,768]{1,2,0:T(8,128)(2,1)} async-done(((bf16[1,2048,768]{1,2,0:T(8,128)(2,1)}), bf16[1,512,768]{1,2,0:T(8,128)(2,1)}) %reduce-scatter.13.cloned.1.call-update) | async-done | bytes 786448 | tf_op jit(solution)/shard_map/reduce_scatter | solution.py:303
  870.4 31.6 %reduce-scatter.15.cloned.1.call-done = bf16[1,256,768]{1,2,0:T(8,128)(2,1)} async-done(((bf16[1,1024,768]{1,2,0:T(8,128)(2,1)}), bf16[1,256,768]{1,2,0:T(8,128)(2,1)}) %reduce-scatter.15.cloned.1.call-update) | async-done | bytes 393232 | tf_op jit(solution)/shard_map/reduce_scatter | solution.py:274
  905.0 33.4 %reduce-scatter.17.cloned.1.call-done = bf16[1,256,768]{1,2,0:T(8,128)(2,1)} async-done(((bf16[1,1024,768]{1,2,0:T(8,128)(2,1)}), bf16[1,256,768]{1,2,0:T(8,128)(2,1)}) %reduce-scatter.17.cloned.1.call-update) | async-done | bytes 393232 | tf_op jit(solution)/shard_map/reduce_scatter | solution.py:277
  941.3 17.5 %copy.94 = f32[6,768,768]{2,0,1:T(8,128)} copy(f32[6,768,768]{1,2,0:T(8,128)} %bitcast_dynamic-update-slice_fusion.2) | data formatting | bytes 28311552 | tf_op jit(solution)/shard_map/stack | solution.py:321
  974.6 8.8 fusion.53
  1001.7 42.6 %all-reduce.4 = (f32[10,768]{1,0:T(8,128)}, f32[3,768]{1,0:T(4,128)}, f32[3072]{0:T(1024)}) all-reduce(f32[10,768]{1,0:T(8,128)} %stack.95, f32[3,768]{1,0:T(4,128)S(1)} %pad_maximum_fusion.1, f32[3072]{0:T(1024)} %get-tuple-element.1114), channel_id=14, replica_groups=mesh['leaf'=8,'path'=4] {'leaf','path'}, use_global_device_ids=true, to_apply=%region_44.45.clone | all-reduce | flops 13056 | bytes 104448
  1054.2 111.1 %reduce-scatter.19.cloned.1.call-done = f32[6,24,768]{2,0,1:T(8,128)} async-done(((f32[6,768,768]{2,0,1:T(8,128)}), f32[6,24,768]{2,0,1:T(8,128)}) %reduce-scatter.19.cloned.1.call-update) | async-done | bytes 442384 | tf_op jit(solution)/shard_map/reduce_scatter | solution.py:339
  1167.3 109.8 %reduce-scatter.21.cloned.1.call-done = f32[2,24,768]{2,1,0:T(8,128)} async-done(((f32[2,768,768]{2,1,0:T(8,128)}), f32[2,24,768]{2,1,0:T(8,128)}) %reduce-scatter.21.cloned.1.call-update) | async-done | bytes 147472 | tf_op jit(solution)/shard_map/reduce_scatter | solution.py:340
  1277.1 141.9 %reduce-scatter.23.cloned.1.call-done = f32[24,3072]{1,0:T(8,128)} async-done(((f32[768,3072]{1,0:T(8,128)}), f32[24,3072]{1,0:T(8,128)}) %reduce-scatter.23.cloned.1.call-update) | async-done | bytes 294928 | tf_op jit(solution)/shard_map/reduce_scatter | solution.py:256
  1419.1 141.1 %reduce-scatter.25.cloned.1.call-done = f32[96,768]{1,0:T(8,128)} async-done(((f32[3072,768]{1,0:T(8,128)}), f32[96,768]{1,0:T(8,128)}) %reduce-scatter.25.cloned.1.call-update) | async-done | bytes 294928 | tf_op jit(solution)/shard_map/reduce_scatter | solution.py:257
  (523 shorter events, 412.3 us)
Async XLA Ops:
  7.2 137.2 %copy-start = (bf16[1,256,768]{2,1,0:T(8,128)(2,1)S(1)}, bf16[1,256,768]{2,1,0:T(8,128)(2,1)}, u32[]{:S(2)}) copy-start(bf16[1,256,768]{2,1,0:T(8,128)(2,1)} %param.21) | copy-start | bytes 1179652
  7.2 137.2 %all-gather.15.cloned.1.call-start = ((), (), s32[]{:S(2)}) async-start(), calls=%async_computation.8 | async-start | bytes 7299072 | tf_op jit(solution)/shard_map/all_gather | solution.py:191
  7.9 199.0 %all-gather.27.cloned.1.call-start = ((), (), s32[]{:S(2)}) async-start(), calls=%async_computation.22 | async-start | bytes 1966080 | tf_op jit(solution)/shard_map/all_gather | solution.py:216
  144.4 311.5 %copy-start.45 = (f32[768]{0:T(1024)}, f32[768]{0:T(1024)S(1)}, u32[]{:S(2)}) copy-start(f32[768]{0:T(1024)S(1)} %get-tuple-element.1001) | copy-start | bytes 9220
  144.4 394.7 %copy-start.43 = (f32[768]{0:T(1024)}, f32[768]{0:T(1024)S(1)}, u32[]{:S(2)}) copy-start(f32[768]{0:T(1024)S(1)} %get-tuple-element.997) | copy-start | bytes 9220
  144.4 416.1 %copy-start.39 = (f32[768]{0:T(1024)}, f32[768]{0:T(1024)S(1)}, u32[]{:S(2)}) copy-start(f32[768]{0:T(1024)S(1)} %get-tuple-element.1119) | copy-start | bytes 9220
  146.9 74.0 %all-gather.29.cloned.1.call-start = ((), (), s32[]{:S(2)}) async-start(), calls=%async_computation.23 | async-start | bytes 1966080 | tf_op jit(solution)/shard_map/all_gather | solution.py:215
  149.5 135.7 %all-gather.23.cloned.1.call-start = ((), (), s32[]{:S(2)}) async-start(), calls=%async_computation.20 | async-start | bytes 3932160 | tf_op jit(solution)/shard_map/all_gather | solution.py:214
  152.6 196.9 %all-gather.25.cloned.1.call-start = ((), (), s32[]{:S(2)}) async-start(), calls=%async_computation.21 | async-start | bytes 3932160 | tf_op jit(solution)/shard_map/all_gather | solution.py:213
  155.7 256.3 %all-gather.17.cloned.1.call-start = ((), (), s32[]{:S(2)}) async-start(), calls=%async_computation.9 | async-start | bytes 2433024 | tf_op jit(solution)/shard_map/all_gather | solution.py:192
  156.3 317.5 %all-gather.19.cloned.1.call-start = ((), (), s32[]{:S(2)}) async-start(), calls=%async_computation.10 | async-start | bytes 4866048 | tf_op jit(solution)/shard_map/all_gather | solution.py:195
  157.0 382.0 %all-gather.21.cloned.1.call-start = ((), (), s32[]{:S(2)}) async-start(), calls=%async_computation.11 | async-start | bytes 4866048 | tf_op jit(solution)/shard_map/all_gather | solution.py:196
  157.8 644.1 %reduce-scatter.11.cloned.1.call-start = ((), (), s32[]{:S(2)}) async-start(), calls=%async_computation.12 | async-start | bytes 3932160 | tf_op jit(solution)/shard_map/reduce_scatter | solution.py:300
  458.9 101.6 %copy-start.29 = (f32[512]{0:T(512)}, f32[512]{0:T(512)S(1)}, u32[]{:S(2)}) copy-start(f32[512]{0:T(512)S(1)} %broadcast_multiply_fusion.1) | copy-start | bytes 6148
  460.4 100.1 %copy-start.41 = (f32[512]{0:T(512)}, f32[512]{0:T(512)S(1)}, u32[]{:S(2)}) copy-start(f32[512]{0:T(512)S(1)} %fusion.99) | copy-start | bytes 6148
  473.8 65.2 %copy-start.47 = (f32[768]{0:T(1024)S(1)}, f32[768]{0:T(1024)}, u32[]{:S(2)}) copy-start(f32[768]{0:T(1024)} %get-tuple-element.996) | copy-start | bytes 9220
  742.7 121.7 %reduce-scatter.13.cloned.1.call-start = ((), (), s32[]{:S(2)}) async-start(), calls=%async_computation.13 | async-start | bytes 3932160 | tf_op jit(solution)/shard_map/reduce_scatter | solution.py:303
  743.3 158.8 %reduce-scatter.15.cloned.1.call-start = ((), (), s32[]{:S(2)}) async-start(), calls=%async_computation.14 | async-start | bytes 1966080 | tf_op jit(solution)/shard_map/reduce_scatter | solution.py:274
  744.0 194.5 %reduce-scatter.17.cloned.1.call-start = ((), (), s32[]{:S(2)}) async-start(), calls=%async_computation.15 | async-start | bytes 1966080 | tf_op jit(solution)/shard_map/reduce_scatter | solution.py:277
  744.6 420.8 %reduce-scatter.19.cloned.1.call-start = ((), (), s32[]{:S(2)}) async-start(), calls=%async_computation.16 | async-start | bytes 19464192 | tf_op jit(solution)/shard_map/reduce_scatter | solution.py:339
  805.5 62.5 %copy-start.46 = (f32[768]{0:T(1024)S(1)}, f32[768]{0:T(1024)}, u32[]{:S(2)}) copy-start(f32[768]{0:T(1024)} %copy-done.45) | copy-start | bytes 9220
  958.9 318.3 %reduce-scatter.21.cloned.1.call-start = ((), (), s32[]{:S(2)}) async-start(), calls=%async_computation.17 | async-start | bytes 4866048 | tf_op jit(solution)/shard_map/reduce_scatter | solution.py:340
  964.3 454.8 %reduce-scatter.23.cloned.1.call-start = ((), (), s32[]{:S(2)}) async-start(), calls=%async_computation.18 | async-start | bytes 9732096 | tf_op jit(solution)/shard_map/reduce_scatter | solution.py:256
  973.4 586.8 %reduce-scatter.25.cloned.1.call-start = ((), (), s32[]{:S(2)}) async-start(), calls=%async_computation.19 | async-start | bytes 9732096 | tf_op jit(solution)/shard_map/reduce_scatter | solution.py:257
  (54 other events, 472.1 us)
Sparse Core Ops, SparseCore 0:
  11.1 75.6 all-gather.14
  147.0 35.4 all-gather.26
  184.7 36.1 all-gather.28
  222.9 62.3 all-gather.22
  287.3 62.1 all-gather.24
  352.4 56.0 all-gather.16
  411.3 62.5 all-gather.18
  476.6 62.3 all-gather.20
  742.8 59.0 reduce-scatter.10
  804.0 60.2 reduce-scatter.12
  866.7 35.3 reduce-scatter.14
  904.2 34.2 reduce-scatter.16
  959.0 206.3 reduce-scatter.18
  1171.2 105.8 reduce-scatter.20
  1284.5 134.5 reduce-scatter.22
  1425.4 134.6 reduce-scatter.24
where the time goes:
time: 1570 us
  waiting for transfers between devices  890 us (57%)
  matrix products  223 us (14%)
  blocking collectives  218 us (14%)
  local copies, waits for them, and re-layouts  167 us (11%)
  other arithmetic  51.1 us (3%)
    reduce_scatter x1, waiting for transfers between devices, body(): lax.psum_scatter(grad_w1, ('leaf', 'path'), scatter_dimension=0, tiled=True)  142 us
    reduce_scatter x1, waiting for transfers between devices, body(): lax.psum_scatter(grad_w2, ('leaf', 'path'), scatter_dimension=0, tiled=True)  141 us
    reduce_scatter x1, waiting for transfers between devices, body(): lax.psum_scatter(stacked_in, ('leaf', 'path'), scatter_dimension=1, tiled...  111 us
    reduce_scatter x1, waiting for transfers between devices, body(): lax.psum_scatter(stacked_out, ('leaf', 'path'), scatter_dimension=1, tile...  110 us
    unnamed x2, blocking collectives  83.4 us
    all_gather x1, blocking collectives, body(): lax.all_gather(gains, ('leaf', 'path'), axis=1, tiled=True)  70.3 us
    dynamic_slice x84, local copies, waits for them, and re-layouts, split_pair(): piece = lax.dynamic_slice_in_dim(matrix, offset, 2 * HEAD, 2)  67 us
    all_gather x1, blocking collectives, body(): lax.all_gather(shifts, ('leaf', 'path'), axis=1, tiled=True)  64.8 us
  transfers between devices with their start and end apart: 16, of which 13 were waited for; matrix products, arithmetic and copies ran while one was open for 13% of the time, Pallas kernels for 0%

commit v1 on v0

v1 whole, which is shorter than its diff:
```python
import functools

import jax
import jax.numpy as jnp
from jax import lax
from jax.experimental import pallas as pl
from jax.experimental.pallas import tpu as pltpu
from jax.sharding import PartitionSpec as P

HEAD = 64
BLK = 128
PAIR = 2 * HEAD
MESH = pl.DeviceIdType.MESH
F32 = jnp.float32
BF16 = jnp.bfloat16
VMEM_LIMIT = 62 * 1024 * 1024


class Place:
    def __init__(self, leaf_count, path_count):
        self.leafs, self.paths = leaf_count, path_count
        outer = leaf_count // 2
        self.A = 2 if outer % 2 == 0 else 1
        self.B = outer // self.A
        leaf = lax.axis_index("leaf")
        self.leaf, self.p = leaf, lax.axis_index("path")
        self.c = leaf % 2
        self.a = (leaf // 2) // self.B
        self.b = (leaf // 2) % self.B

    def leaf_at(self, a, b, c):
        return (a * self.B + b) * 2 + c

    def at_core(self):
        return (self.leaf_at(self.a, self.b, 1 - self.c), self.p)

    def at_a(self, a):
        return (self.leaf_at(a, self.b, self.c), self.p)

    def at_b(self, b):
        return (self.leaf_at(self.a, b, self.c), self.p)

    def at_p(self, p):
        return (self.leaf, p)

    def lines(self):
        return [
            (self.paths, self.p, self.at_p),
            (self.A, self.a, self.at_a),
            (self.B, self.b, self.at_b),
            (2, self.c, lambda c: (self.leaf_at(self.a, self.b, c), self.p)),
        ]


def greet(place):
    barrier = pltpu.get_barrier_semaphore()
    peers = 0
    for size, pos, to in place.lines():
        if size == 1:
            continue
        if size == 2:
            pl.semaphore_signal(barrier, inc=1, device_id=to(1 - pos), device_id_type=MESH)
            peers = peers + 1
            continue
        for step in (-1, 1):
            there = pos + step
            inside = (there >= 0) & (there < size)

            @pl.when(inside)
            def _():
                pl.semaphore_signal(barrier, inc=1, device_id=to(there), device_id_type=MESH)

            peers = peers + jnp.where(inside, 1, 0)
    pl.semaphore_wait(barrier, peers)


class Mail:
    def __init__(self, send_sems, recv_sems):
        self.send_sems, self.recv_sems = send_sems, recv_sems
        self.count = 0
        self.sent = []

    def post(self, when, src, dst, to, hear_when, landing):
        k = self.count
        self.count += 1
        send = pltpu.make_async_remote_copy(
            src_ref=src,
            dst_ref=dst,
            send_sem=self.send_sems.at[k],
            recv_sem=self.recv_sems.at[k],
            device_id=to,
            device_id_type=MESH,
        )
        hear = pltpu.make_async_remote_copy(
            src_ref=landing,
            dst_ref=landing,
            send_sem=self.send_sems.at[k],
            recv_sem=self.recv_sems.at[k],
            device_id=to,
            device_id_type=MESH,
        )
        self.sent.append((when, send))

        def start():
            guarded(when, send.start)

        def wait():
            guarded(hear_when, hear.wait_recv)

        return start, wait

    def finish(self):
        for when, send in self.sent:
            guarded(when, send.wait_send)


def guarded(when, action):
    if when is None:
        action()
    else:

        @pl.when(when)
        def _():
            action()


def clamp(index, size):
    return jnp.clip(index, 0, size - 1)


def flood(mail, line, views, src_views=None):
    size, pos, to = line
    steps = []
    if size == 1:
        return steps
    first = src_views if src_views is not None else views(pos)
    if size == 2:
        jobs = [
            mail.post(None, s, d, to(1 - pos), None, w)
            for s, d, w in zip(first, views(pos), views(1 - pos))
        ]
        return [([j[0] for j in jobs], [j[1] for j in jobs])]
    for step in range(1, size):
        starts, waits = [], []
        for sign in (1, -1):
            item = pos - sign * (step - 1)
            there = pos + sign
            when = (there >= 0) & (there < size) & (item >= 0) & (item < size)
            heard = pos - sign * step
            hear_when = (heard >= 0) & (heard < size)
            item_c = clamp(item, size)
            sources = first if step == 1 else views(item_c)
            for s, d, w in zip(sources, views(item_c), views(clamp(heard, size))):
                start, wait = mail.post(when, s, d, to(clamp(there, size)), hear_when, w)
                starts.append(start)
                waits.append(wait)
        steps.append((starts, waits))
    return steps


def run(actions):
    for action in actions:
        action()


def gather_stages(mail, place, shards, wholes):
    A, B, c = place.A, place.B, place.c

    def half(ref, leaf, h):
        width = ref.shape[-1] // 2
        return ref.at[:, leaf, :, :, pl.ds(h * width, width)]

    line_p, line_a, line_b, line_c = place.lines()
    along_p = flood(
        mail, line_p, lambda i: [w.at[:, place.leaf, i] for w in wholes], list(shards)
    )

    def of_b(h, across_a):
        ays = range(A) if across_a else [place.a]
        return lambda i: [half(w, place.leaf_at(a, i, c), h) for a in ays for w in wholes]

    def of_a(h, across_b):
        bees = range(B) if across_b else [place.b]
        return lambda i: [half(w, place.leaf_at(i, b, c), h) for b in bees for w in wholes]

    first = [flood(mail, line_b, of_b(0, False)), flood(mail, line_a, of_a(1, False))]
    second = [flood(mail, line_a, of_a(0, True)), flood(mail, line_b, of_b(1, True))]
    own_core = [
        mail.post(
            None,
            w.at[:, place.leaf],
            w.at[:, place.leaf],
            place.at_core(),
            None,
            w.at[:, place.leaf_at(place.a, place.b, 1 - c)],
        )
        for w in wholes
    ]
    rest_core = []
    for offset in range(1, A * B):
        spot = (place.a * B + place.b + offset) % (A * B)
        for w in wholes:
            rest_core.append(
                mail.post(
                    None,
                    w.at[:, spot * 2 + c],
                    w.at[:, spot * 2 + c],
                    place.at_core(),
                    None,
                    w.at[:, spot * 2 + 1 - c],
                )
            )
    stages = []
    pending = []

    def advance(waits, starts):
        def stage():
            run(waits)
            run(starts)

        stages.append(stage)

    for starts, waits in along_p:
        advance(pending, starts)
        pending = waits
    opening = [own_core[i][0] for i in range(len(wholes))]
    for phase in (first, second):
        for s in range(max(len(f) for f in phase)):
            starts, waits = [], []
            for f in phase:
                if s < len(f):
                    starts += f[s][0]
                    waits += f[s][1]
            advance(pending, starts + opening)
            opening = []
            pending = waits
    advance(pending, opening + [j[0] for j in rest_core])
    advance([j[1] for j in own_core + rest_core], [])
    return stages


def gather_kernel(sizes, n, n_rows, *refs):
    place = Place(*sizes)
    shards, rows = refs[:n], refs[n : n + n_rows]
    wholes, all_rows = refs[n + n_rows : 2 * n + n_rows], refs[2 * n + n_rows : 2 * (n + n_rows)]
    send_sems, recv_sems, own_sems = refs[2 * (n + n_rows) :]
    greet(place)
    mail = Mail(send_sems, recv_sems)
    own = []
    for k, (s, w) in enumerate(zip(shards, wholes)):
        own.append(pltpu.make_async_copy(s, w.at[:, place.leaf, place.p], own_sems.at[k]))
    for k, (s, w) in enumerate(zip(rows, all_rows)):
        own.append(pltpu.make_async_copy(s, w.at[place.p], own_sems.at[n + k]))
    for copy in own:
        copy.start()
    lists = [gather_stages(mail, place, [s], [w]) for s, w in zip(shards, wholes)]
    row_lists = []
    for s, w in zip(rows, all_rows):
        steps = flood(mail, place.lines()[0], lambda i, w=w: [w.at[i]], [s])
        stages = []
        pending = []
        for starts, waits in steps:
            stages.append(functools.partial(lambda p, q: (run(p), run(q)), pending, starts))
            pending = waits
        stages.append(functools.partial(run, pending))
        row_lists.append(stages)
    for copy in own:
        copy.wait()
    order = lists[:1] + row_lists + lists[1:]
    for t in range(max(len(l) + g for g, l in enumerate(order))):
        for g, l in enumerate(order):
            if 0 <= t - g < len(l):
                l[t - g]()
    mail.finish()


ANY = pl.BlockSpec(memory_space=pl.ANY)


def gather_all(sizes, shards, rows, collective_id):
    leafs, paths = sizes
    out_shape = [
        jax.ShapeDtypeStruct((s.shape[0], leafs, paths) + s.shape[1:], s.dtype) for s in shards
    ] + [jax.ShapeDtypeStruct((paths,) + r.shape, r.dtype) for r in rows]
    count = 100 * (len(shards) + len(rows))
    return pl.pallas_call(
        functools.partial(gather_kernel, sizes, len(shards), len(rows)),
        out_shape=out_shape,
        in_specs=[ANY] * (len(shards) + len(rows)),
        out_specs=[ANY] * len(out_shape),
        scratch_shapes=[
            pltpu.SemaphoreType.DMA((count,)),
            pltpu.SemaphoreType.DMA((count,)),
            pltpu.SemaphoreType.DMA((len(out_shape),)),
        ],
        compiler_params=pltpu.CompilerParams(
            collective_id=collective_id, has_side_effects=True, vmem_limit_bytes=VMEM_LIMIT
        ),
        name="gather_all",
    )(*shards, *rows)


def shift_sum(mail, line, mine, slots_up, slots_down, add):
    size, pos, to = line
    if size == 1:
        return []
    if size == 2:
        jobs = [
            mail.post(None, s, slot, to(1 - pos), None, slot)
            for s, slot in zip(mine(1 - pos), slots_up[0])
        ]

        def begin():
            run([j[0] for j in jobs])

        def end():
            for job, dst, slot in zip(jobs, mine(pos), slots_up[0]):
                job[1]()
                add(dst, slot)

        return [begin, end]
    stages = []
    for k in range(size - 1):
        actions = []
        for sign, slots in ((1, slots_up), (-1, slots_down)):
            dest = size - 1 - k if sign == 1 else k
            when = (pos < dest) if sign == 1 else (pos > dest)
            hear_when = (
                ((pos > 0) & (pos <= dest)) if sign == 1 else ((pos < size - 1) & (pos >= dest))
            )
            there = clamp(pos + sign, size)
            jobs = [
                mail.post(when, s, slot, to(there), None, slot)
                for s, slot in zip(mine(dest), slots[k])
            ]

            def take(jobs=jobs, dst_refs=mine(dest), slot_refs=slots[k]):
                for job, dst, slot in zip(jobs, dst_refs, slot_refs):
                    job[1]()
                    add(dst, slot)

            actions.append(functools.partial(guarded, hear_when, take))
            actions += [job[0] for job in jobs]
        stages.append(functools.partial(run, actions))
    return stages


def add_rows(dst, src):
    lead = dst.shape[:-2]
    total = 1
    for extent in lead:
        total *= extent

    def body(i, _):
        index = []
        rest = i
        for extent in reversed(lead):
            index.insert(0, rest % extent)
            rest = rest // extent
        index = tuple(index)
        dst[index] = dst[index] + src[index]
        return 0

    lax.fori_loop(0, total, body, 0)


def scatter_scratch(sizes, shapes, dtypes):
    leafs, paths = sizes
    outer = leafs // 2
    A = 2 if outer % 2 == 0 else 1
    B = outer // A
    out = []
    for (k, R, C), dtype in zip(shapes, dtypes):
        nb, na = max(B - 1, 1) * (2 if B > 2 else 1), max(A - 1, 1)
        out += [
            pltpu.VMEM((k, A, B, paths, R, C), dtype),
            pltpu.VMEM((k, A, B, paths, R, C), dtype),
            pltpu.VMEM((nb, k, A, paths, R, C // 2), dtype),
            pltpu.VMEM((na, k, paths, R, C // 2), dtype),
            pltpu.VMEM((na, k, B, paths, R, C // 2), dtype),
            pltpu.VMEM((nb, k, paths, R, C // 2), dtype),
            pltpu.VMEM((2 * max(paths - 1, 1), k, R, C), dtype),
        ]
    return out


def scatter_stages(mail, place, own_sem, partials, outs, scratch):
    A, B, c, p = place.A, place.B, place.c, place.p
    line_p, line_a, line_b, line_c = place.lines()
    groups = [scratch[7 * i : 7 * i + 7] for i in range(len(partials))]
    local = [
        pltpu.make_async_copy(x.at[:, :, :, c], g[0], own_sem.at[i])
        for i, (x, g) in enumerate(zip(partials, groups))
    ]
    cores = [
        mail.post(None, x.at[:, :, :, 1 - c], g[1], place.at_core(), None, g[1])
        for x, g in zip(partials, groups)
    ]

    def begin():
        for copy in local:
            copy.start()
        run([j[0] for j in cores])

    def join():
        for copy, job, g in zip(local, cores, groups):
            copy.wait()
            job[1]()
            add_rows(g[0], g[1])

    def cols(ref, h):
        width = ref.shape[-1] // 2
        return pl.ds(h * width, width)

    def up_down(ref, size, at):
        if size <= 2:
            return [[at(r, 0) for r in ref]], None
        return (
            [[at(r, k) for r in ref] for k in range(size - 1)],
            [[at(r, size - 1 + k) for r in ref] for k in range(size - 1)],
        )

    acc = [g[0] for g in groups]
    pick = lambda r, k: r.at[k]
    up, down = up_down([g[2] for g in groups], B, pick)
    h0_b = shift_sum(
        mail, line_b, lambda d: [x.at[:, :, d, :, :, cols(x, 0)] for x in acc], up, down, add_rows
    )
    up, down = up_down([g[3] for g in groups], A, pick)
    h0_a = shift_sum(
        mail, line_a, lambda d: [x.at[:, d, place.b, :, :, cols(x, 0)] for x in acc], up, down, add_rows
    )
    up, down = up_down([g[4] for g in groups], A, pick)
    h1_a = shift_sum(
        mail, line_a, lambda d: [x.at[:, d, :, :, :, cols(x, 1)] for x in acc], up, down, add_rows
    )
    up, down = up_down([g[5] for g in groups], B, pick)
    h1_b = shift_sum(
        mail, line_b, lambda d: [x.at[:, place.a, d, :, :, cols(x, 1)] for x in acc], up, down, add_rows
    )
    up, down = up_down([g[6] for g in groups], place.paths, pick)
    along_p = shift_sum(
        mail, line_p, lambda d: [x.at[:, place.a, place.b, d] for x in acc], up, down, add_rows
    )

    def finish():
        for x, out in zip(acc, outs):
            for j in range(out.shape[0]):
                out[j] = x[j, place.a, place.b, p].astype(out.dtype)

    def side_by_side(one, two):
        merged = []
        for k in range(max(len(one), len(two))):
            merged.append(functools.partial(run, [s[k] for s in (one, two) if k < len(s)]))
        return merged

    return [
        begin,
        join,
        *side_by_side(h0_b, h1_a),
        *side_by_side(h0_a, h1_b),
        *along_p,
        finish,
    ]


def scatter_kernel(sizes, n, n_rows, *refs):
    place = Place(*sizes)
    partials, rows = refs[:n], refs[n : n + n_rows]
    bases = refs[n + n_rows : n + 2 * n_rows]
    refs = refs[n + 2 * n_rows :]
    outs, row_outs = refs[:n], refs[n : n + n_rows]
    refs = refs[n + n_rows :]
    send_sems, recv_sems, own_sems = refs[:3]
    scratch = refs[3 : 3 + 7 * n]
    row_scratch = refs[3 + 7 * n :]
    greet(place)
    mail = Mail(send_sems, recv_sems)
    line_p = place.lines()[0]
    lists = []
    for i in range(n):
        lists.append(
            scatter_stages(
                mail,
                place,
                own_sems.at[pl.ds(i, 1)],
                [partials[i]],
                [outs[i]],
                scratch[7 * i : 7 * i + 7],
            )
        )
    row_lists = []
    for i in range(n_rows):
        held, slots = row_scratch[2 * i : 2 * i + 2]
        load = pltpu.make_async_copy(rows[i], held, own_sems.at[n + i])
        size = place.paths
        if size == 2:
            ups, downs = [[slots.at[0]]], None
        else:
            ups = [[slots.at[k]] for k in range(size - 1)]
            downs = [[slots.at[size - 1 + k]] for k in range(size - 1)]
        load.start()
        load.wait()
        stages = shift_sum(
            mail, line_p, lambda d, held=held: [held.at[d]], ups, downs, add_tall
        )

        def last(i=i, held=held):
            def body(r, _):
                at = pl.ds(pl.multiple_of(r * 16, 16), 16)
                row_outs[i][at] = bases[i][at] + held[place.p, at].astype(F32)
                return 0

            lax.fori_loop(0, row_outs[i].shape[0] // 16, body, 0)

        row_lists.append(stages + [last])
    order = row_lists + lists
    for t in range(max(len(l) + g for g, l in enumerate(order))):
        for g, l in enumerate(order):
            if 0 <= t - g < len(l):
                l[t - g]()
    mail.finish()


def add_tall(dst, src):
    def body(r, _):
        at = pl.ds(pl.multiple_of(r * 16, 16), 16)
        dst[at] = dst[at] + src[at]
        return 0

    lax.fori_loop(0, dst.shape[0] // 16, body, 0)


def scatter_all(sizes, partials, rows, bases, collective_id):
    leafs, paths = sizes
    outer = leafs // 2
    A = 2 if outer % 2 == 0 else 1
    B = outer // A
    shapes = [(x.shape[0],) + x.shape[3:] for x in partials]
    partials = [
        x.reshape((x.shape[0], A, B, 2, paths) + x.shape[3:]) for x in partials
    ]
    n, n_rows = len(partials), len(rows)
    out_shape = [jax.ShapeDtypeStruct(s, F32) for s in shapes] + [
        jax.ShapeDtypeStruct(b.shape, F32) for b in bases
    ]
    row_scratch = []
    for r in rows:
        row_scratch += [
            pltpu.VMEM(r.shape, r.dtype),
            pltpu.VMEM((2 * max(paths - 1, 1),) + r.shape[1:], r.dtype),
        ]
    count = 120 * (n + n_rows)
    VM = pl.BlockSpec(memory_space=pltpu.VMEM)
    return pl.pallas_call(
        functools.partial(scatter_kernel, sizes, n, n_rows),
        out_shape=out_shape,
        in_specs=[ANY] * (n + n_rows) + [VM] * n_rows,
        out_specs=[VM] * (n + n_rows),
        scratch_shapes=[
            pltpu.SemaphoreType.DMA((count,)),
            pltpu.SemaphoreType.DMA((count,)),
            pltpu.SemaphoreType.DMA((n + n_rows,)),
            *scatter_scratch(sizes, shapes, [x.dtype for x in partials]),
            *row_scratch,
        ],
        compiler_params=pltpu.CompilerParams(
            collective_id=collective_id, has_side_effects=True, vmem_limit_bytes=VMEM_LIMIT
        ),
        name="scatter_all",
    )(*partials, *rows, *bases)


def dot(x, y, contract):
    return lax.dot_general(x, y, (contract, ((), ())), preferred_element_type=F32)


def attend_kernel(masked, q_ref, k_ref, v_ref, *refs):
    if masked:
        bias_ref, o_ref, lse_ref = refs
    else:
        o_ref, lse_ref = refs
    rows = q_ref.shape[0]
    step = min(256, rows)
    lane = lax.broadcasted_iota(jnp.int32, (1, PAIR), 1)
    k = k_ref[...]
    v = v_ref[...]

    def block(i, _):
        at = pl.ds(pl.multiple_of(i * step, step), step)
        q = q_ref[at]
        out = jnp.zeros((step, PAIR), F32)
        lse = jnp.zeros((step, PAIR), F32)
        for h in range(2):
            own = (lane >= HEAD) if h else (lane < HEAD)
            s = dot(jnp.where(own, q, jnp.zeros_like(q)), k, ((1,), (1,)))
            if masked:
                s = s + bias_ref[at].astype(F32)
            peak = jnp.max(s, axis=1, keepdims=True)
            e = jnp.exp(s - peak)
            mass = jnp.sum(e, axis=1, keepdims=True)
            o = dot(e.astype(BF16), v, ((1,), (0,)))
            out = jnp.where(own, o / mass, out)
            lse = jnp.where(own, peak + jnp.log(mass), lse)
        o_ref[at] = out.astype(BF16)
        lse_ref[at] = lse
        return 0

    lax.fori_loop(0, rows // step, block, 0)


def attend(q, k, v, bias):
    rows, width = q.shape
    keys = k.shape[0]
    pairs = width // PAIR
    qs = pl.BlockSpec((rows, PAIR), lambda h: (0, h))
    ks = pl.BlockSpec((keys, PAIR), lambda h: (0, h))
    ins, specs = [q, k, v], [qs, ks, ks]
    if bias is not None:
        ins.append(bias)
        specs.append(pl.BlockSpec((rows, keys), lambda h: (0, 0)))
    return pl.pallas_call(
        functools.partial(attend_kernel, bias is not None),
        grid=(pairs,),
        in_specs=specs,
        out_specs=[qs, qs],
        out_shape=[
            jax.ShapeDtypeStruct((rows, width), BF16),
            jax.ShapeDtypeStruct((rows, width), F32),
        ],
        compiler_params=pltpu.CompilerParams(vmem_limit_bytes=VMEM_LIMIT),
        name="attend",
    )(*ins)


def attend_back_kernel(masked, q_ref, k_ref, v_ref, do_ref, o_ref, lse_ref, *refs):
    if masked:
        bias_ref, dq_ref, dk_ref, dv_ref, dk_acc, dv_acc = refs
    else:
        dq_ref, dk_ref, dv_ref, dk_acc, dv_acc = refs
    rows = q_ref.shape[0]
    step = min(256, rows)
    lane = lax.broadcasted_iota(jnp.int32, (1, PAIR), 1)
    k = k_ref[...]
    v = v_ref[...]
    dk_acc[...] = jnp.zeros_like(dk_acc)
    dv_acc[...] = jnp.zeros_like(dv_acc)

    def block(i, _):
        at = pl.ds(pl.multiple_of(i * step, step), step)
        q = q_ref[at]
        do = do_ref[at]
        both = do.astype(F32) * o_ref[at].astype(F32)
        lse_pair = lse_ref[at]
        dq = jnp.zeros((step, PAIR), F32)
        for h in range(2):
            own = (lane >= HEAD) if h else (lane < HEAD)
            q_h = jnp.where(own, q, jnp.zeros_like(q))
            do_h = jnp.where(own, do, jnp.zeros_like(do))
            delta = jnp.sum(jnp.where(own, both, 0.0), axis=1, keepdims=True)
            lse = lse_pair[:, h * HEAD : h * HEAD + 1]
            s = dot(q_h, k, ((1,), (1,)))
            if masked:
                s = s + bias_ref[at].astype(F32)
            e = jnp.exp(s - lse)
            dp = dot(do_h, v, ((1,), (1,)))
            ds = (e * (dp - delta)).astype(BF16)
            dq = jnp.where(own, dot(ds, k, ((1,), (0,))), dq)
            dk_acc[...] += dot(ds, q_h, ((0,), (0,)))
            dv_acc[...] += dot(e.astype(BF16), do_h, ((0,), (0,)))
        dq_ref[at] = (dq.astype(BF16) * BF16(HEAD**-0.5)).astype(BF16)
        return 0

    lax.fori_loop(0, rows // step, block, 0)
    dk_ref[...] = dk_acc[...].astype(BF16)
    dv_ref[...] = dv_acc[...].astype(BF16)


def attend_back(q, k, v, do, o, lse, bias):
    rows, width = q.shape
    keys = k.shape[0]
    pairs = width // PAIR
    qs = pl.BlockSpec((rows, PAIR), lambda h: (0, h))
    ks = pl.BlockSpec((keys, PAIR), lambda h: (0, h))
    ins, specs = [q, k, v, do, o, lse], [qs, ks, ks, qs, qs, qs]
    if bias is not None:
        ins.append(bias)
        specs.append(pl.BlockSpec((rows, keys), lambda h: (0, 0)))
    return pl.pallas_call(
        functools.partial(attend_back_kernel, bias is not None),
        grid=(pairs,),
        in_specs=specs,
        out_specs=[qs, ks, ks],
        out_shape=[
            jax.ShapeDtypeStruct((rows, width), BF16),
            jax.ShapeDtypeStruct((keys, width), BF16),
            jax.ShapeDtypeStruct((keys, width), BF16),
        ],
        scratch_shapes=[pltpu.VMEM((keys, PAIR), F32), pltpu.VMEM((keys, PAIR), F32)],
        compiler_params=pltpu.CompilerParams(vmem_limit_bytes=VMEM_LIMIT),
        name="attend_back",
    )(*ins)


def layer_norm(values, norm_gain, norm_shift):
    centre = values - jnp.mean(values, axis=-1, keepdims=True)
    spread = jnp.mean(centre * centre, axis=-1, keepdims=True)
    return centre * lax.rsqrt(spread + 1e-05) * norm_gain + norm_shift


def gelu_exact(values):
    return 0.5 * values * (1.0 + jax.scipy.special.erf(values * 0.7071067811865476))


def slot_links(parent, assignment):
    count = parent.shape[0]
    blocks = jnp.arange(count, dtype=jnp.int32)
    reached = (
        (parent[:, None] == blocks[None, :]) & (blocks[:, None] != blocks[None, :])
    ).astype(F32)
    turns = count.bit_length()
    for _ in range(turns):
        reached = jnp.minimum(
            reached + jnp.sum(reached[:, :, None] * reached[None, :, :], axis=1), 1.0
        )
    placed = (assignment[:, None] == blocks[None, :]).astype(F32)
    linked = jnp.sum(placed[:, :, None] * reached[None], axis=1)
    return jnp.sum(linked[:, None, :] * placed[None, :, :], axis=2)


def mask_bias(linked, first_query, query_count, key_count):
    query_pos = first_query + jnp.arange(query_count, dtype=jnp.int32)
    key_pos = jnp.arange(key_count, dtype=jnp.int32)
    slots = linked.shape[0]
    own = lax.dynamic_slice_in_dim(linked, first_query // BLK, query_count // BLK, 0)
    ancestral = jnp.broadcast_to(
        own[:, None, :, None], (query_count // BLK, BLK, slots, BLK)
    ).reshape(query_count, key_count)
    inside = (query_pos[:, None] // BLK == key_pos[None, :] // BLK) & (
        key_pos[None, :] <= query_pos[:, None]
    )
    return jnp.where((ancestral > 0.5) | inside, 0.0, -1e30).astype(BF16)


def mm(x, w):
    return jnp.dot(x, w, preferred_element_type=F32)


def mm_t(x, w):
    return lax.dot_general(x, w, (((1,), (1,)), ((), ())), preferred_element_type=F32)


def t_mm(x, y):
    return lax.dot_general(x, y, (((0,), (0,)), ((), ())), preferred_element_type=F32)


def col(x):
    return jnp.sum(x.astype(F32), axis=0)


def body(
    tokens, encoded, cotangent, parent, assignment, attn_in, attn_out, ffn_in, ffn_out, shifts, gains, ffn_bias
):
    sizes = (lax.axis_size("leaf"), lax.axis_size("path"))
    leafs, paths = sizes
    devices = leafs * paths
    scale = HEAD ** (-0.5)
    tokens, encoded, cotangent = tokens[0], encoded[0], cotangent[0]
    rows, width = tokens.shape
    hidden_width = ffn_in.shape[1]
    tree_rows = rows * paths
    n_shift, piece = shifts.shape
    n_gain = gains.shape[0]
    n_bias = ffn_bias.shape[0]

    small = jnp.concatenate([shifts.reshape(-1), gains.reshape(-1), ffn_bias])
    small_rows = -(-small.shape[0] // 4096) * 16
    small = jnp.pad(small, (0, small_rows * 256 - small.shape[0])).reshape(1, small_rows, 256)

    got = gather_all(
        sizes,
        [small, attn_in, attn_out, ffn_in[None], ffn_out[None]],
        [tokens, encoded],
        0,
    )
    small_all, w_in, w_out, w1, w2, all_tokens, all_encoded = got
    w_in = w_in.reshape(attn_in.shape[0], width, width)
    w_out = w_out.reshape(attn_out.shape[0], width, width)
    w1 = w1.reshape(width, hidden_width)
    w2 = w2.reshape(hidden_width, width)
    all_tokens = all_tokens.reshape(tree_rows, width)
    all_encoded = all_encoded.reshape(-1, width)
    small_all = small_all.reshape(devices, -1).astype(F32)
    shift = small_all[:, : n_shift * piece].reshape(devices, n_shift, piece)
    shift = shift.transpose(1, 0, 2).reshape(n_shift, width)
    gain = small_all[:, n_shift * piece : (n_shift + n_gain) * piece]
    gain = gain.reshape(devices, n_gain, piece).transpose(1, 0, 2).reshape(n_gain, width)
    start = (n_shift + n_gain) * piece
    b1 = small_all[:, start : start + n_bias].reshape(hidden_width)

    first_row = lax.axis_index("path") * rows
    linked = slot_links(parent[0], assignment[0])
    bias = mask_bias(linked, first_row, rows, tree_rows)

    q = ((mm(tokens, w_in[0]) + shift[0]) * scale).astype(BF16)
    k = mm(all_tokens, w_in[1]).astype(BF16)
    v = (mm(all_tokens, w_in[2]) + shift[1]).astype(BF16)
    ck = mm(all_encoded, w_in[4]).astype(BF16)
    cv = (mm(all_encoded, w_in[5]) + shift[4]).astype(BF16)
    attended, self_mass = attend(q, k, v, bias)
    branch = mm(attended, w_out[0]) + shift[2]
    first_norm, norm_back_one = jax.vjp(
        layer_norm, tokens.astype(F32) + branch, gain[0], shift[7]
    )
    first_low = first_norm.astype(BF16)
    cq = ((mm(first_low, w_in[3]) + shift[3]) * scale).astype(BF16)
    crossed, cross_mass = attend(cq, ck, cv, None)
    cross_branch = mm(crossed, w_out[1]) + shift[5]
    second_norm, norm_back_two = jax.vjp(layer_norm, first_norm + cross_branch, gain[1], shift[8])
    second_low = second_norm.astype(BF16)
    hidden_pre = mm(second_low, w1) + b1
    hidden, gelu_back = jax.vjp(gelu_exact, hidden_pre)
    hidden_low = hidden.astype(BF16)
    ffn_branch = mm(hidden_low, w2) + shift[6]
    result, norm_back_three = jax.vjp(layer_norm, second_norm + ffn_branch, gain[2], shift[9])
    output = result.astype(BF16)

    g_pre3, g_gain3, g_shift9 = norm_back_three(cotangent.astype(F32))
    g_ffn = g_pre3.astype(BF16)
    g_w2 = t_mm(hidden_low, g_ffn).astype(BF16)
    (g_hidden_pre,) = gelu_back(mm_t(g_ffn, w2))
    g_hidden = g_hidden_pre.astype(BF16)
    g_w1 = t_mm(second_low, g_hidden).astype(BF16)
    g_b1 = col(g_hidden)
    g_pre2, g_gain2, g_shift8 = norm_back_two(g_pre3 + mm_t(g_hidden, w1))
    g_cb = g_pre2.astype(BF16)
    g_wo1 = t_mm(crossed, g_cb).astype(BF16)
    g_crossed = mm_t(g_cb, w_out[1]).astype(BF16)
    g_cq, g_ck, g_cv = attend_back(cq, ck, cv, g_crossed, crossed, cross_mass, None)
    g_in3 = t_mm(first_low, g_cq).astype(BF16)
    g_in4 = t_mm(all_encoded, g_ck).astype(BF16)
    g_in5 = t_mm(all_encoded, g_cv).astype(BF16)
    g_enc = (mm_t(g_ck, w_in[4]) + mm_t(g_cv, w_in[5])).astype(BF16)
    g_pre1, g_gain1, g_shift7 = norm_back_one(g_pre2 + mm_t(g_cq, w_in[3]))
    g_br = g_pre1.astype(BF16)
    g_wo0 = t_mm(attended, g_br).astype(BF16)
    g_att = mm_t(g_br, w_out[0]).astype(BF16)
    g_q, g_k, g_v = attend_back(q, k, v, g_att, attended, self_mass, bias)
    g_in0 = t_mm(tokens, g_q).astype(BF16)
    g_in1 = t_mm(all_tokens, g_k).astype(BF16)
    g_in2 = t_mm(all_tokens, g_v).astype(BF16)
    g_tok = (mm_t(g_k, w_in[1]) + mm_t(g_v, w_in[2])).astype(BF16)
    g_tok_own = g_pre1 + mm_t(g_q, w_in[0])

    g_shifts = jnp.stack(
        [col(g_q), col(g_v), col(g_br), col(g_cq), col(g_cv), col(g_cb), col(g_ffn), g_shift7, g_shift8, g_shift9]
    )
    g_gains = jnp.stack([g_gain1, g_gain2, g_gain3])
    g_small = jnp.concatenate(
        [
            g_shifts.reshape(n_shift, devices, piece).transpose(1, 0, 2).reshape(devices, -1),
            g_gains.reshape(n_gain, devices, piece).transpose(1, 0, 2).reshape(devices, -1),
            g_b1.reshape(devices, n_bias),
        ],
        axis=1,
    )
    small_count = g_small.shape[1]
    g_small_rows = -(-small_count // 2048) * 8
    g_small = jnp.pad(g_small, ((0, 0), (0, g_small_rows * 256 - small_count)))
    g_small = g_small.reshape(1, leafs, paths, g_small_rows, 256)

    g_w_in = jnp.stack([g_in0, g_in1, g_in2, g_in3, g_in4, g_in5])
    g_w_out = jnp.stack([g_wo0, g_wo1])

    def spread(g):
        return g.reshape(g.shape[0], leafs, paths, g.shape[1] // devices, g.shape[2])

    o_w1, o_w2, o_out, o_in, o_small, o_tok, o_enc = scatter_all(
        sizes,
        [spread(g_w1[None]), spread(g_w2[None]), spread(g_w_out), spread(g_w_in), g_small],
        [g_tok.reshape(paths, rows, width), g_enc.reshape(paths, -1, width)],
        [g_tok_own, jnp.zeros(encoded.shape, F32)],
        1,
    )
    o_small = o_small.reshape(-1)
    o_shifts = o_small[: n_shift * piece].reshape(n_shift, piece)
    o_gains = o_small[n_shift * piece : (n_shift + n_gain) * piece].reshape(n_gain, piece)
    o_bias = o_small[start : start + n_bias]
    return (
        output[None],
        o_tok[None],
        o_enc[None],
        o_in,
        o_out,
        o_w1[0],
        o_w2[0],
        o_shifts,
        o_gains,
        o_bias,
    )


def solution(mesh):
    both = ("leaf", "path")
    rows = P("leaf", "path", None)
    return jax.shard_map(
        body,
        mesh=mesh,
        in_specs=(
            rows,
            rows,
            rows,
            P("leaf", None),
            P("leaf", None),
            P(None, both, None),
            P(None, both, None),
            P(both, None),
            P(both, None),
            P(None, both),
            P(None, both),
            P(both),
        ),
        out_specs=(
            rows,
            rows,
            rows,
            P(None, both, None),
            P(None, both, None),
            P(both, None),
            P(both, None),
            P(None, both),
            P(None, both),
            P(both),
        ),
        check_vma=False,
    )
```

time: 1570 us -> 1000 us (0.64)
  waiting for transfers between devices: 890 us -> 0 us
  Pallas kernels: 0 us -> 812 us
  blocking collectives: 218 us -> 0 us
  matrix products: 223 us -> 96.3 us
  local copies, waits for them, and re-layouts: 167 us -> 63.2 us
  other arithmetic: 51.1 us -> 20.4 us
    pallas_call x0 -> x6, Pallas kernels: none -> 812 us  [the longest x1 444 us: scatter_all(): pl.pallas_call(functools.partial(scatter_kernel, sizes, n, n_rows), out_s...]
    reduce_scatter x8 -> x0, waiting for transfers between devices: 681 us -> none  [the longest x1 142 us: body(): lax.psum_scatter(grad_w1, ('leaf', 'path'), scatter_dimension=0, tiled=True)]
    all_gather x8 -> x0, waiting for transfers between devices: 204 us -> none  [the longest x1 61.8 us: body(): lax.all_gather(value_rows, 'path', axis=1, tiled=True)]
    all_gather x2 -> x0, blocking collectives: 135 us -> none  [the longest x1 70.3 us: body(): lax.all_gather(gains, ('leaf', 'path'), axis=1, tiled=True)]
    dot_general x123 -> x30, matrix products: 223 us -> 96.3 us  [the longest x10 37.1 us: mm(): return jnp.dot(x, w, preferred_element_type=F32)]
    unnamed x2 -> x0, blocking collectives: 83.4 us -> none
    dynamic_slice x84 -> x0, local copies, waits for them, and re-layouts: 67 us -> none  [split_pair(): piece = lax.dynamic_slice_in_dim(matrix, offset, 2 * HEAD, 2)]
    dynamic_update_slice x36 -> x0, local copies, waits for them, and re-layouts: 27.6 us -> none  [the longest x12 11.6 us: per_pair(): lax.dynamic_update_slice_in_dim(grad_values, value_term.reshape(groups, k...]
  transfers between devices with their start and end apart: 16 -> 0, of which waited for: 13 -> 0; matrix products, arithmetic and copies ran while one was open for 13% -> 0% of each run, Pallas kernels for 0% -> 0%
where the time goes in v1:
time: 1000 us; the launch traced here: 994 us
  Pallas kernels  812 us (81%)
  matrix products  96.3 us (10%)
  local copies, waits for them, and re-layouts  63.2 us (6%)
  other arithmetic  20.4 us (2%)
    pallas_call x1, Pallas kernels, scatter_all(): pl.pallas_call(functools.partial(scatter_kernel, sizes, n, n_rows), out_s...  444 us
    pallas_call x1, Pallas kernels, gather_all(): pl.pallas_call(functools.partial(gather_kernel, sizes, len(shards), len(r...  253 us
    pallas_call x2, Pallas kernels, attend_back(): pl.pallas_call(functools.partial(attend_back_kernel, bias is not None), g...  70.1 us
    pallas_call x2, Pallas kernels, attend(): pl.pallas_call(functools.partial(attend_kernel, bias is not None), grid=(...  44.8 us
    dot_general x10, matrix products, mm(): return jnp.dot(x, w, preferred_element_type=F32)  37.1 us
    dot_general x10, matrix products, mm_t(): lax.dot_general(x, w, (((1,), (1,)), ((), ())), preferred_element_type=F32)  33.8 us
    unnamed x173, local copies, waits for them, and re-layouts  28.8 us
    dot_general x10, matrix products, t_mm(): lax.dot_general(x, y, (((0,), (0,)), ((), ())), preferred_element_type=F32)  25.3 us

profile of v1, /device:TPU:0, one launch (start us, length us, event | category | flops | bytes accessed | tf_op | source)
XLA Modules:
  0.0 993.8 jit_solution(18409945529002564323)
XLA Ops:
  3.5 253.0 %gather_all.1 = (bf16[1,8,4,16,256]{4,3,2,1,0:T(8,128)(2,1)}, bf16[6,8,4,24,768]{4,3,2,1,0:T(8,128)(2,1)}, bf16[2,8,4,24,768]{4,3,2,1,0:T(8,128)(2,1)}, bf16[1,8...) custom-call(bf16[1,16,256]{2,1,0:T(8,128)(2,1)} %reshape.773.refs_0_, ...), custom_call_target="tpu_custom_call" | custom-call | tf_op jit(solution)/shard_map/gather_all/pallas_call | solution.py:286
  260.6 6.5 fusion.44
  271.8 2.9 fusion.9.q_ref
  274.8 4.0 convolution_convert_fusion.2.k_ref
  278.9 6.3 add_convert_fusion.2.v_ref
  286.8 3.3 select_convert_fusion.refs_0_
  290.1 28.9 %attend.2 = (bf16[512,768]{1,0:T(8,128)(2,1)}, f32[512,768]{1,0:T(8,128)}) custom-call(bf16[512,768]{1,0:T(8,128)(2,1)} %fusion.9.q_ref, bf16[2048,768]{1,0:T(8,128)(2,1)} %convolution_convert_fusion.2.k_ref, bf16[2048,768]{1,0:T(8,128)(2,1)} %add_convert_fusion.2.v_ref, bf16[512,2048]{1,0:T(8,128)(2,1)} %select_convert_fusion.refs_0_), custom_call_target="tpu_custom_call" | custom-call | tf_op jit(solution)/shard_map/attend/pallas_call | solution.py:622
  328.6 3.9 add_convert_fusion.4.v_ref
  332.5 15.9 %attend.3 = (bf16[512,768]{1,0:T(8,128)(2,1)}, f32[512,768]{1,0:T(8,128)}) custom-call(bf16[512,768]{1,0:T(8,128)(2,1)} %multiply_convert_fusion.1.q_ref, bf16[1024,768]{1,0:T(8,128)(2,1)} %convolution_convert_fusion.3.k_ref, bf16[1024,768]{1,0:T(8,128)(2,1)} %add_convert_fusion.4.v_ref), custom_call_target="tpu_custom_call" | custom-call | tf_op jit(solution)/shard_map/attend/pallas_call | solution.py:622
  348.4 3.5 fusion.50
  354.2 6.7 multiply_convert_fusion
  369.4 7.8 convert_reduce_fusion
  377.2 4.8 convolution_convert_fusion.1
  382.0 4.3 convolution_convert_fusion
  386.3 3.7 multiply_reduce_fusion
  395.9 23.3 %attend_back.2 = (bf16[512,768]{1,0:T(8,128)(2,1)}, bf16[1024,768]{1,0:T(8,128)(2,1)}, bf16[1024,768]{1,0:T(8,128)(2,1)}) custom-call(bf16[512,768]{1,0:T(8,128)(2,1)} %multiply_convert_fusion.1.q_ref, bf16[1024,768]{1,0:T(8,128)(2,1)} %convolution_convert_fusion.3.k_ref, bf16[1024,768]{1,0:T(8,128)(2,1)} %add_convert_fusion.4.v_ref, ...), custom_call_target="tpu_custom_call" | custom-call | tf_op jit(solution)/shard_map/attend_back/pallas_call | solution.py:689
  419.3 4.0 multiply_reduce_fusion.1
  430.2 46.8 %attend_back.3 = (bf16[512,768]{1,0:T(8,128)(2,1)}, bf16[2048,768]{1,0:T(8,128)(2,1)}, bf16[2048,768]{1,0:T(8,128)(2,1)}) custom-call(bf16[512,768]{1,0:T(8,128)(2,1)} %fusion.9.q_ref, bf16[2048,768]{1,0:T(8,128)(2,1)} %convolution_convert_fusion.2.k_ref, bf16[2048,768]{1,0:T(8,128)(2,1)} %add_convert_fusion.2.v_ref, ...), custom_call_target="tpu_custom_call" | custom-call | tf_op jit(solution)/shard_map/attend_back/pallas_call | solution.py:689
  480.3 4.8 convolution_convert_fusion.8
  486.2 2.8 convolution_convert_fusion.7
  524.4 4.8 fusion.52
  529.3 4.1 add_convert_fusion
  540.3 443.7 %scatter_all.1 = (f32[1,24,3072]{2,1,0:T(8,128)}, f32[1,96,768]{2,1,0:T(8,128)}, f32[2,24,768]{2,1,0:T(8,128)}, f32[6,24,768]{2,1,0:T(8,128)}, f32[1,8,256]{2,1,...) custom-call(bf16[1,2,2,2,4,24,3072]{6,5,4,3,2,1,0:T(8,128)(2,1)} %bitcast.140, ...), custom_call_target="tpu_custom_call" | custom-call | tf_op jit(solution)/shard_map/scatter_all/pallas_call | solution.py:555
  986.8 2.7 copy.130
  (298 shorter events, 98.9 us)
Async XLA Ops:
  267.1 7.6 copy-start.12
  267.1 7.6 copy-start.20
  267.1 11.8 %copy-start.18 = (bf16[1,8,4,24,768]{4,3,2,1,0:T(8,128)(2,1)}, bf16[1,8,4,24,768]{4,3,2,1,0:T(8,128)(2,1)S(1)}, u32[]{:S(2)}) copy-start(bf16[1,8,4,24,768]{4,3,2,1,0:T(8,128)(2,1)S(1)} %get-tuple-element.83) | copy-start | bytes 3538948
  278.9 6.3 copy-start.60
  278.9 6.4 copy-start.51
  290.1 28.9 %copy-start.58 = (f32[768]{0:T(1024)S(1)}, f32[768]{0:T(1024)}, u32[]{:S(2)}) copy-start(f32[768]{0:T(1024)} %add.317) | copy-start | bytes 9220
  321.7 26.7 %copy-start.1 = (f32[512,768]{1,0:T(8,128)}, f32[512,768]{1,0:T(8,128)S(1)}, u32[]{:S(2)}) copy-start(f32[512,768]{1,0:T(8,128)S(1)} %get-tuple-element.103) | copy-start | bytes 4718596
  321.9 26.5 %copy-start.52 = (f32[768]{0:T(1024)}, f32[768]{0:T(1024)S(1)}, u32[]{:S(2)}) copy-start(f32[768]{0:T(1024)S(1)} %add.322) | copy-start | bytes 9220
  332.5 15.9 %copy-start.55 = (f32[768]{0:T(1024)S(1)}, f32[768]{0:T(1024)}, u32[]{:S(2)}) copy-start(f32[768]{0:T(1024)} %add.331) | copy-start | bytes 9220
  352.3 8.6 slice-start.2
  354.2 6.7 copy-start.54
  354.2 6.7 slice-start.3
  369.4 7.8 copy-start.5
  377.2 4.8 copy-start.69
  377.2 9.1 slice-start
  382.0 4.3 slice-start.1
  390.6 5.3 copy-start.8
  395.9 23.3 %copy-start.24 = (bf16[1,8,4,24,768]{4,3,2,1,0:T(8,128)(2,1)S(1)}, bf16[1,8,4,24,768]{4,3,2,1,0:T(8,128)(2,1)}, u32[]{:S(2)}) copy-start(bf16[1,8,4,24,768]{4,3,2,1,0:T(8,128)(2,1)} %get-tuple-element.82) | copy-start | bytes 3538948
  430.2 46.8 %copy-start.27 = (bf16[1,512,768]{2,1,0:T(8,128)(2,1)S(1)}, bf16[1,512,768]{2,1,0:T(8,128)(2,1)}, u32[]{:S(2)}) copy-start(bf16[1,512,768]{2,1,0:T(8,128)(2,1)} %param.12) | copy-start | bytes 2359300
  480.3 5.9 copy-start.9
  505.8 18.6 %copy-start.21 = (bf16[1,8,4,24,768]{4,3,2,1,0:T(8,128)(2,1)S(1)}, bf16[1,8,4,24,768]{4,3,2,1,0:T(8,128)(2,1)}, u32[]{:S(2)}) copy-start(bf16[1,8,4,24,768]{4,3,2,1,0:T(8,128)(2,1)} %copy-done.20) | copy-start | bytes 3538948
  524.4 4.8 copy-start.10
  524.4 4.8 copy-start.19
  529.2 4.1 copy-start.17
  (50 other events, 117.7 us)

commit v2 on v0

v2 whole, which is shorter than its diff:
```python
import functools

import jax
import jax.numpy as jnp
from jax import lax
from jax.experimental import pallas as pl
from jax.experimental.pallas import tpu as pltpu
from jax.sharding import PartitionSpec as P

HEAD = 64
BLK = 128
PAIR = 2 * HEAD
MESH = pl.DeviceIdType.MESH
F32 = jnp.float32
BF16 = jnp.bfloat16
VMEM_LIMIT = 62 * 1024 * 1024
ANY = pl.BlockSpec(memory_space=pl.ANY)
VMEM = pl.BlockSpec(memory_space=pltpu.VMEM)


class Shape:
    def __init__(self, leafs, paths):
        self.leafs, self.paths, self.half = leafs, paths, paths // 2
        outer = leafs // 2
        self.A = 2 if outer % 2 == 0 else 1
        self.B = outer // self.A


class Place:
    def __init__(self, shape):
        self.shape = shape
        self.leafs, self.paths, self.half = shape.leafs, shape.paths, shape.half
        self.A, self.B = shape.A, shape.B
        leaf = lax.axis_index("leaf")
        self.leaf, self.p = leaf, lax.axis_index("path")
        self.c = leaf % 2
        self.a = (leaf // 2) // self.B
        self.b = (leaf // 2) % self.B
        n = self.paths
        self.tree = jnp.where(self.p >= self.half, 1, 0)
        self.primary = self.c == self.tree
        self.pm = jnp.where(self.tree == 0, self.p, n - 1 - self.p)
        self.inward = jnp.where(self.tree == 0, 1, -1)
        self.own_rank = jnp.where(self.c == 0, self.p, n - 1 - self.p)
        self.block = jnp.where(self.primary, self.p, n - 1 - self.p)

    def leaf_at(self, a, b, c):
        return (a * self.B + b) * 2 + c

    def at_core(self):
        return (self.leaf_at(self.a, self.b, 1 - self.c), self.p)

    def at_a(self, a):
        return (self.leaf_at(a, self.b, self.c), self.p)

    def at_b(self, b):
        return (self.leaf_at(self.a, b, self.c), self.p)

    def at_p(self, p):
        return (self.leaf, clamp(p, self.paths))

    def at_mirror(self):
        return (self.leaf_at(self.a, self.b, 1 - self.c), self.paths - 1 - self.p)

    def shard_of_rank(self, rank):
        return jnp.where(self.tree == 0, rank, self.paths - 1 - rank)

    def line_p(self):
        return (self.paths, self.p, self.at_p)

    def line_a(self):
        return (self.A, self.a, self.at_a)

    def line_b(self):
        return (self.B, self.b, self.at_b)


def clamp(index, size):
    return jnp.clip(index, 0, size - 1)


def guarded(when, action):
    if when is None:
        action()
    else:

        @pl.when(when)
        def _():
            action()


def run(actions):
    for action in actions:
        action()


def greet(place, column, mirror):
    barrier = pltpu.get_barrier_semaphore()
    peers = 1

    def signal(to):
        pl.semaphore_signal(barrier, inc=1, device_id=to, device_id_type=MESH)

    signal(place.at_core())
    if column:
        for k in range(1, place.paths):
            for core in range(2):
                there = (place.p + k) % place.paths
                signal((place.leaf_at(place.a, place.b, core), there))
        peers = peers + 2 * (place.paths - 1)
    for size, pos, to in (place.line_a(), place.line_b()):
        if size == 1:
            continue
        if size == 2:
            signal(to(1 - pos))
            peers = peers + 1
            continue
        for step in (-1, 1):
            there = pos + step
            inside = (there >= 0) & (there < size)

            @pl.when(inside)
            def _():
                signal(to(clamp(there, size)))

            peers = peers + jnp.where(inside, 1, 0)
    if mirror and not column:

        @pl.when(jnp.logical_not(place.primary))
        def _():
            signal(place.at_mirror())

        peers = peers + jnp.where(place.primary, 0, 1)
    pl.semaphore_wait(barrier, peers)


class Mail:
    def __init__(self, send_sems, recv_sems, own_sems):
        self.send_sems, self.recv_sems, self.own_sems = send_sems, recv_sems, own_sems
        self.sends = self.recvs = self.owns = 0
        self.sent = []

    def new_recv(self, count=1):
        self.recvs += count
        return self.recvs - count

    def send(self, when, src, dst, to, recv):
        k = self.sends
        self.sends += 1
        copy = pltpu.make_async_remote_copy(
            src_ref=src,
            dst_ref=dst,
            send_sem=self.send_sems.at[k],
            recv_sem=self.recv_sems.at[recv],
            device_id=to,
            device_id_type=MESH,
        )
        self.sent.append((when, copy))
        return functools.partial(guarded, when, copy.start)

    def hear(self, when, landing, to, recv):
        copy = pltpu.make_async_remote_copy(
            src_ref=landing,
            dst_ref=landing,
            send_sem=self.send_sems.at[0],
            recv_sem=self.recv_sems.at[recv],
            device_id=to,
            device_id_type=MESH,
        )
        return functools.partial(guarded, when, copy.wait_recv)

    def post(self, when, src, dst, to, hear_when, landing):
        k = self.new_recv()
        return self.send(when, src, dst, to, k), self.hear(hear_when, landing, to, k)

    def local(self, when, src, dst):
        k = self.owns
        self.owns += 1
        copy = pltpu.make_async_copy(src, dst, self.own_sems.at[k])
        return functools.partial(guarded, when, copy.start), functools.partial(guarded, when, copy.wait)

    def finish(self):
        for when, copy in self.sent:
            guarded(when, copy.wait_send)


def mail_scratch(count=160, own=24):
    return [
        pltpu.SemaphoreType.DMA((count,)),
        pltpu.SemaphoreType.DMA((count,)),
        pltpu.SemaphoreType.DMA((own,)),
    ]


def flood(mail, line, views, first=None):
    size, pos, to = line
    steps = []
    if size == 1:
        return steps
    first = first if first is not None else views(pos)
    if size == 2:
        jobs = [
            mail.post(None, s, d, to(1 - pos), None, w)
            for s, d, w in zip(first, views(pos), views(1 - pos))
        ]
        return [([j[0] for j in jobs], [j[1] for j in jobs])]
    for step in range(1, size):
        starts, waits = [], []
        for sign in (1, -1):
            item = pos - sign * (step - 1)
            there = pos + sign
            when = (there >= 0) & (there < size) & (item >= 0) & (item < size)
            heard = pos - sign * step
            hear_when = (heard >= 0) & (heard < size)
            item_c = clamp(item, size)
            sources = first if step == 1 else views(item_c)
            for s, d, w in zip(sources, views(item_c), views(clamp(heard, size))):
                start, wait = mail.post(when, s, d, to(clamp(there, size)), hear_when, w)
                starts.append(start)
                waits.append(wait)
        steps.append((starts, waits))
    return steps


def chain(steps, first_starts=()):
    stages, pending = [], []
    for k, (starts, waits) in enumerate(steps):
        stages.append(functools.partial(run, pending + (list(first_starts) if k == 0 else []) + starts))
        pending = waits
    stages.append(functools.partial(run, pending))
    return stages


def half_columns(ref, leaf, h):
    width = ref.shape[-1] // 2
    return ref.at[:, leaf, :, :, pl.ds(h * width, width)]


def block_stages(mail, place, shards, block_views):
    n = place.paths
    own = [mail.local(None, s, d) for s, d in zip(shards, block_views(place.p))]
    starts, waits = [o[0] for o in own], [o[1] for o in own]
    lands = [mail.new_recv(n) for _ in shards]
    for k in range(1, n):
        there = (place.p + k) % n
        for s, d, w, land in zip(shards, block_views(place.p), block_views(there), lands):
            starts.append(mail.send(None, s, d, place.at_p(there), land + place.p))
            waits.append(mail.hear(None, w, place.at_p(there), land + there))
    return [functools.partial(run, starts), functools.partial(run, waits)]


def path_half(ref, h):
    n = ref.shape[1] // 2
    return ref.at[:, pl.ds(h * n, n)]


def spread_stages(mail, place, wholes, blocks=None):
    if (place.A, place.B) != (2, 2):
        return spread_lines(mail, place, wholes, blocks)
    a, b, c = place.a, place.b, place.c
    at = lambda w, a, b, c: w.at[:, place.leaf_at(a, b, c)]
    to_a, to_b, to_core = place.at_a(1 - a), place.at_b(1 - b), place.at_core()
    own = []
    sources = [at(w, a, b, c) for w in wholes]
    if blocks is not None:
        own = [mail.local(None, x, s) for x, s in zip(blocks, sources)]
        sources = list(blocks)
    urgent, calm, relay, near, far = [], [], [], [], []
    for w, s in zip(wholes, sources):
        mine, from_a, from_b = at(w, a, b, c), at(w, 1 - a, b, c), at(w, a, 1 - b, c)
        from_ab = at(w, 1 - a, 1 - b, c)

        def post(src, dst, to, landing, h):
            return mail.post(
                None, path_half(src, h), path_half(dst, h), to, None, path_half(landing, h)
            )

        urgent += [post(s, mine, to_b, from_b, 0), post(s, mine, to_a, from_a, 1)]
        calm += [post(s, mine, to_b, from_b, 1), post(s, mine, to_a, from_a, 0)]
        relay += [post(from_b, from_b, to_a, from_ab, 0), post(from_a, from_a, to_b, from_ab, 1)]
        near.append(mail.post(None, s, mine, to_core, None, at(w, a, b, 1 - c)))
        for x, y, l in ((1 - a, b, near), (a, 1 - b, near), (1 - a, 1 - b, far)):
            l.append(mail.post(None, at(w, x, y, c), at(w, x, y, c), to_core, None, at(w, x, y, 1 - c)))
    start = lambda jobs: run([j[0] for j in jobs])
    wait = lambda jobs: run([j[1] for j in jobs])
    first = near[::3]
    second = [j for k, j in enumerate(near) if k % 3]

    def opening():
        start(urgent)
        start(calm)
        start(first)
        run([o[0] for o in own])

    def passing():
        wait(urgent)
        start(relay)

    def sharing():
        wait(calm)
        run([o[1] for o in own])
        start(second)

    def ending():
        wait(relay)
        start(far)

    return [opening, passing, sharing, ending, lambda: wait(near + far)]


def spread_lines(mail, place, wholes, blocks=None):
    A, B, c = place.A, place.B, place.c

    def of_b(h, across_a):
        ays = range(A) if across_a else [place.a]
        return lambda i: [half_columns(w, place.leaf_at(a, i, c), h) for a in ays for w in wholes]

    def of_a(h, across_b):
        bees = range(B) if across_b else [place.b]
        return lambda i: [half_columns(w, place.leaf_at(i, b, c), h) for b in bees for w in wholes]

    own = []
    firsts = [None, None]
    sources = [w.at[:, place.leaf] for w in wholes]
    if blocks is not None:
        own = [mail.local(None, x, w.at[:, place.leaf]) for x, w in zip(blocks, wholes)]
        firsts = [
            [x.at[:, :, :, pl.ds(h * (x.shape[-1] // 2), x.shape[-1] // 2)] for x in blocks]
            for h in range(2)
        ]
        sources = list(blocks)
    line_a, line_b = place.line_a(), place.line_b()
    phases = [
        (flood(mail, line_b, of_b(0, False), firsts[0]), flood(mail, line_a, of_a(1, False), firsts[1])),
        (flood(mail, line_a, of_a(0, True)), flood(mail, line_b, of_b(1, True))),
    ]
    core = [
        mail.post(
            None,
            s,
            w.at[:, place.leaf],
            place.at_core(),
            None,
            w.at[:, place.leaf_at(place.a, place.b, 1 - c)],
        )
        for s, w in zip(sources, wholes)
    ]
    rest = []
    for offset in range(1, A * B):
        spot = (place.a * B + place.b + offset) % (A * B)
        for w in wholes:
            mine, other = w.at[:, spot * 2 + c], w.at[:, spot * 2 + 1 - c]
            rest.append(mail.post(None, mine, mine, place.at_core(), None, other))
    steps = []
    opening = [o[0] for o in own] + [j[0] for j in core]
    for n_phase, phase in enumerate(phases):
        before = [o[1] for o in own] if n_phase == 1 else []
        for s in range(max(len(f) for f in phase)):
            starts, waits = list(before), []
            before = []
            for f in phase:
                if s < len(f):
                    starts += f[s][0]
                    waits += f[s][1]
            steps.append((starts + opening, waits))
            opening = []
    steps.append((opening + [j[0] for j in rest], [j[1] for j in core + rest]))
    return chain(steps)


def pair_gather_stages(mail, place, shard, whole):
    n, h = place.paths, place.half
    rows = shard.shape[0] // 2
    half = lambda ref, u: ref.at[pl.ds(pl.multiple_of(u * rows, rows), rows)]
    lands, core_lands = mail.new_recv(n), mail.new_recv(n)
    own = mail.local(place.primary, shard, whole.at[place.p])
    starts = [own[0]]
    first = jnp.where(place.c == 0, 0, h)
    order = [(first + q) for q in range(h)]
    for u in range(2):
        for q in order:
            to = (place.leaf_at(place.a, place.b, u), q)
            away = jnp.logical_not((q == place.p) & (place.c == u))
            starts.append(
                mail.send(away, half(shard, u), half(whole.at[place.p], u), to, lands + place.p)
            )
    stages = [functools.partial(run, starts)]
    for r in range(n):
        j = place.shard_of_rank(r)
        item = whole.at[j]
        mine = place.primary & (place.p == j)
        got = jnp.logical_not(mine)
        actions = [
            mail.hear(got, half(item, place.c), place.at_core(), lands + j),
            mail.send(
                jnp.logical_not(place.p == j),
                half(item, place.c),
                half(item, place.c),
                place.at_core(),
                core_lands + j,
            ),
        ]
        stages.append(functools.partial(run, actions))
    rest = [own[1]]
    k = mail.new_recv()
    near = place.primary
    mate = whole.at[place.p]
    send_rest = mail.send(
        near, half(shard, place.c), half(mate, place.c), place.at_core(), k
    )
    stages[0] = functools.partial(run, starts + [send_rest])
    rest.append(mail.hear(jnp.logical_not(near), half(mate, 1 - place.c), place.at_core(), k))
    for r in range(n):
        j = place.shard_of_rank(r)
        rest.append(
            mail.hear(
                jnp.logical_not(place.p == j),
                half(whole.at[j], 1 - place.c),
                place.at_core(),
                core_lands + j,
            )
        )
    stages.append(functools.partial(run, rest))
    return stages


def mirror_stages(mail, place, own, mine):
    local = mail.local(place.primary, own, mine)
    other = jnp.logical_not(place.primary)
    start, wait = mail.post(other, own, mine, place.at_mirror(), other, mine)
    return [lambda: run([local[0], start]), lambda: run([local[1], wait])]


def add_rows(dst, src):
    lead = dst.shape[:-2]
    total = 1
    for extent in lead:
        total *= extent

    def body(i, _):
        index = []
        rest = i
        for extent in reversed(lead):
            index.insert(0, rest % extent)
            rest = rest // extent
        index = tuple(index)
        dst[index] = dst[index] + src[index]
        return 0

    if total == 1:
        body(0, 0)
    else:
        lax.fori_loop(0, total, body, 0)


def add_tall(dst, src):
    rows = dst.shape[0]
    step = 64 if rows % 64 == 0 else rows

    def body(r, _):
        at = pl.ds(pl.multiple_of(r * step, step), step)
        dst[at] = dst[at] + src[at]
        return 0

    lax.fori_loop(0, rows // step, body, 0)


def shift_sum(mail, line, mine, slots_up, slots_down, add):
    size, pos, to = line
    if size == 1:
        return []
    if size == 2:
        jobs = [
            mail.post(None, s, slot, to(1 - pos), None, slot)
            for s, slot in zip(mine(1 - pos), slots_up[0])
        ]

        def end():
            for job, dst, slot in zip(jobs, mine(pos), slots_up[0]):
                job[1]()
                add(dst, slot)

        return [lambda: run([j[0] for j in jobs]), end]
    stages = []
    for k in range(size - 1):
        early, actions = [], []
        for sign, slots in ((1, slots_up), (-1, slots_down)):
            dest = size - 1 - k if sign == 1 else k
            when = (pos < dest) if sign == 1 else (pos > dest)
            hear_when = (
                ((pos > 0) & (pos <= dest)) if sign == 1 else ((pos < size - 1) & (pos >= dest))
            )
            there = clamp(pos + sign, size)
            jobs = [
                mail.post(when, s, slot, to(there), None, slot)
                for s, slot in zip(mine(dest), slots[k])
            ]

            def take(jobs=jobs, dst_refs=mine(dest), slot_refs=slots[k]):
                for job, dst, slot in zip(jobs, dst_refs, slot_refs):
                    job[1]()
                    add(dst, slot)

            end = (pos == 0) if sign == 1 else (pos == size - 1)
            starts = functools.partial(run, [job[0] for job in jobs])
            early.append(functools.partial(guarded, end, starts))
            actions.append(functools.partial(guarded, hear_when, take))
            actions.append(functools.partial(guarded, jnp.logical_not(end), starts))
        stages.append(functools.partial(run, early + actions))
    return stages


def fold_scratch(shape, k, R, C, dtype):
    if (shape.A, shape.B) != (2, 2):
        return fold_lines_scratch(shape, k, R, C, dtype)
    block = (k, 2, 2, shape.paths, R, C)
    halves = (2, k, shape.paths // 2, R, C)
    return [pltpu.VMEM(block, dtype)] * 2 + [pltpu.VMEM(halves, dtype)] * 3 + [pltpu.VMEM((1, R, C), dtype)]


def fold_lines_scratch(shape, k, R, C, dtype):
    A, B, paths = shape.A, shape.B, shape.paths
    nb, na = max(B - 1, 1) * (2 if B > 2 else 1), max(A - 1, 1)
    return [
        pltpu.VMEM((k, A, B, paths, R, C), dtype),
        pltpu.VMEM((k, A, B, paths, R, C), dtype),
        pltpu.VMEM((nb, k, A, paths, R, C // 2), dtype),
        pltpu.VMEM((na, k, paths, R, C // 2), dtype),
        pltpu.VMEM((na, k, B, paths, R, C // 2), dtype),
        pltpu.VMEM((nb, k, paths, R, C // 2), dtype),
    ]


N_FOLD = 6


def up_down(ref, size):
    if size <= 2:
        return [[ref.at[0]]], None
    return (
        [[ref.at[k]] for k in range(size - 1)],
        [[ref.at[size - 1 + k]] for k in range(size - 1)],
    )


def fold_stages(mail, place, partial, scratch):
    if (place.A, place.B) != (2, 2):
        return fold_lines(mail, place, partial, scratch)
    a, b, c = place.a, place.b, place.c
    acc, got, far, direct, relayed = scratch[:5]
    own = mail.local(None, partial.at[:, :, :, c], acc)
    core = mail.post(None, partial.at[:, :, :, 1 - c], got, place.at_core(), None, got)
    to_a, to_b = place.at_a(1 - a), place.at_b(1 - b)
    of_a, of_b, of_ab = acc.at[:, 1 - a, b], acc.at[:, a, 1 - b], acc.at[:, 1 - a, 1 - b]
    mine = acc.at[:, a, b]

    def post(src, h, slot, to):
        return mail.post(None, path_half(src, h), slot, to, None, slot)

    urgent = [post(of_ab, 0, far.at[0], to_b), post(of_ab, 1, far.at[1], to_a)]
    calm = [post(of_b, 0, direct.at[0], to_b), post(of_a, 1, direct.at[1], to_a)]
    late = [post(of_a, 0, relayed.at[0], to_a), post(of_b, 1, relayed.at[1], to_b)]

    def join():
        own[1]()
        core[1]()
        add_rows(of_ab, got.at[:, 1 - a, 1 - b])
        run([j[0] for j in urgent])
        add_rows(of_b, got.at[:, a, 1 - b])
        calm[0][0]()
        add_rows(of_a, got.at[:, 1 - a, b])
        calm[1][0]()
        add_rows(mine, got.at[:, a, b])

    def passing():
        urgent[0][1]()
        add_rows(path_half(of_a, 0), far.at[0])
        late[0][0]()
        urgent[1][1]()
        add_rows(path_half(of_b, 1), far.at[1])
        late[1][0]()

    def taking():
        for h in range(2):
            calm[h][1]()
            add_rows(path_half(mine, h), direct.at[h])

    def ending():
        for h in range(2):
            late[h][1]()
            add_rows(path_half(mine, h), relayed.at[h])

    return [lambda: run([own[0], core[0]]), join, passing, taking, ending], mine


def fold_lines(mail, place, partial, scratch):
    c = place.c
    acc, got, sb0, sa0, sa1, sb1 = scratch
    own = mail.local(None, partial.at[:, :, :, c], acc)
    core = mail.post(None, partial.at[:, :, :, 1 - c], got, place.at_core(), None, got)
    width = acc.shape[-1] // 2
    left, right = pl.ds(0, width), pl.ds(width, width)

    def join():
        own[1]()
        core[1]()
        add_rows(acc, got)

    line_a, line_b = place.line_a(), place.line_b()
    h0_b = shift_sum(
        mail, line_b, lambda d: [acc.at[:, :, d, :, :, left]], *up_down(sb0, place.B), add_rows
    )
    h1_a = shift_sum(
        mail, line_a, lambda d: [acc.at[:, d, :, :, :, right]], *up_down(sa1, place.A), add_rows
    )
    h0_a = shift_sum(
        mail, line_a, lambda d: [acc.at[:, d, place.b, :, :, left]], *up_down(sa0, place.A), add_rows
    )
    h1_b = shift_sum(
        mail, line_b, lambda d: [acc.at[:, place.a, d, :, :, right]], *up_down(sb1, place.B), add_rows
    )

    def beside(one, two):
        return [
            functools.partial(run, [s[k] for s in (one, two) if k < len(s)])
            for k in range(max(len(one), len(two)))
        ]

    def joined(first, second):
        if not first or not second:
            return first + second
        return first[:-1] + [functools.partial(run, [first[-1], second[0]])] + second[1:]

    stages = joined(
        [lambda: run([own[0], core[0]]), join], beside(h0_b, h1_a)
    )
    stages = joined(stages, beside(h0_a, h1_b))
    return stages, acc.at[:, place.a, place.b]


def line_scratch(shape, k, R, C, dtype):
    return [pltpu.VMEM((max(shape.paths - 1, 1), k, R, C), dtype)]


def line_stages(mail, place, sums, slots, out):
    n = place.paths
    jobs = []
    for k in range(1, n):
        there = (place.p + k) % n
        slot = slots.at[k - 1]
        jobs.append(mail.post(None, sums.at[:, there], slot, place.at_p(there), None, slot))

    def end():
        run([j[1] for j in jobs])
        for j in range(out.shape[0]):
            total = sums[j, place.p].astype(F32)
            for k in range(n - 1):
                total = total + slots[k, j].astype(F32)
            out[j] = total.astype(out.dtype)

    return [lambda: run([j[0] for j in jobs]), end]


def pair_sum_scratch(shape, R, C):
    return [pltpu.VMEM((shape.paths, R // 2, C), BF16), pltpu.VMEM((shape.half, R, C), BF16)]


def pair_sum_stages(mail, place, part, scratch, out):
    n, h = place.paths, place.half
    core_slot, landing = scratch
    rows = part.shape[1] // 2
    half = lambda ref, u: ref.at[pl.ds(pl.multiple_of(u * rows, rows), rows)]
    lands = [mail.new_recv(2) for _ in range(h)]
    sends, sums = [], []
    for r in range(n - 1, -1, -1):
        j = place.shard_of_rank(r)
        item = part.at[j]
        send, hear = mail.post(
            None, half(item, 1 - place.c), core_slot.at[r], place.at_core(), None, core_slot.at[r]
        )
        owner = (place.leaf_at(place.a, place.b, place.tree), j)
        away = jnp.logical_not(place.primary & (place.p == j))
        out_copy = []
        for q in range(h):
            out_copy.append(
                mail.send(
                    away & (place.pm == q),
                    half(item, place.c),
                    half(landing.at[q], place.c),
                    owner,
                    lands[q] + place.c,
                )
            )

        def settle(hear=hear, item=item, slot=core_slot.at[r], out_copy=out_copy):
            hear()
            add_tall(half(item, place.c), slot)
            run(out_copy)

        sends.append(send)
        sums.append(settle)
    stages = [sends[0]]
    for k in range(1, n):
        stages.append(functools.partial(run, [sends[k], sums[k - 1]]))
    stages.append(sums[n - 1])

    def end():
        own_rank = jnp.where(place.c == 0, place.p, n - 1 - place.p)
        for q in range(h):
            for u in range(2):
                self_made = place.primary & (own_rank == q) & (place.c == u)
                mail.hear(
                    jnp.logical_not(self_made), half(landing.at[q], u), place.at_core(), lands[q] + u
                )()

        step = 64 if rows % 64 == 0 else rows
        for u in range(2):

            def body(i, _, u=u):
                at = pl.ds(pl.multiple_of(u * rows + i * step, step), step)
                for q in range(h):
                    self_made = place.primary & (own_rank == q) & (place.c == u)
                    term = jnp.where(self_made, part[place.p, at], landing[q, at]).astype(F32)
                    total = term if q == 0 else total + term
                out[at] = total
                return 0

            lax.fori_loop(0, rows // step, body, 0)

    return stages + [end]


def hooked(count, unit, hooks):
    def body(i, _):
        for at, stages in hooks.items():
            if stages:

                @pl.when(i == at)
                def _():
                    run(stages)

        unit(i)
        return 0

    lax.fori_loop(0, count, body, 0)


def kernel_call(kernel, name, collective_id, ins, in_specs, outs, out_specs, scratch):
    return pl.pallas_call(
        kernel,
        out_shape=outs,
        in_specs=in_specs,
        out_specs=out_specs,
        scratch_shapes=scratch,
        compiler_params=pltpu.CompilerParams(
            collective_id=collective_id,
            has_side_effects=True,
            vmem_limit_bytes=VMEM_LIMIT,
        )
        if collective_id is not None
        else pltpu.CompilerParams(vmem_limit_bytes=VMEM_LIMIT),
        name=name,
    )(*ins)


def dot(x, y, contract):
    return lax.dot_general(x, y, (contract, ((), ())), preferred_element_type=F32)


def mm(x, w):
    return dot(x, w, ((1,), (0,)))


def mm_t(x, w):
    return dot(x, w, ((1,), (1,)))


def t_mm(x, y):
    return dot(x, y, ((0,), (0,)))


def open_kernel(shape, column, mirror, sems):
    place = Place(shape)
    greet(place, column, mirror)
    return place, Mail(*sems)


def opening_kernel(shape, turns, tok, small, attn_in, links, all_tok, g_small, g_qkv, bias, *scratch):
    sems, (links_got, reach, spot) = scratch[:3], scratch[3:]
    place, mail = open_kernel(shape, True, False, sems)
    three = g_qkv.shape[0]
    to_core = mail.post(None, links, links_got, place.at_core(), None, links_got)
    to_core[0]()
    shards = [small, attn_in.at[pl.ds(0, three)]]
    wholes = [g_small, g_qkv]
    weights = block_stages(
        mail, place, shards, lambda i: [w.at[:, place.leaf, i] for w in wholes]
    )
    spread = spread_stages(mail, place, wholes)
    tokens = pair_gather_stages(mail, place, tok, all_tok)
    weights[0]()
    tokens[0]()
    to_core[1]()

    count = links.shape[0] // 2
    mine = jnp.where(place.primary, links[...], links_got[...])
    reach[...] = jnp.zeros_like(reach)
    spot[...] = jnp.zeros_like(spot)
    reach[pl.ds(0, count)] = mine[:count]
    spot[pl.ds(0, count)] = mine[count:]
    for _ in range(turns):
        r = reach[...]
        reach[...] = jnp.minimum(r + mm(r.astype(BF16), r.astype(BF16)), 1.0)
    placed = spot[...].astype(BF16)
    linked = mm_t(mm(placed, reach[...].astype(BF16)).astype(BF16), placed).astype(BF16)
    rows, keys = bias.shape
    step = min(128, rows)

    def fill(i, _):
        first = i * step
        at = pl.ds(pl.multiple_of(first, step), step)
        q_slot = (place.block * rows + first + lax.broadcasted_iota(jnp.int32, (step, 128), 0)) // BLK
        pick_q = (q_slot == lax.broadcasted_iota(jnp.int32, (step, 128), 1)).astype(F32)
        own = mm(pick_q.astype(BF16), linked).astype(BF16)
        k_slot = lax.broadcasted_iota(jnp.int32, (128, keys), 1) // BLK
        pick_k = (k_slot == lax.broadcasted_iota(jnp.int32, (128, keys), 0)).astype(F32)
        seen = mm(own, pick_k.astype(BF16))
        q_at = place.block * rows + first + lax.broadcasted_iota(jnp.int32, (step, keys), 0)
        k_at = lax.broadcasted_iota(jnp.int32, (step, keys), 1)
        inside = (q_at // BLK == k_at // BLK) & (k_at <= q_at)
        bias[at] = jnp.where((seen > 0.5) | inside, 0.0, -1e30).astype(bias.dtype)
        return 0

    run(weights[1:] + spread[:1])
    lax.fori_loop(0, rows // step, fill, 0)
    spread[1]()
    tokens[1]()
    spread[2]()
    tokens[2]()
    run(spread[3:])
    run(tokens[3:])
    mail.finish()


def attend_unit(q_ref, k_ref, v_ref, bias_ref, o_ref, lse_ref, row, step, pair):
    at = pl.ds(pl.multiple_of(row, step), step)
    cols = pl.ds(pl.multiple_of(pair * PAIR, PAIR), PAIR)
    lane = lax.broadcasted_iota(jnp.int32, (1, PAIR), 1)
    q = q_ref[at, cols]
    k = k_ref[:, cols]
    v = v_ref[:, cols]
    out = jnp.zeros((step, PAIR), F32)
    lse = jnp.zeros((step, PAIR), F32)
    for h in range(2):
        own = (lane >= HEAD) if h else (lane < HEAD)
        s = mm_t(jnp.where(own, q, jnp.zeros_like(q)), k)
        if bias_ref is not None:
            s = s + bias_ref[at].astype(F32)
        peak = jnp.max(s, axis=1, keepdims=True)
        e = jnp.exp(s - peak)
        mass = jnp.sum(e, axis=1, keepdims=True)
        o = mm(e.astype(BF16), v)
        out = jnp.where(own, o / mass, out)
        lse = jnp.where(own, peak + jnp.log(mass), lse)
    o_ref[at, cols] = out.astype(BF16)
    lse_ref[at, cols] = lse


def attend_back_unit(q_ref, k_ref, v_ref, bias_ref, do_ref, o_ref, lse_ref, dq_ref, dk_acc, dv_acc, row, step, pair):
    at = pl.ds(pl.multiple_of(row, step), step)
    cols = pl.ds(pl.multiple_of(pair * PAIR, PAIR), PAIR)
    lane = lax.broadcasted_iota(jnp.int32, (1, PAIR), 1)
    k = k_ref[:, cols]
    v = v_ref[:, cols]
    q = q_ref[at, cols]
    do = do_ref[at, cols]
    both = do.astype(F32) * o_ref[at, cols].astype(F32)
    lse_pair = lse_ref[at, cols]
    dq = jnp.zeros((step, PAIR), F32)
    for h in range(2):
        own = (lane >= HEAD) if h else (lane < HEAD)
        q_h = jnp.where(own, q, jnp.zeros_like(q))
        do_h = jnp.where(own, do, jnp.zeros_like(do))
        delta = jnp.sum(jnp.where(own, both, 0.0), axis=1, keepdims=True)
        lse = lse_pair[:, h * HEAD : h * HEAD + 1]
        s = mm_t(q_h, k)
        if bias_ref is not None:
            s = s + bias_ref[at].astype(F32)
        e = jnp.exp(s - lse)
        dp = mm_t(do_h, v)
        ds = (e * (dp - delta)).astype(BF16)
        dq = jnp.where(own, mm(ds, k), dq)
        dk_acc[...] += t_mm(ds, q_h)
        dv_acc[...] += t_mm(e.astype(BF16), do_h)
    dq_ref[at, cols] = dq.astype(BF16) * BF16(HEAD**-0.5)


def attend_units(rows, width):
    step = min(256, rows)
    return rows // step, step, width // PAIR


def self_kernel(
    shape, all_tok, w_qkv, vec, bias, enc, attn_in, attn_out, ffn_in, ffn_out,
    q, k, v, att, lse, all_enc, g_in, g_out, z_1, z_2, *sems,
):
    place, mail = open_kernel(shape, True, False, sems)
    n, rows, width = all_tok.shape
    three = g_in.shape[0]
    e = pair_gather_stages(mail, place, enc, all_enc)
    shards = [attn_in.at[pl.ds(attn_in.shape[0] - three, three)], attn_out]
    wholes = [g_in, g_out]
    w = block_stages(mail, place, shards, lambda i: [g.at[:, place.leaf, i] for g in wholes])
    w += spread_stages(mail, place, wholes)
    f = block_stages(mail, place, [ffn_in, ffn_out], lambda i: [z_1.at[:, i], z_2.at[:, i]])
    plan = []
    w[0]()
    e[0]()
    scale = HEAD**-0.5
    q[...] = ((mm(all_tok[place.block], w_qkv[0]) + vec[pl.ds(0, 1)]) * scale).astype(BF16)

    def project(i):
        x = all_tok[i]
        at = pl.ds(pl.multiple_of(i * rows, rows), rows)
        k[at] = mm(x, w_qkv[1]).astype(BF16)
        v[at] = (mm(x, w_qkv[2]) + vec[pl.ds(1, 1)]).astype(BF16)

    stages = w[1:3] + e[1:3] + w[3:4] + f[:1] + e[3:] + w[4:5] + f[1:2] + w[5:6] + f[2:3] + w[6:] + f[3:]
    blocks, step, pairs = attend_units(rows, width)
    total = n + blocks * pairs
    early, late = {}, {}
    for s, stage in enumerate(stages):
        at = min(1 + (s * (total - 2)) // len(stages), total - 1)
        if at < n:
            early.setdefault(at, []).append(stage)
        else:
            late.setdefault(at - n, []).append(stage)
    hooked(n, project, early)

    def unit(i):
        attend_unit(q, k, v, bias, att, lse, (i % blocks) * step, step, i // blocks)

    hooked(blocks * pairs, unit, late)
    mail.finish()


def cross_kernel(
    shape, cq, all_enc, w_k, w_v, vec, z_1, z_2, cot,
    ck, cv, crossed, lse, g_1, g_2, my_cot, *sems,
):
    place, mail = open_kernel(shape, False, True, sems)
    rows, width = cq.shape
    n, enc_rows, _ = all_enc.shape
    w = spread_stages(mail, place, [g_1, g_2], [z_1, z_2])
    c = mirror_stages(mail, place, cot, my_cot)
    w[0]()
    c[0]()

    def project(i):
        x = all_enc[i]
        at = pl.ds(pl.multiple_of(i * enc_rows, enc_rows), enc_rows)
        ck[at] = mm(x, w_k[...]).astype(BF16)
        cv[at] = (mm(x, w_v[...]) + vec[pl.ds(4, 1)]).astype(BF16)

    hooked(n, project, {})
    blocks, step, pairs = attend_units(rows, width)
    total = blocks * pairs
    late = {}
    stages = w[1:] + c[1:]
    for s, stage in enumerate(stages):
        late.setdefault(min((s + 1) * total // (len(stages)), total - 1), []).append(stage)

    def unit(i):
        attend_unit(cq, ck, cv, None, crossed, lse, (i % blocks) * step, step, i // blocks)

    hooked(total, unit, late)
    mail.finish()


def cross_back_kernel(
    shape, cq, ck, cv, do, o, lse, p_1, p_2, out_rows,
    dq, dk, dv, s_1, s_2, my_out, dk_acc, dv_acc, *scratch,
):
    sems, scratch = scratch[:3], scratch[3:]
    place, mail = open_kernel(shape, False, True, sems)
    rows, width = cq.shape
    f_1, sum_1 = fold_stages(mail, place, p_1, scratch[:N_FOLD])
    f_2, sum_2 = fold_stages(mail, place, p_2, scratch[N_FOLD:])
    c = mirror_stages(mail, place, out_rows, my_out)
    f_1[0]()
    blocks, step, pairs = attend_units(rows, width)
    total = blocks * pairs
    stages = f_2[:1] + c[:1]
    for k in range(max(len(f_1), len(f_2))):
        stages += f_1[k + 1 : k + 2] + f_2[k + 1 : k + 2]
    stages += c[1:]
    hooks = {}
    for s, stage in enumerate(stages):
        hooks.setdefault(min((s + 1) * total // len(stages), total - 1), []).append(stage)

    def unit(i):
        first = i % blocks == 0

        @pl.when(first)
        def _():
            dk_acc[...] = jnp.zeros_like(dk_acc)
            dv_acc[...] = jnp.zeros_like(dv_acc)

        pair = i // blocks
        attend_back_unit(cq, ck, cv, None, do, o, lse, dq, dk_acc, dv_acc, (i % blocks) * step, step, pair)

        @pl.when(i % blocks == blocks - 1)
        def _():
            cols = pl.ds(pl.multiple_of(pair * PAIR, PAIR), PAIR)
            dk[:, cols] = dk_acc[...].astype(BF16)
            dv[:, cols] = dv_acc[...].astype(BF16)

    hooked(total, unit, hooks)
    s_1[...] = sum_1[...]
    s_2[...] = sum_2[...]
    mail.finish()


def self_back_kernel(
    shape, q, k, v, bias, do, o, lse, z_1, z_2, p_in, p_out, p_enc,
    dq, dk, dv, o_1, o_2, o_in, o_out, o_enc, dk_acc, dv_acc, *scratch,
):
    sems, scratch = scratch[:3], scratch[3:]
    place, mail = open_kernel(shape, True, False, sems)
    rows, width = q.shape
    l_1 = line_stages(mail, place, z_1, scratch[0], o_1)
    l_2 = line_stages(mail, place, z_2, scratch[1], o_2)
    f_in, sum_in = fold_stages(mail, place, p_in, scratch[2 : 2 + N_FOLD])
    f_out, sum_out = fold_stages(mail, place, p_out, scratch[2 + N_FOLD : 2 + 2 * N_FOLD])
    rest = scratch[2 + 2 * N_FOLD :]
    l_in = line_stages(mail, place, sum_in, rest[0], o_in)
    l_out = line_stages(mail, place, sum_out, rest[1], o_out)
    e = pair_sum_stages(mail, place, p_enc, rest[2:], o_enc)
    f_in[0]()
    f_out[0]()
    l_1[0]()
    blocks, step, pairs = attend_units(rows, width)
    total = blocks * pairs
    stages = []
    tracks = [
        [f for two in zip(f_in[1:], f_out[1:]) for f in two] + l_in + l_out,
        l_1[1:] + l_2 + e,
    ]
    longest = max(len(t) for t in tracks)
    hooks = {}
    for t in tracks:
        for s, stage in enumerate(t):
            hooks.setdefault(min((s + 1) * total // len(t), total - 1), []).append(stage)

    def unit(i):
        @pl.when(i % blocks == 0)
        def _():
            dk_acc[...] = jnp.zeros_like(dk_acc)
            dv_acc[...] = jnp.zeros_like(dv_acc)

        pair = i // blocks
        attend_back_unit(q, k, v, bias, do, o, lse, dq, dk_acc, dv_acc, (i % blocks) * step, step, pair)

        @pl.when(i % blocks == blocks - 1)
        def _():
            cols = pl.ds(pl.multiple_of(pair * PAIR, PAIR), PAIR)
            dk[:, cols] = dk_acc[...].astype(BF16)
            dv[:, cols] = dv_acc[...].astype(BF16)

    hooked(total, unit, hooks)
    mail.finish()


def closing_kernel(shape, p_qkv, p_small, p_tok, o_qkv, o_small, o_tok, *scratch):
    sems, scratch = scratch[:3], scratch[3:]
    place, mail = open_kernel(shape, True, False, sems)
    f_q, sum_q = fold_stages(mail, place, p_qkv, scratch[:N_FOLD])
    f_s, sum_s = fold_stages(mail, place, p_small, scratch[N_FOLD : 2 * N_FOLD])
    rest = scratch[2 * N_FOLD :]
    l_q = line_stages(mail, place, sum_q, rest[0], o_qkv)
    l_s = line_stages(mail, place, sum_s, rest[1], o_small)
    t = pair_sum_stages(mail, place, p_tok, rest[2:], o_tok)
    a = [functools.partial(run, two) for two in zip(f_q, f_s)]
    b = [functools.partial(run, two) for two in zip(l_q, l_s)]
    a[0]()
    t[0]()
    tracks = [a[1:], t[1:]]
    for k in range(max(len(x) for x in tracks)):
        for x in tracks:
            if k < len(x) and x[k] is not t[-1]:
                x[k]()
    run(b)
    t[-1]()
    mail.finish()


def layer_norm(values, norm_gain, norm_shift):
    centre = values - jnp.mean(values, axis=-1, keepdims=True)
    spread = jnp.mean(centre * centre, axis=-1, keepdims=True)
    return centre * lax.rsqrt(spread + 1e-05) * norm_gain + norm_shift


def gelu_exact(values):
    return 0.5 * values * (1.0 + jax.scipy.special.erf(values * 0.7071067811865476))


def col(x):
    return jnp.sum(x.astype(F32), axis=0)


def body(
    tokens, encoded, cotangent, parent, assignment, attn_in, attn_out, ffn_in, ffn_out, shifts, gains, ffn_bias
):
    shape = Shape(lax.axis_size("leaf"), lax.axis_size("path"))
    leafs, paths = shape.leafs, shape.paths
    devices = leafs * paths
    scale = HEAD ** (-0.5)
    tokens, encoded, cotangent = tokens[0], encoded[0], cotangent[0]
    rows, width = tokens.shape
    enc_rows = encoded.shape[0]
    hidden_width = ffn_in.shape[1]
    tree_rows, tree_enc = rows * paths, enc_rows * paths
    piece = shifts.shape[1]
    n_shift, n_gain, n_bias = shifts.shape[0], gains.shape[0], ffn_bias.shape[0]
    n_vec = n_shift + n_gain
    ffn_in, ffn_out = ffn_in[None], ffn_out[None]

    def sds(shape_, dtype=BF16):
        return jax.ShapeDtypeStruct(shape_, dtype)

    small = jnp.concatenate([shifts.reshape(-1), gains.reshape(-1), ffn_bias])
    small_rows = -(-small.shape[0] // 4096) * 16
    small = jnp.pad(small, (0, small_rows * 256 - small.shape[0])).reshape(1, small_rows, 256)
    blocks = parent.shape[1]
    ids = jnp.arange(blocks, dtype=jnp.int32)
    lanes = jnp.arange(128, dtype=jnp.int32)
    links = jnp.concatenate(
        [
            (parent[0][:, None] == lanes[None, :]) & (ids[:, None] != lanes[None, :]),
            assignment[0][:, None] == lanes[None, :],
        ]
    ).astype(F32)

    three = 3
    all_tok, g_small, w_qkv, bias = kernel_call(
        functools.partial(opening_kernel, shape, blocks.bit_length()),
        "opening",
        0,
        [tokens, small, attn_in, links],
        [ANY, ANY, ANY, VMEM],
        [
            sds((paths, rows, width)),
            sds((1, leafs, paths) + small.shape[1:]),
            sds((three, leafs, paths) + attn_in.shape[1:]),
            sds((rows, tree_rows)),
        ],
        [ANY, ANY, ANY, VMEM],
        mail_scratch()
        + [pltpu.VMEM(links.shape, F32), pltpu.VMEM((128, 128), F32), pltpu.VMEM((128, 128), F32)],
    )
    flat = g_small.reshape(devices, -1)
    vec = flat[:, : n_vec * piece].reshape(devices, n_vec, piece).transpose(1, 0, 2)
    vec = vec.reshape(n_vec, width).astype(F32)
    shift, gain = vec[:n_shift], vec[n_shift:]
    b1 = flat[:, n_vec * piece : n_vec * piece + n_bias].reshape(hidden_width).astype(F32)
    w_qkv = w_qkv.reshape(three, width, width)

    rest_in = attn_in.shape[0] - three
    q, k, v, attended, self_mass, all_enc, w_in, w_out, z_1, z_2 = kernel_call(
        functools.partial(self_kernel, shape),
        "self_attention",
        1,
        [all_tok, w_qkv, vec, bias, encoded, attn_in, attn_out, ffn_in, ffn_out],
        [VMEM] * 4 + [ANY] * 5,
        [
            sds((rows, width)),
            sds((tree_rows, width)),
            sds((tree_rows, width)),
            sds((rows, width)),
            sds((rows, width), F32),
            sds((paths, enc_rows, width)),
            sds((rest_in, leafs, paths) + attn_in.shape[1:]),
            sds((attn_out.shape[0], leafs, paths) + attn_out.shape[1:]),
            sds((1, paths) + ffn_in.shape[1:]),
            sds((1, paths) + ffn_out.shape[1:]),
        ],
        [VMEM] * 5 + [ANY] * 5,
        mail_scratch(),
    )
    w_in = w_in.reshape(rest_in, width, width)
    w_out = w_out.reshape(attn_out.shape[0], width, width)

    p = lax.axis_index("path")
    upper = p >= shape.half
    primary = (lax.axis_index("leaf") % 2 == 1) == upper
    block = jnp.where(primary, p, paths - 1 - p)
    my_tokens = lax.dynamic_index_in_dim(all_tok, block, 0, False)
    branch = mm(attended, w_out[0]) + shift[2]
    first_norm, norm_back_one = jax.vjp(
        layer_norm, my_tokens.astype(F32) + branch, gain[0], shift[7]
    )
    first_low = first_norm.astype(BF16)
    cq = ((mm(first_low, w_in[0]) + shift[3]) * scale).astype(BF16)
    ck, cv, crossed, cross_mass, w1, w2, my_cot = kernel_call(
        functools.partial(cross_kernel, shape),
        "cross_attention",
        2,
        [cq, all_enc, w_in[1], w_in[2], vec, z_1, z_2, cotangent],
        [VMEM] * 5 + [ANY] * 3,
        [
            sds((tree_enc, width)),
            sds((tree_enc, width)),
            sds((rows, width)),
            sds((rows, width), F32),
            sds((1, leafs, paths) + ffn_in.shape[1:]),
            sds((1, leafs, paths) + ffn_out.shape[1:]),
            sds((rows, width)),
        ],
        [VMEM] * 4 + [ANY] * 3,
        mail_scratch(),
    )
    w1 = w1.reshape(width, hidden_width)
    w2 = w2.reshape(hidden_width, width)
    cross_branch = mm(crossed, w_out[1]) + shift[5]
    second_norm, norm_back_two = jax.vjp(layer_norm, first_norm + cross_branch, gain[1], shift[8])
    second_low = second_norm.astype(BF16)
    hidden_pre = mm(second_low, w1) + b1
    hidden, gelu_back = jax.vjp(gelu_exact, hidden_pre)
    hidden_low = hidden.astype(BF16)
    ffn_branch = mm(hidden_low, w2) + shift[6]
    result, norm_back_three = jax.vjp(layer_norm, second_norm + ffn_branch, gain[2], shift[9])
    output = result.astype(BF16)

    g_pre3, g_gain3, g_shift9 = norm_back_three(my_cot.astype(F32))
    g_ffn = g_pre3.astype(BF16)
    g_w2 = t_mm(hidden_low, g_ffn).astype(BF16)
    (g_hidden_pre,) = gelu_back(mm_t(g_ffn, w2))
    g_hidden = g_hidden_pre.astype(BF16)
    g_w1 = t_mm(second_low, g_hidden).astype(BF16)
    g_b1 = col(g_hidden)
    g_pre2, g_gain2, g_shift8 = norm_back_two(g_pre3 + mm_t(g_hidden, w1))
    g_cb = g_pre2.astype(BF16)
    g_crossed = mm_t(g_cb, w_out[1]).astype(BF16)

    def spread(g):
        return g.reshape(
            g.shape[0], shape.A, shape.B, 2, paths, g.shape[1] // devices, g.shape[2]
        )

    r1, r2 = ffn_in.shape[1:], ffn_out.shape[1:]
    g_cq, g_ck, g_cv, s_1, s_2, output = kernel_call(
        functools.partial(cross_back_kernel, shape),
        "cross_back",
        3,
        [cq, ck, cv, g_crossed, crossed, cross_mass, spread(g_w1[None]), spread(g_w2[None]), output],
        [VMEM] * 6 + [ANY] * 3,
        [
            sds((rows, width)),
            sds((tree_enc, width)),
            sds((tree_enc, width)),
            sds((1, paths) + r1),
            sds((1, paths) + r2),
            sds((rows, width)),
        ],
        [VMEM] * 5 + [ANY],
        [pltpu.VMEM((tree_enc, PAIR), F32)] * 2
        + mail_scratch()
        + fold_scratch(shape, 1, *r1, BF16)
        + fold_scratch(shape, 1, *r2, BF16),
    )
    flat_enc = all_enc.reshape(tree_enc, width)
    g_wo1 = t_mm(crossed, g_cb).astype(BF16)
    g_in3 = t_mm(first_low, g_cq).astype(BF16)
    g_in4 = t_mm(flat_enc, g_ck).astype(BF16)
    g_in5 = t_mm(flat_enc, g_cv).astype(BF16)
    g_enc = (mm_t(g_ck, w_in[1]) + mm_t(g_cv, w_in[2])).astype(BF16)
    g_pre1, g_gain1, g_shift7 = norm_back_one(g_pre2 + mm_t(g_cq, w_in[0]))
    g_br = g_pre1.astype(BF16)
    g_wo0 = t_mm(attended, g_br).astype(BF16)
    g_att = mm_t(g_br, w_out[0]).astype(BF16)
    p_in = spread(jnp.stack([g_in3, g_in4, g_in5]))
    p_out = spread(jnp.stack([g_wo0, g_wo1]))
    ri = attn_in.shape[1:]
    g_q, g_k, g_v, o_w1, o_w2, o_in, o_out, o_enc = kernel_call(
        functools.partial(self_back_kernel, shape),
        "self_back",
        4,
        [q, k, v, bias, g_att, attended, self_mass, s_1, s_2, p_in, p_out, g_enc.reshape(paths, enc_rows, width)],
        [VMEM] * 9 + [ANY] * 2 + [VMEM],
        [
            sds((rows, width)),
            sds((tree_rows, width)),
            sds((tree_rows, width)),
            sds((1,) + r1, F32),
            sds((1,) + r2, F32),
            sds((rest_in,) + ri, F32),
            sds((2,) + ri, F32),
            sds((enc_rows, width), F32),
        ],
        [VMEM] * 8,
        [pltpu.VMEM((tree_rows, PAIR), F32)] * 2
        + mail_scratch()
        + line_scratch(shape, 1, *r1, BF16)
        + line_scratch(shape, 1, *r2, BF16)
        + fold_scratch(shape, rest_in, *ri, BF16)
        + fold_scratch(shape, 2, *ri, BF16)
        + line_scratch(shape, rest_in, *ri, BF16)
        + line_scratch(shape, 2, *ri, BF16)
        + pair_sum_scratch(shape, enc_rows, width),
    )
    flat_tok = all_tok.reshape(tree_rows, width)
    g_in0 = t_mm(my_tokens, g_q).astype(BF16)
    g_in1 = t_mm(flat_tok, g_k).astype(BF16)
    g_in2 = t_mm(flat_tok, g_v).astype(BF16)
    g_tok = (mm_t(g_k, w_qkv[1]) + mm_t(g_v, w_qkv[2])).reshape(paths, rows, width)
    g_own = g_pre1 + mm_t(g_q, w_qkv[0])
    mine = (jnp.arange(paths) == block)[:, None, None]
    g_tok = jnp.where(mine, g_tok + g_own[None], g_tok).astype(BF16)

    g_vec = jnp.stack(
        [
            col(g_q), col(g_v), col(g_br), col(g_cq), col(g_cv), col(g_cb), col(g_ffn),
            g_shift7, g_shift8, g_shift9, g_gain1, g_gain2, g_gain3,
        ]
    )
    g_small = jnp.concatenate(
        [
            g_vec.reshape(n_vec, devices, piece).transpose(1, 0, 2).reshape(devices, -1),
            g_b1.reshape(devices, n_bias),
        ],
        axis=1,
    )
    small_count = g_small.shape[1]
    g_small_rows = -(-small_count // 2048) * 8
    g_small = jnp.pad(g_small, ((0, 0), (0, g_small_rows * 256 - small_count)))
    p_small = g_small.reshape(1, shape.A, shape.B, 2, paths, g_small_rows, 256)
    p_qkv = spread(jnp.stack([g_in0, g_in1, g_in2]))
    o_qkv, o_small, o_tok = kernel_call(
        functools.partial(closing_kernel, shape),
        "closing",
        5,
        [p_qkv, p_small, g_tok],
        [ANY, ANY, VMEM],
        [
            sds((three,) + ri, F32),
            sds((1, g_small_rows, 256), F32),
            sds((rows, width), F32),
        ],
        [VMEM] * 3,
        mail_scratch()
        + fold_scratch(shape, three, *ri, BF16)
        + fold_scratch(shape, 1, g_small_rows, 256, F32)
        + line_scratch(shape, three, *ri, BF16)
        + line_scratch(shape, 1, g_small_rows, 256, F32)
        + pair_sum_scratch(shape, rows, width),
    )
    o_small = o_small.reshape(-1)
    o_vec = o_small[: n_vec * piece].reshape(n_vec, piece)
    return (
        output[None],
        o_tok[None],
        o_enc[None],
        jnp.concatenate([o_qkv, o_in]),
        o_out,
        o_w1[0],
        o_w2[0],
        o_vec[:n_shift],
        o_vec[n_shift:],
        o_small[n_vec * piece : n_vec * piece + n_bias],
    )


def solution(mesh):
    both = ("leaf", "path")
    rows = P("leaf", "path", None)
    weights = (P(None, both, None), P(None, both, None), P(both, None), P(both, None), P(None, both), P(None, both), P(both))
    return jax.shard_map(
        body,
        mesh=mesh,
        in_specs=(rows, rows, rows, P("leaf", None), P("leaf", None)) + weights,
        out_specs=(rows, rows, rows) + weights,
        check_vma=False,
    )
```

time: 1570 us -> 597 us (0.38)
  waiting for transfers between devices: 890 us -> 0 us
  Pallas kernels: 0 us -> 426 us
  blocking collectives: 218 us -> 0 us
  matrix products: 223 us -> 74.1 us
  local copies, waits for them, and re-layouts: 167 us -> 58.6 us
  other arithmetic: 51.1 us -> 28.2 us
    reduce_scatter x8 -> x0, waiting for transfers between devices: 681 us -> none  [the longest x1 142 us: body(): lax.psum_scatter(grad_w1, ('leaf', 'path'), scatter_dimension=0, tiled=True)]
    pallas_call x0 -> x6, Pallas kernels: none -> 426 us  [kernel_call(): pl.pallas_call(kernel, out_shape=outs, in_specs=in_specs, out_specs=out_s...]
    all_gather x8 -> x0, waiting for transfers between devices: 204 us -> none  [the longest x1 61.8 us: body(): lax.all_gather(value_rows, 'path', axis=1, tiled=True)]
    dot_general x123 -> x25, matrix products: 223 us -> 74.1 us  [dot(): lax.dot_general(x, y, (contract, ((), ())), preferred_element_type=F32)]
    all_gather x2 -> x0, blocking collectives: 135 us -> none  [the longest x1 70.3 us: body(): lax.all_gather(gains, ('leaf', 'path'), axis=1, tiled=True)]
    unnamed x2 -> x0, blocking collectives: 83.4 us -> none
    dynamic_slice x84 -> x0, local copies, waits for them, and re-layouts: 67 us -> none  [split_pair(): piece = lax.dynamic_slice_in_dim(matrix, offset, 2 * HEAD, 2)]
    dynamic_update_slice x36 -> x0, local copies, waits for them, and re-layouts: 27.6 us -> none  [the longest x12 11.6 us: per_pair(): lax.dynamic_update_slice_in_dim(grad_values, value_term.reshape(groups, k...]
  transfers between devices with their start and end apart: 16 -> 0, of which waited for: 13 -> 0; matrix products, arithmetic and copies ran while one was open for 13% -> 0% of each run, Pallas kernels for 0% -> 0%
where the time goes in v2:
time: 597 us; the launch traced here: 589 us
  Pallas kernels  426 us (71%)
  matrix products  74.1 us (12%)
  local copies, waits for them, and re-layouts  58.6 us (10%)
  other arithmetic  28.2 us (5%)
    pallas_call x6, Pallas kernels, kernel_call(): pl.pallas_call(kernel, out_shape=outs, in_specs=in_specs, out_specs=out_s...  426 us
    dot_general x25, matrix products, dot(): lax.dot_general(x, y, (contract, ((), ())), preferred_element_type=F32)  74.1 us
    unnamed x102, local copies, waits for them, and re-layouts  28.1 us
    another operation x14, local copies, waits for them, and re-layouts, body(): jnp.stack([col(g_q), col(g_v), col(g_br), col(g_cq), col(g_cv), col(g_cb)...  14.6 us

profile of v2, /device:TPU:0, one launch (start us, length us, event | category | flops | bytes accessed | tf_op | source)
XLA Modules:
  0.0 588.7 jit_solution(4992240170917420200)
XLA Ops:
  4.9 53.9 %opening.1 = (bf16[4,512,768]{2,1,0:T(8,128)(2,1)}, bf16[1,8,4,16,256]{4,3,2,1,0:T(8,128)(2,1)}, bf16[3,8,4,24,768]{4,3,2,1,0:T(8,128)(2,1)}, bf16[512,2048]{1,0:T(8,128)(2,1)}) custom-call(bf16[512,768]{1,0:T(8,128)(2,1)} %bitcast.136, bf16[1,16,256]{2,1,0:T(8,128)(2,1)} %reshape.268.small, bf16[6,24,768]{2,1,0:T(8,128)(2,1)} %attn_in.3, ...), custom_call_target="tpu_custom_call" | custom-call | tf_op jit(solution)/shard_map/opening/pallas_call | solution.py:749
  60.8 85.3 %self_attention.1 = (bf16[512,768]{1,0:T(8,128)(2,1)}, bf16[2048,768]{1,0:T(8,128)(2,1)}, bf16[2048,768]{1,0:T(8,128)(2,1)}, bf16[512,768]{1,0:T(8,128)(2,1)}, f...) custom-call(bf16[4,512,768]{2,1,0:T(8,128)(2,1)} %get-tuple-element., ...), custom_call_target="tpu_custom_call" | custom-call | tf_op jit(solution)/shard_map/self_attention/pallas_call | solution.py:749
  146.1 4.0 fusion.28
  152.0 2.6 fusion.31
  157.7 71.2 %cross_attention.1 = (bf16[1024,768]{1,0:T(8,128)(2,1)}, bf16[1024,768]{1,0:T(8,128)(2,1)}, bf16[512,768]{1,0:T(8,128)(2,1)}, f32[512,768]{1,0:T(8,128)}, bf16[1...) custom-call(bf16[512,768]{1,0:T(8,128)(2,1)} %multiply_convert_fusion.1.cq, ...), custom_call_target="tpu_custom_call" | custom-call | tf_op jit(solution)/shard_map/cross_attention/pallas_call | solution.py:749
  229.0 2.5 fusion.32
  232.3 8.1 %multiply_convert_fusion = (bf16[512,3072]{1,0:T(8,128)(2,1)}, f32[512,3072]{1,0:T(8,128)}) fusion(f32[3072]{0:T(1024)S(1)} %reshape.281, bf16[768,3072]{1,0:T(8,128)(2,1)} %bitcast.154, f32[512,768]{1,0:T(8,128)S(1)} %get-tuple-element.131, f32[768]{0:T(1024)S(1)} %add.176, f32[768]{0:T(1024)S(1)} %mul.215, f32[512]{0:T(512)S(1)} %fusion.16, ...), kind=kOutput, calls=%fused_computation.5 | convolution fusion | flops 2427322368 | bytes 15751168 | tf_op jit(solution)/shard_map/dot_general | solution.py:767
  240.6 6.5 %fusion.33 = (f32[512]{0:T(512)S(1)}, f32[512,768]{1,0:T(8,128)S(1)}) fusion(f32[768]{0:T(1024)S(1)} %add.183, bf16[512,3072]{1,0:T(8,128)(2,1)} %get-tuple-element.132, bf16[3072,768]{1,0:T(8,128)(2,1)} %bitcast.158, f32[768]{0:T(1024)S(1)} %add.176, f32[768]{0:T(1024)S(1)} %mul.215, f32[512]{0:T(512)S(1)} %fusion.16, f32[512,768]{1,0:T(8,128)} %copy-done.1, ...), kind=kOutput, calls=%fused_computation.120 | convolution fusion | flops 2418671104 | bytes 11025408 | tf_op jit(solution)/shard_map/dot_general | solution.py:767
  247.6 2.4 fusion.4
  250.2 2.9 fusion.26
  253.9 7.5 %convert_reduce_fusion = (f32[3072]{0:T(1024)S(1)}, bf16[512,3072]{1,0:T(8,128)(2,1)S(1)}) fusion(f32[512,3072]{1,0:T(8,128)S(1)} %copy-done.36, f32[3072]{0:T(1024)S(1)} %reshape.281, bf16[512,768]{1,0:T(8,128)(2,1)S(1)} %get-tuple-element.96, bf16[3072,768]{1,0:T(8,128)(2,1)} %bitcast.159), kind=kOutput, calls=%fused_computation.2 | convolution fusion | flops 2441081856 | bytes 14966784 | tf_op jit(solution)/shard_map/dot_general | solution.py:767
  261.5 3.7 multiply_reduce_fusion
  269.5 4.8 convolution_convert_fusion.1
  274.3 4.4 convolution_convert_fusion
  278.7 58.7 %cross_back.1 = (bf16[512,768]{1,0:T(8,128)(2,1)}, bf16[1024,768]{1,0:T(8,128)(2,1)}, bf16[1024,768]{1,0:T(8,128)(2,1)}, bf16[1,4,24,3072]{3,2,1,0:T(8,128)(2,1)...) custom-call(bf16[512,768]{1,0:T(8,128)(2,1)} %multiply_convert_fusion.1.cq, ...), custom_call_target="tpu_custom_call" | custom-call | tf_op jit(solution)/shard_map/cross_back/pallas_call | solution.py:749
  337.3 3.8 multiply_reduce_fusion.1
  357.0 2.6 add_convert_fusion.1
  359.5 96.5 %self_back.1 = (bf16[512,768]{1,0:T(8,128)(2,1)}, bf16[2048,768]{1,0:T(8,128)(2,1)}, bf16[2048,768]{1,0:T(8,128)(2,1)}, f32[1,24,3072]{2,1,0:T(8,128)}, f32[1,96...) custom-call(bf16[512,768]{1,0:T(8,128)(2,1)} %get-tuple-element.66.q, ...), custom_call_target="tpu_custom_call" | custom-call | tf_op jit(solution)/shard_map/self_back/pallas_call | solution.py:749
  456.1 5.7 convolution_convert_fusion.2
  461.8 2.8 convolution_convert_fusion.3
  508.6 2.6 fusion.35
  511.3 2.7 convolution_add_fusion
  514.9 2.6 fusion.p_tok
  517.4 60.5 %closing.1 = (f32[3,24,768]{2,1,0:T(8,128)}, f32[1,8,256]{2,1,0:T(8,128)}, f32[512,768]{1,0:T(8,128)}) custom-call(bf16[3,2,2,2,4,24,768]{6,5,4,3,2,1,0:T(8,128)(2,1)} %pad_maximum_fusion.1.p_qkv, f32[1,2,2,2,4,8,256]{6,5,4,3,2,1,0:T(8,128)} %bitcast.132, bf16[4,512,768]{2,1,0:T(8,128)(2,1)} %fusion.p_tok), custom_call_target="tpu_custom_call" | custom-call | tf_op jit(solution)/shard_map/closing/pallas_call | solution.py:749
  (201 shorter events, 88.9 us)
Async XLA Ops:
  146.1 4.3 copy-start.11
  231.5 8.9 %copy-start.1 = (f32[512,768]{1,0:T(8,128)}, f32[512,768]{1,0:T(8,128)S(1)}, u32[]{:S(2)}) copy-start(f32[512,768]{1,0:T(8,128)S(1)} %get-tuple-element.131) | copy-start | bytes 4718596
  250.2 3.7 copy-start.36
  253.1 8.4 %slice-start = ((s8[4718592]{0:T(1024)(128)(4,1)}), s8[4194304]{0:T(1024)(128)(4,1)S(1)}, s32[]{:S(2)}) async-start(s8[4718592]{0:T(1024)(128)(4,1)} %bitcast.155), calls=%async_computation | async-start | bytes 8388608
  253.9 7.6 %copy-start.2 = (f32[512,768]{1,0:T(8,128)S(1)}, f32[512,768]{1,0:T(8,128)}, u32[]{:S(2)}) copy-start(f32[512,768]{1,0:T(8,128)} %copy-done.1) | copy-start | bytes 4718596
  253.9 7.6 %slice-start.1 = ((s8[4718592]{0:T(1024)(128)(4,1)}), s8[524288]{0:T(1024)(128)(4,1)S(1)}, s32[]{:S(2)}) async-start(s8[4718592]{0:T(1024)(128)(4,1)} %bitcast.155), calls=%async_computation.1 | async-start | bytes 1048576
  269.5 4.8 copy-start.37
  341.8 3.6 copy-start.3
  341.8 3.5 copy-start.31
  349.8 2.2 copy-start.19
  349.8 2.2 copy-start.26
  456.1 5.7 copy-start.10
  456.1 5.7 copy-start.33
  461.8 2.8 copy-start.22
  465.4 4.4 copy-start.8
  473.6 33.0 %copy-start = (bf16[3,8,4,24,768]{4,3,2,1,0:T(8,128)(2,1)S(1)}, bf16[3,8,4,24,768]{4,3,2,1,0:T(8,128)(2,1)}, u32[]{:S(2)}) copy-start(bf16[3,8,4,24,768]{4,3,2,1,0:T(8,128)(2,1)} %get-tuple-element.49) | copy-start | bytes 10616836
  508.6 2.7 copy-start.9
  511.2 2.8 copy-start.4
  511.2 2.8 copy-start.23
  511.3 2.8 copy-start.32
  517.4 60.5 %copy-start.29 = (f32[3,24,768]{2,1,0:T(8,128)S(1)}, f32[3,24,768]{2,1,0:T(8,128)}, u32[]{:S(2)}) copy-start(f32[3,24,768]{2,1,0:T(8,128)} %get-tuple-element.81) | copy-start | bytes 663556
  517.4 65.1 %copy-start.20 = (bf16[512,768]{1,0:T(8,128)(2,1)S(1)}, bf16[512,768]{1,0:T(8,128)(2,1)}, u32[]{:S(2)}) copy-start(bf16[512,768]{1,0:T(8,128)(2,1)} %get-tuple-element.65) | copy-start | bytes 2359300
  578.0 5.5 copy-start.13
  585.1 2.4 copy-start.27
  (16 other events, 25.2 us)

commit v3 on v2

--- a/solution.py
+++ b/solution.py
@@ -374,42 +374,41 @@
     half = lambda ref, u: ref.at[pl.ds(pl.multiple_of(u * rows, rows), rows)]
     lands, core_lands = mail.new_recv(n), mail.new_recv(n)
     own = mail.local(place.primary, shard, whole.at[place.p])
-    starts = [own[0]]
     first = jnp.where(place.c == 0, 0, h)
-    order = [(first + q) for q in range(h)]
+    edge = jnp.where(place.c == 0, h - 1, h)
+    starts = []
     for u in range(2):
-        for q in order:
+        for q in range(h):
+            q = first + q
             to = (place.leaf_at(place.a, place.b, u), q)
-            away = jnp.logical_not((q == place.p) & (place.c == u))
+            near = place.primary & jnp.logical_not((q == place.p) & (place.c == u))
+            away = near | (jnp.logical_not(place.primary) & (q == edge))
             starts.append(
                 mail.send(away, half(shard, u), half(whole.at[place.p], u), to, lands + place.p)
             )
+    k = mail.new_recv()
+    mate = whole.at[place.p]
+    starts.append(
+        mail.send(place.primary, half(shard, place.c), half(mate, place.c), place.at_core(), k)
+    )
+    starts.append(own[0])
     stages = [functools.partial(run, starts)]
+    outward = place.at_p(place.p - place.inward)
     for r in range(n):
         j = place.shard_of_rank(r)
-        item = whole.at[j]
-        mine = place.primary & (place.p == j)
-        got = jnp.logical_not(mine)
-        actions = [
-            mail.hear(got, half(item, place.c), place.at_core(), lands + j),
-            mail.send(
-                jnp.logical_not(place.p == j),
-                half(item, place.c),
-                half(item, place.c),
-                place.at_core(),
-                core_lands + j,
-            ),
-        ]
+        item = half(whole.at[j], place.c)
+        got = jnp.logical_not(place.primary & (place.p == j))
+        actions = [mail.hear(got, item, place.at_core(), lands + j)]
+        if r >= h and h > 1:
+            actions.append(mail.send(place.pm > 0, item, item, outward, lands + j))
+        actions.append(
+            mail.send(jnp.logical_not(place.p == j), item, item, place.at_core(), core_lands + j)
+        )
         stages.append(functools.partial(run, actions))
     rest = [own[1]]
-    k = mail.new_recv()
-    near = place.primary
-    mate = whole.at[place.p]
-    send_rest = mail.send(
-        near, half(shard, place.c), half(mate, place.c), place.at_core(), k
-    )
-    stages[0] = functools.partial(run, starts + [send_rest])
-    rest.append(mail.hear(jnp.logical_not(near), half(mate, 1 - place.c), place.at_core(), k))
+    rest.append(
+        mail.hear(jnp.logical_not(place.primary), half(mate, 1 - place.c), place.at_core(), k)
+    )
     for r in range(n):
         j = place.shard_of_rank(r)
         rest.append(
@@ -662,78 +661,119 @@
 
 
 def pair_sum_scratch(shape, R, C):
-    return [pltpu.VMEM((shape.paths, R // 2, C), BF16), pltpu.VMEM((shape.half, R, C), BF16)]
+    return [
+        pltpu.VMEM((shape.paths, R // 2, C), BF16),
+        pltpu.VMEM((shape.paths, R // 2, C), BF16),
+        pltpu.VMEM((shape.half, R, C), BF16),
+    ]
 
 
 def pair_sum_stages(mail, place, part, scratch, out):
     n, h = place.paths, place.half
-    core_slot, landing = scratch
+    core_slot, in_slot, landing = scratch
     rows = part.shape[1] // 2
     half = lambda ref, u: ref.at[pl.ds(pl.multiple_of(u * rows, rows), rows)]
     lands = [mail.new_recv(2) for _ in range(h)]
-    sends, sums = [], []
+    inner = place.at_p(place.p + place.inward)
+    sends, sums, passes = [], [], []
     for r in range(n - 1, -1, -1):
         j = place.shard_of_rank(r)
         item = part.at[j]
+        mine = half(item, place.c)
         send, hear = mail.post(
             None, half(item, 1 - place.c), core_slot.at[r], place.at_core(), None, core_slot.at[r]
         )
         owner = (place.leaf_at(place.a, place.b, place.tree), j)
-        away = jnp.logical_not(place.primary & (place.p == j))
-        out_copy = []
-        for q in range(h):
-            out_copy.append(
-                mail.send(
-                    away & (place.pm == q),
-                    half(item, place.c),
-                    half(landing.at[q], place.c),
-                    owner,
-                    lands[q] + place.c,
+        leave = []
+        if r >= h:
+            k = mail.new_recv()
+            slot = in_slot.at[r]
+            in_send = mail.send(place.pm < h - 1, mine, slot, inner, k)
+            in_hear = mail.hear(None, slot, place.at_core(), k)
+            go = mail.send(
+                place.pm == h - 1, mine, half(landing.at[h - 1], place.c), owner, lands[h - 1] + place.c
+            )
+
+            def inward(in_send=in_send, in_hear=in_hear, mine=mine, slot=slot, go=go):
+                if h > 1:
+
+                    @pl.when(place.pm > 0)
+                    def _():
+                        in_hear()
+                        add_tall(mine, slot)
+
+                    in_send()
+                go()
+
+            passes.append(inward)
+        else:
+            away = jnp.logical_not(place.primary & (place.p == j))
+            for q in range(h):
+                leave.append(
+                    mail.send(
+                        away & (place.pm == q),
+                        mine,
+                        half(landing.at[q], place.c),
+                        owner,
+                        lands[q] + place.c,
+                    )
                 )
-            )
-
-        def settle(hear=hear, item=item, slot=core_slot.at[r], out_copy=out_copy):
+
+        def settle(hear=hear, mine=mine, slot=core_slot.at[r], leave=leave):
             hear()
-            add_tall(half(item, place.c), slot)
-            run(out_copy)
+            add_tall(mine, slot)
+            run(leave)
 
         sends.append(send)
         sums.append(settle)
-    stages = [sends[0]]
+    stages = [[sends[0]]]
     for k in range(1, n):
-        stages.append(functools.partial(run, [sends[k], sums[k - 1]]))
-    stages.append(sums[n - 1])
+        stages.append([sends[k], sums[k - 1]])
+    stages.append([sums[n - 1]])
+    for k, step in enumerate(passes):
+        stages[k + 1].append(step)
 
     def end():
-        own_rank = jnp.where(place.c == 0, place.p, n - 1 - place.p)
         for q in range(h):
             for u in range(2):
-                self_made = place.primary & (own_rank == q) & (place.c == u)
-                mail.hear(
-                    jnp.logical_not(self_made), half(landing.at[q], u), place.at_core(), lands[q] + u
-                )()
+                self_made = place.primary & (place.own_rank == q) & (place.c == u)
+                comes = jnp.logical_not(self_made) & (place.primary | (q == h - 1))
+                mail.hear(comes, half(landing.at[q], u), place.at_core(), lands[q] + u)()
 
         step = 64 if rows % 64 == 0 else rows
         for u in range(2):
 
             def body(i, _, u=u):
                 at = pl.ds(pl.multiple_of(u * rows + i * step, step), step)
-                for q in range(h):
-                    self_made = place.primary & (own_rank == q) & (place.c == u)
-                    term = jnp.where(self_made, part[place.p, at], landing[q, at]).astype(F32)
-                    total = term if q == 0 else total + term
-                out[at] = total
+
+                @pl.when(place.primary)
+                def _():
+                    for q in range(h):
+                        self_made = (place.own_rank == q) & (place.c == u)
+                        term = jnp.where(self_made, part[place.p, at], landing[q, at]).astype(F32)
+                        total = term if q == 0 else total + term
+                    out[at] = total
+
+                @pl.when(jnp.logical_not(place.primary))
+                def _():
+                    out[at] = landing[h - 1, at].astype(F32)
+
                 return 0
 
             lax.fori_loop(0, rows // step, body, 0)
 
-    return stages + [end]
+    return [functools.partial(run, x) for x in stages] + [end]
+
+
+def at_units(hooks, stages, units):
+    for stage, unit in zip(stages, units, strict=True):
+        hooks.setdefault(unit, []).append(stage)
 
 
 def hooked(count, unit, hooks):
     def body(i, _):
         for at, stages in hooks.items():
-            if stages:
+            if at < count:
 
                 @pl.when(i == at)
                 def _():
@@ -743,6 +783,9 @@
         return 0
 
     lax.fori_loop(0, count, body, 0)
+    for at in sorted(hooks):
+        if at >= count:
+            run(hooks[at])
 
 
 def kernel_call(kernel, name, collective_id, ins, in_specs, outs, out_specs, scratch):
@@ -832,13 +875,12 @@
         return 0
 
     run(weights[1:] + spread[:1])
+    run(tokens[1:-3])
+    spread[1]()
     lax.fori_loop(0, rows // step, fill, 0)
-    spread[1]()
-    tokens[1]()
-    spread[2]()
-    tokens[2]()
-    run(spread[3:])
-    run(tokens[3:])
+    run(tokens[-3:-1])
+    run(spread[2:])
+    tokens[-1]()
     mail.finish()
 
 
@@ -902,7 +944,7 @@
 
 def self_kernel(
     shape, all_tok, w_qkv, vec, bias, enc, attn_in, attn_out, ffn_in, ffn_out,
-    q, k, v, att, lse, all_enc, g_in, g_out, z_1, z_2, *sems,
+    q, k, v, att, lse, all_enc, g_in, g_out, g_1, z_2, *sems,
 ):
     place, mail = open_kernel(shape, True, False, sems)
     n, rows, width = all_tok.shape
@@ -912,10 +954,10 @@
     wholes = [g_in, g_out]
     w = block_stages(mail, place, shards, lambda i: [g.at[:, place.leaf, i] for g in wholes])
     w += spread_stages(mail, place, wholes)
-    f = block_stages(mail, place, [ffn_in, ffn_out], lambda i: [z_1.at[:, i], z_2.at[:, i]])
-    plan = []
+    f = block_stages(mail, place, [ffn_in], lambda i: [g_1.at[:, place.leaf, i]])
+    f += spread_stages(mail, place, [g_1])
+    z = block_stages(mail, place, [ffn_out], lambda i: [z_2.at[:, i]])
     w[0]()
-    e[0]()
     scale = HEAD**-0.5
     q[...] = ((mm(all_tok[place.block], w_qkv[0]) + vec[pl.ds(0, 1)]) * scale).astype(BF16)
 
@@ -925,16 +967,20 @@
         k[at] = mm(x, w_qkv[1]).astype(BF16)
         v[at] = (mm(x, w_qkv[2]) + vec[pl.ds(1, 1)]).astype(BF16)
 
-    stages = w[1:3] + e[1:3] + w[3:4] + f[:1] + e[3:] + w[4:5] + f[1:2] + w[5:6] + f[2:3] + w[6:] + f[3:]
     blocks, step, pairs = attend_units(rows, width)
-    total = n + blocks * pairs
-    early, late = {}, {}
-    for s, stage in enumerate(stages):
-        at = min(1 + (s * (total - 2)) // len(stages), total - 1)
-        if at < n:
-            early.setdefault(at, []).append(stage)
-        else:
-            late.setdefault(at - n, []).append(stage)
+    units = blocks * pairs
+    t = lambda x: n + (x * units) // 12
+    hooks, last = {}, n + units
+    at_units(hooks, w[1:3], [t(1)] * 2)
+    at_units(hooks, e[:1], [1])
+    at_units(hooks, f[:1], [2])
+    at_units(hooks, z[:1], [t(1)])
+    at_units(hooks, w[3:5] + w[5:-1], [t(4), t(6)] + [t(7)] * len(w[5:-1]))
+    at_units(hooks, e[1:-1], [t(3)] * len(e[1:3]) + [t(8)] * len(e[3:-1]))
+    at_units(hooks, f[1:5] + f[5:-1], [t(6), t(6), t(10), t(11)] + [last] * len(f[5:-1]))
+    at_units(hooks, e[-1:] + w[-1:] + f[-1:] + z[1:], [last] * 4)
+    early = {at: stages for at, stages in hooks.items() if at < n}
+    late = {at - n: stages for at, stages in hooks.items() if at >= n}
     hooked(n, project, early)
 
     def unit(i):
@@ -944,31 +990,77 @@
     mail.finish()
 
 
+ROOT_HALF = 0.7071067811865476
+NORM = 0.3989422804014327
+
+
+def normed(v):
+    centre = v - jnp.mean(v, axis=1, keepdims=True)
+    inverse = lax.rsqrt(jnp.mean(centre * centre, axis=1, keepdims=True) + 1e-05)
+    return centre * inverse, inverse
+
+
+def normed_back(g, gain, hat, inverse):
+    gx = g * gain
+    mean_g = jnp.mean(gx, axis=1, keepdims=True)
+    mean_gh = jnp.mean(gx * hat, axis=1, keepdims=True)
+    return inverse * (gx - mean_g - hat * mean_gh)
+
+
+def by_rows(rows, action):
+    step = min(128, rows)
+
+    def one(i, _):
+        action(pl.ds(pl.multiple_of(i * step, step), step))
+        return 0
+
+    lax.fori_loop(0, rows // step, one, 0)
+
+
+def row_sum(x):
+    return jnp.sum(x, axis=0, keepdims=True)
+
+
 def cross_kernel(
-    shape, cq, all_enc, w_k, w_v, vec, z_1, z_2, cot,
-    ck, cv, crossed, lse, g_1, g_2, my_cot, *sems,
+    shape, shifts, att, all_tok, all_enc, w_in, w_out, vec, z_2, cot,
+    hat1, inv1, first_low, cq, ck, cv, crossed, lse, g_2, my_cot, toks, *sems,
 ):
     place, mail = open_kernel(shape, False, True, sems)
     rows, width = cq.shape
     n, enc_rows, _ = all_enc.shape
-    w = spread_stages(mail, place, [g_1, g_2], [z_1, z_2])
+    w = spread_stages(mail, place, [g_2], [z_2])
     c = mirror_stages(mail, place, cot, my_cot)
+    mine = mail.local(None, all_tok.at[place.block], toks)
+    mine[0]()
     w[0]()
     c[0]()
 
     def project(i):
         x = all_enc[i]
         at = pl.ds(pl.multiple_of(i * enc_rows, enc_rows), enc_rows)
-        ck[at] = mm(x, w_k[...]).astype(BF16)
-        cv[at] = (mm(x, w_v[...]) + vec[pl.ds(4, 1)]).astype(BF16)
+        ck[at] = mm(x, w_in[1]).astype(BF16)
+        cv[at] = (mm(x, w_in[2]) + vec[pl.ds(4, 1)]).astype(BF16)
 
     hooked(n, project, {})
+    mine[1]()
+    scale = HEAD**-0.5
+
+    def first(at):
+        v = toks[at].astype(F32) + mm(att[at], w_out[0]) + vec[pl.ds(2, 1)]
+        hat, inverse = normed(v)
+        hat1[at] = hat
+        inv1[at] = jnp.broadcast_to(inverse, (hat.shape[0], 128))
+        low = (hat * vec[pl.ds(shifts, 1)] + vec[pl.ds(7, 1)]).astype(BF16)
+        first_low[at] = low
+        cq[at] = ((mm(low, w_in[0]) + vec[pl.ds(3, 1)]) * scale).astype(BF16)
+
+    by_rows(rows, first)
     blocks, step, pairs = attend_units(rows, width)
     total = blocks * pairs
+    t = lambda x: (x * total) // 12
     late = {}
-    stages = w[1:] + c[1:]
-    for s, stage in enumerate(stages):
-        late.setdefault(min((s + 1) * total // (len(stages)), total - 1), []).append(stage)
+    at_units(late, w[1:], [t(1), t(4), t(5)] + [total] * (len(w) - 4))
+    at_units(late, c[1:], [total])
 
     def unit(i):
         attend_unit(cq, ck, cv, None, crossed, lse, (i % blocks) * step, step, i // blocks)
@@ -977,26 +1069,99 @@
     mail.finish()
 
 
+def ffn_kernel(
+    shifts, hat1, crossed, w_out, w1, w2, vec, b1, cot,
+    out, gw1, gw2, gwo, g_crossed, g_pre2, sums, gb1,
+    hat2, inv2, low2, acc, slope, hidden, g_pre3, g_ffn, acc2, g_cb,
+):
+    rows, width = crossed.shape
+    wide = hidden.shape[1]
+    piece = 512
+    gain = lambda i: vec[pl.ds(shifts + i, 1)]
+    shift = lambda i: vec[pl.ds(i, 1)]
+    sums[...] = jnp.zeros_like(sums)
+
+    def second(at):
+        v = hat1[at] * gain(0) + shift(7) + mm(crossed[at], w_out[1]) + shift(5)
+        hat, inverse = normed(v)
+        hat2[at] = hat
+        inv2[at] = jnp.broadcast_to(inverse, (hat.shape[0], 128))
+        low2[at] = (hat * gain(1) + shift(8)).astype(BF16)
+
+    by_rows(rows, second)
+    acc[...] = jnp.zeros_like(acc)
+
+    def up(j, _):
+        cols = pl.ds(pl.multiple_of(j * piece, piece), piece)
+        u = mm(low2[...], w1[:, cols]) + b1[:, cols]
+        phi = 0.5 * (1.0 + lax.erf(u * ROOT_HALF))
+        slope[:, cols] = phi + u * jnp.exp(-0.5 * u * u) * NORM
+        h = (u * phi).astype(BF16)
+        hidden[:, cols] = h
+        acc[...] += mm(h, w2[cols])
+        return 0
+
+    lax.fori_loop(0, wide // piece, up, 0)
+
+    def third(at):
+        v = hat2[at] * gain(1) + shift(8) + acc[at] + shift(6)
+        hat, inverse = normed(v)
+        out[at] = (hat * gain(2) + shift(9)).astype(BF16)
+        g = cot[at].astype(F32)
+        sums[pl.ds(shifts + 2, 1)] += row_sum(g * hat)
+        sums[pl.ds(9, 1)] += row_sum(g)
+        back = normed_back(g, gain(2), hat, inverse)
+        g_pre3[at] = back
+        low = back.astype(BF16)
+        g_ffn[at] = low
+        sums[pl.ds(6, 1)] += row_sum(low.astype(F32))
+
+    by_rows(rows, third)
+    acc2[...] = jnp.zeros_like(acc2)
+
+    def down(j, _):
+        cols = pl.ds(pl.multiple_of(j * piece, piece), piece)
+        g = (mm_t(g_ffn[...], w2[cols]) * slope[:, cols]).astype(BF16)
+        gb1[:, cols] = row_sum(g.astype(F32))
+        gw2[cols] = t_mm(hidden[:, cols], g_ffn[...]).astype(BF16)
+        gw1[:, cols] = t_mm(low2[...], g).astype(BF16)
+        acc2[...] += mm_t(g, w1[:, cols])
+        return 0
+
+    lax.fori_loop(0, wide // piece, down, 0)
+
+    def back_two(at):
+        g = g_pre3[at] + acc2[at]
+        hat = hat2[at]
+        sums[pl.ds(shifts + 1, 1)] += row_sum(g * hat)
+        sums[pl.ds(8, 1)] += row_sum(g)
+        back = normed_back(g, gain(1), hat, inv2[at, :1])
+        g_pre2[at] = back
+        low = back.astype(BF16)
+        g_cb[at] = low
+        sums[pl.ds(5, 1)] += row_sum(low.astype(F32))
+        g_crossed[at] = mm_t(low, w_out[1]).astype(BF16)
+
+    by_rows(rows, back_two)
+    gwo[...] = t_mm(crossed[...], g_cb[...]).astype(BF16)
+
+
 def cross_back_kernel(
-    shape, cq, ck, cv, do, o, lse, p_1, p_2, out_rows,
-    dq, dk, dv, s_1, s_2, my_out, dk_acc, dv_acc, *scratch,
+    shape, shifts, cq, ck, cv, do, o, lse, first_low, hat1, inv1, all_enc, w_in, w_out, att, g_pre2, vec, sums_in, p_2, out_rows,
+    g_in, g_wo, g_enc, g_att, g_pre1, sums, s_2, my_out, dq, dk, dv, g_br, dk_acc, dv_acc, *scratch,
 ):
     sems, scratch = scratch[:3], scratch[3:]
     place, mail = open_kernel(shape, False, True, sems)
     rows, width = cq.shape
-    f_1, sum_1 = fold_stages(mail, place, p_1, scratch[:N_FOLD])
-    f_2, sum_2 = fold_stages(mail, place, p_2, scratch[N_FOLD:])
+    f, sum_2 = fold_stages(mail, place, p_2, scratch[:N_FOLD])
     c = mirror_stages(mail, place, out_rows, my_out)
-    f_1[0]()
+    f[0]()
     blocks, step, pairs = attend_units(rows, width)
     total = blocks * pairs
-    stages = f_2[:1] + c[:1]
-    for k in range(max(len(f_1), len(f_2))):
-        stages += f_1[k + 1 : k + 2] + f_2[k + 1 : k + 2]
-    stages += c[1:]
+    t = lambda x: (x * total) // 12
     hooks = {}
-    for s, stage in enumerate(stages):
-        hooks.setdefault(min((s + 1) * total // len(stages), total - 1), []).append(stage)
+    at_units(hooks, f[1:5] + f[5:], [t(1), t(5), t(7), t(10)] + [total] * len(f[5:]))
+    at_units(hooks, c, [0, total])
 
     def unit(i):
         first = i % blocks == 0
@@ -1015,42 +1180,77 @@
             dk[:, cols] = dk_acc[...].astype(BF16)
             dv[:, cols] = dv_acc[...].astype(BF16)
 
+    last = hooks.pop(total)
     hooked(total, unit, hooks)
-    s_1[...] = sum_1[...]
+    sums[...] = sums_in[...]
+    n, enc_rows, _ = all_enc.shape
+    g_in[0] = t_mm(first_low[...], dq[...]).astype(BF16)
+    flat = all_enc.reshape(n * enc_rows, width)
+    g_in[1] = t_mm(flat[...], dk[...]).astype(BF16)
+    g_in[2] = t_mm(flat[...], dv[...]).astype(BF16)
+    sums[pl.ds(3, 1)] = row_sum(dq[...].astype(F32))
+    sums[pl.ds(4, 1)] = row_sum(dv[...].astype(F32))
+
+    def encoder(i, _):
+        at = pl.ds(pl.multiple_of(i * enc_rows, enc_rows), enc_rows)
+        g_enc[i] = (mm_t(dk[at], w_in[1]) + mm_t(dv[at], w_in[2])).astype(BF16)
+        return 0
+
+    lax.fori_loop(0, n, encoder, 0)
+
+    def back_one(at):
+        g = g_pre2[at] + mm_t(dq[at], w_in[0])
+        hat = hat1[at]
+        sums[pl.ds(shifts, 1)] += row_sum(g * hat)
+        sums[pl.ds(7, 1)] += row_sum(g)
+        back = normed_back(g, vec[pl.ds(shifts, 1)], hat, inv1[at, :1])
+        g_pre1[at] = back
+        low = back.astype(BF16)
+        g_br[at] = low
+        sums[pl.ds(2, 1)] += row_sum(low.astype(F32))
+        g_att[at] = mm_t(low, w_out[0]).astype(BF16)
+
+    by_rows(rows, back_one)
+    g_wo[...] = t_mm(att[...], g_br[...]).astype(BF16)
+    run(last)
     s_2[...] = sum_2[...]
     mail.finish()
 
 
 def self_back_kernel(
-    shape, q, k, v, bias, do, o, lse, z_1, z_2, p_in, p_out, p_enc,
-    dq, dk, dv, o_1, o_2, o_in, o_out, o_enc, dk_acc, dv_acc, *scratch,
+    shape, q, k, v, bias, do, o, lse, z_2, sums_in, p_1, p_in, p_o0, p_o1, p_enc,
+    dq, dk, dv, o_1, o_2, o_in, o_o0, o_o1, o_enc, sums, dk_acc, dv_acc, *scratch,
 ):
     sems, scratch = scratch[:3], scratch[3:]
     place, mail = open_kernel(shape, True, False, sems)
     rows, width = q.shape
-    l_1 = line_stages(mail, place, z_1, scratch[0], o_1)
-    l_2 = line_stages(mail, place, z_2, scratch[1], o_2)
-    f_in, sum_in = fold_stages(mail, place, p_in, scratch[2 : 2 + N_FOLD])
-    f_out, sum_out = fold_stages(mail, place, p_out, scratch[2 + N_FOLD : 2 + 2 * N_FOLD])
-    rest = scratch[2 + 2 * N_FOLD :]
-    l_in = line_stages(mail, place, sum_in, rest[0], o_in)
-    l_out = line_stages(mail, place, sum_out, rest[1], o_out)
-    e = pair_sum_stages(mail, place, p_enc, rest[2:], o_enc)
-    f_in[0]()
-    f_out[0]()
-    l_1[0]()
+    l_2 = line_stages(mail, place, z_2, scratch[0], o_2)
+    f_1, sum_1 = fold_stages(mail, place, p_1, scratch[1 : 1 + N_FOLD])
+    rest = scratch[1 + N_FOLD :]
+    f_in, sum_in = fold_stages(mail, place, p_in, rest[:N_FOLD])
+    f_o0, sum_o0 = fold_stages(mail, place, p_o0, rest[N_FOLD : 2 * N_FOLD])
+    f_o1, sum_o1 = fold_stages(mail, place, p_o1, rest[2 * N_FOLD : 3 * N_FOLD])
+    rest = rest[3 * N_FOLD :]
+    l_1 = line_stages(mail, place, sum_1, rest[0], o_1)
+    l_in = line_stages(mail, place, sum_in, rest[1], o_in)
+    l_o0 = line_stages(mail, place, sum_o0, rest[2], o_o0)
+    l_o1 = line_stages(mail, place, sum_o1, rest[3], o_o1)
+    e = pair_sum_stages(mail, place, p_enc, rest[4:], o_enc)
+    f_w = [functools.partial(run, three) for three in zip(f_in, f_o0, f_o1)]
+    l_w = [functools.partial(run, three) for three in zip(l_in, l_o0, l_o1)]
+    f_1[0]()
+    l_2[0]()
+    e[0]()
     blocks, step, pairs = attend_units(rows, width)
     total = blocks * pairs
-    stages = []
-    tracks = [
-        [f for two in zip(f_in[1:], f_out[1:]) for f in two] + l_in + l_out,
-        l_1[1:] + l_2 + e,
-    ]
-    longest = max(len(t) for t in tracks)
+    t = lambda x: (x * total) // 12
     hooks = {}
-    for t in tracks:
-        for s, stage in enumerate(t):
-            hooks.setdefault(min((s + 1) * total // len(t), total - 1), []).append(stage)
+    more = len(f_1) - 5
+    at_units(hooks, f_1[1:], [t(1), t(4), t(5), t(6)] + [t(6)] * more)
+    at_units(hooks, f_w, [t(1), t(3), t(8), t(9), t(11)] + [t(11)] * more)
+    at_units(hooks, e[1:-1], [t(2)] * 2 + [t(4)] * (len(e) - 4))
+    at_units(hooks, l_2[1:] + l_1[:1] + l_w[:1], [t(4), t(6), t(11)])
+    at_units(hooks, l_1[1:] + e[-1:] + l_w[1:], [total] * 3)
 
     def unit(i):
         @pl.when(i % blocks == 0)
@@ -1067,7 +1267,12 @@
             dk[:, cols] = dk_acc[...].astype(BF16)
             dv[:, cols] = dv_acc[...].astype(BF16)
 
+    last = hooks.pop(total)
     hooked(total, unit, hooks)
+    sums[...] = sums_in[...]
+    sums[pl.ds(0, 1)] = row_sum(dq[...].astype(F32))
+    sums[pl.ds(1, 1)] = row_sum(dv[...].astype(F32))
+    run(last)
     mail.finish()
 
 
@@ -1094,20 +1299,6 @@
     mail.finish()
 
 
-def layer_norm(values, norm_gain, norm_shift):
-    centre = values - jnp.mean(values, axis=-1, keepdims=True)
-    spread = jnp.mean(centre * centre, axis=-1, keepdims=True)
-    return centre * lax.rsqrt(spread + 1e-05) * norm_gain + norm_shift
-
-
-def gelu_exact(values):
-    return 0.5 * values * (1.0 + jax.scipy.special.erf(values * 0.7071067811865476))
-
-
-def col(x):
-    return jnp.sum(x.astype(F32), axis=0)
-
-
 def body(
     tokens, encoded, cotangent, parent, assignment, attn_in, attn_out, ffn_in, ffn_out, shifts, gains, ffn_bias
 ):
@@ -1160,13 +1351,12 @@
     )
     flat = g_small.reshape(devices, -1)
     vec = flat[:, : n_vec * piece].reshape(devices, n_vec, piece).transpose(1, 0, 2)
-    vec = vec.reshape(n_vec, width).astype(F32)
-    shift, gain = vec[:n_shift], vec[n_shift:]
-    b1 = flat[:, n_vec * piece : n_vec * piece + n_bias].reshape(hidden_width).astype(F32)
+    vec = jnp.pad(vec.reshape(n_vec, width).astype(F32), ((0, -n_vec % 8), (0, 0)))
+    b1 = flat[:, n_vec * piece : n_vec * piece + n_bias].reshape(1, hidden_width).astype(F32)
     w_qkv = w_qkv.reshape(three, width, width)
 
     rest_in = attn_in.shape[0] - three
-    q, k, v, attended, self_mass, all_enc, w_in, w_out, z_1, z_2 = kernel_call(
+    q, k, v, attended, self_mass, all_enc, w_in, w_out, w1, z_2 = kernel_call(
         functools.partial(self_kernel, shape),
         "self_attention",
         1,
@@ -1181,7 +1371,7 @@
             sds((paths, enc_rows, width)),
             sds((rest_in, leafs, paths) + attn_in.shape[1:]),
             sds((attn_out.shape[0], leafs, paths) + attn_out.shape[1:]),
-            sds((1, paths) + ffn_in.shape[1:]),
+            sds((1, leafs, paths) + ffn_in.shape[1:]),
             sds((1, paths) + ffn_out.shape[1:]),
         ],
         [VMEM] * 5 + [ANY] * 5,
@@ -1195,52 +1385,60 @@
     primary = (lax.axis_index("leaf") % 2 == 1) == upper
     block = jnp.where(primary, p, paths - 1 - p)
     my_tokens = lax.dynamic_index_in_dim(all_tok, block, 0, False)
-    branch = mm(attended, w_out[0]) + shift[2]
-    first_norm, norm_back_one = jax.vjp(
-        layer_norm, my_tokens.astype(F32) + branch, gain[0], shift[7]
-    )
-    first_low = first_norm.astype(BF16)
-    cq = ((mm(first_low, w_in[0]) + shift[3]) * scale).astype(BF16)
-    ck, cv, crossed, cross_mass, w1, w2, my_cot = kernel_call(
-        functools.partial(cross_kernel, shape),
+    hat1, inv1, first_low, cq, ck, cv, crossed, cross_mass, w2, my_cot = kernel_call(
+        functools.partial(cross_kernel, shape, n_shift),
         "cross_attention",
         2,
-        [cq, all_enc, w_in[1], w_in[2], vec, z_1, z_2, cotangent],
-        [VMEM] * 5 + [ANY] * 3,
+        [attended, all_tok, all_enc, w_in, w_out, vec, z_2, cotangent],
+        [VMEM, ANY] + [VMEM] * 4 + [ANY] * 2,
         [
+            sds((rows, width), F32),
+            sds((rows, 128), F32),
+            sds((rows, width)),
+            sds((rows, width)),
             sds((tree_enc, width)),
             sds((tree_enc, width)),
             sds((rows, width)),
             sds((rows, width), F32),
-            sds((1, leafs, paths) + ffn_in.shape[1:]),
             sds((1, leafs, paths) + ffn_out.shape[1:]),
             sds((rows, width)),
         ],
-        [VMEM] * 4 + [ANY] * 3,
-        mail_scratch(),
+        [VMEM] * 8 + [ANY] * 2,
+        [pltpu.VMEM((rows, width), BF16)] + mail_scratch(),
     )
     w1 = w1.reshape(width, hidden_width)
     w2 = w2.reshape(hidden_width, width)
-    cross_branch = mm(crossed, w_out[1]) + shift[5]
-    second_norm, norm_back_two = jax.vjp(layer_norm, first_norm + cross_branch, gain[1], shift[8])
-    second_low = second_norm.astype(BF16)
-    hidden_pre = mm(second_low, w1) + b1
-    hidden, gelu_back = jax.vjp(gelu_exact, hidden_pre)
-    hidden_low = hidden.astype(BF16)
-    ffn_branch = mm(hidden_low, w2) + shift[6]
-    result, norm_back_three = jax.vjp(layer_norm, second_norm + ffn_branch, gain[2], shift[9])
-    output = result.astype(BF16)
-
-    g_pre3, g_gain3, g_shift9 = norm_back_three(my_cot.astype(F32))
-    g_ffn = g_pre3.astype(BF16)
-    g_w2 = t_mm(hidden_low, g_ffn).astype(BF16)
-    (g_hidden_pre,) = gelu_back(mm_t(g_ffn, w2))
-    g_hidden = g_hidden_pre.astype(BF16)
-    g_w1 = t_mm(second_low, g_hidden).astype(BF16)
-    g_b1 = col(g_hidden)
-    g_pre2, g_gain2, g_shift8 = norm_back_two(g_pre3 + mm_t(g_hidden, w1))
-    g_cb = g_pre2.astype(BF16)
-    g_crossed = mm_t(g_cb, w_out[1]).astype(BF16)
+    vm = lambda s, dtype=BF16: pltpu.VMEM(s, dtype)
+    output, g_w1, g_w2, g_wo1, g_crossed, g_pre2, sums, g_b1 = kernel_call(
+        functools.partial(ffn_kernel, n_shift),
+        "feed_forward",
+        None,
+        [hat1, crossed, w_out, w1, w2, vec, b1, my_cot],
+        [VMEM] * 8,
+        [
+            sds((rows, width)),
+            sds((width, hidden_width)),
+            sds((hidden_width, width)),
+            sds((width, width)),
+            sds((rows, width)),
+            sds((rows, width), F32),
+            sds(vec.shape, F32),
+            sds((1, hidden_width), F32),
+        ],
+        [VMEM] * 8,
+        [
+            vm((rows, width), F32),
+            vm((rows, 128), F32),
+            vm((rows, width)),
+            vm((rows, width), F32),
+            vm((rows, hidden_width), F32),
+            vm((rows, hidden_width)),
+            vm((rows, width), F32),
+            vm((rows, width)),
+            vm((rows, width), F32),
+            vm((rows, width)),
+        ],
+    )
 
     def spread(g):
         return g.reshape(
@@ -1248,45 +1446,41 @@
         )
 
     r1, r2 = ffn_in.shape[1:], ffn_out.shape[1:]
-    g_cq, g_ck, g_cv, s_1, s_2, output = kernel_call(
-        functools.partial(cross_back_kernel, shape),
+    g_rest, g_wo0, g_enc, g_att, g_pre1, sums, s_2, output = kernel_call(
+        functools.partial(cross_back_kernel, shape, n_shift),
         "cross_back",
         3,
-        [cq, ck, cv, g_crossed, crossed, cross_mass, spread(g_w1[None]), spread(g_w2[None]), output],
-        [VMEM] * 6 + [ANY] * 3,
         [
+            cq, ck, cv, g_crossed, crossed, cross_mass, first_low, hat1, inv1, all_enc, w_in, w_out, attended,
+            g_pre2, vec, sums, spread(g_w2[None]), output,
+        ],
+        [VMEM] * 16 + [ANY] * 2,
+        [
+            sds((rest_in, width, width)),
+            sds((width, width)),
+            sds((paths, enc_rows, width)),
             sds((rows, width)),
-            sds((tree_enc, width)),
-            sds((tree_enc, width)),
-            sds((1, paths) + r1),
+            sds((rows, width), F32),
+            sds(vec.shape, F32),
             sds((1, paths) + r2),
             sds((rows, width)),
         ],
-        [VMEM] * 5 + [ANY],
-        [pltpu.VMEM((tree_enc, PAIR), F32)] * 2
+        [VMEM] * 7 + [ANY],
+        [vm((rows, width)), vm((tree_enc, width)), vm((tree_enc, width)), vm((rows, width))]
+        + [pltpu.VMEM((tree_enc, PAIR), F32)] * 2
         + mail_scratch()
-        + fold_scratch(shape, 1, *r1, BF16)
         + fold_scratch(shape, 1, *r2, BF16),
     )
-    flat_enc = all_enc.reshape(tree_enc, width)
-    g_wo1 = t_mm(crossed, g_cb).astype(BF16)
-    g_in3 = t_mm(first_low, g_cq).astype(BF16)
-    g_in4 = t_mm(flat_enc, g_ck).astype(BF16)
-    g_in5 = t_mm(flat_enc, g_cv).astype(BF16)
-    g_enc = (mm_t(g_ck, w_in[1]) + mm_t(g_cv, w_in[2])).astype(BF16)
-    g_pre1, g_gain1, g_shift7 = norm_back_one(g_pre2 + mm_t(g_cq, w_in[0]))
-    g_br = g_pre1.astype(BF16)
-    g_wo0 = t_mm(attended, g_br).astype(BF16)
-    g_att = mm_t(g_br, w_out[0]).astype(BF16)
-    p_in = spread(jnp.stack([g_in3, g_in4, g_in5]))
-    p_out = spread(jnp.stack([g_wo0, g_wo1]))
     ri = attn_in.shape[1:]
-    g_q, g_k, g_v, o_w1, o_w2, o_in, o_out, o_enc = kernel_call(
+    g_q, g_k, g_v, o_w1, o_w2, o_in, o_o0, o_o1, o_enc, sums = kernel_call(
         functools.partial(self_back_kernel, shape),
         "self_back",
         4,
-        [q, k, v, bias, g_att, attended, self_mass, s_1, s_2, p_in, p_out, g_enc.reshape(paths, enc_rows, width)],
-        [VMEM] * 9 + [ANY] * 2 + [VMEM],
+        [
+            q, k, v, bias, g_att, attended, self_mass, s_2, sums, spread(g_w1[None]), spread(g_rest),
+            spread(g_wo0[None]), spread(g_wo1[None]), g_enc,
+        ],
+        [VMEM] * 9 + [ANY] * 4 + [VMEM],
         [
             sds((rows, width)),
             sds((tree_rows, width)),
@@ -1294,18 +1488,23 @@
             sds((1,) + r1, F32),
             sds((1,) + r2, F32),
             sds((rest_in,) + ri, F32),
-            sds((2,) + ri, F32),
+            sds((1,) + ri, F32),
+            sds((1,) + ri, F32),
             sds((enc_rows, width), F32),
+            sds(vec.shape, F32),
         ],
-        [VMEM] * 8,
+        [VMEM] * 10,
         [pltpu.VMEM((tree_rows, PAIR), F32)] * 2
         + mail_scratch()
+        + line_scratch(shape, 1, *r2, BF16)
+        + fold_scratch(shape, 1, *r1, BF16)
+        + fold_scratch(shape, rest_in, *ri, BF16)
+        + fold_scratch(shape, 1, *ri, BF16)
+        + fold_scratch(shape, 1, *ri, BF16)
         + line_scratch(shape, 1, *r1, BF16)
-        + line_scratch(shape, 1, *r2, BF16)
-        + fold_scratch(shape, rest_in, *ri, BF16)
-        + fold_scratch(shape, 2, *ri, BF16)
         + line_scratch(shape, rest_in, *ri, BF16)
-        + line_scratch(shape, 2, *ri, BF16)
+        + line_scratch(shape, 1, *ri, BF16)
+        + line_scratch(shape, 1, *ri, BF16)
         + pair_sum_scratch(shape, enc_rows, width),
     )
     flat_tok = all_tok.reshape(tree_rows, width)
@@ -1317,12 +1516,7 @@
     mine = (jnp.arange(paths) == block)[:, None, None]
     g_tok = jnp.where(mine, g_tok + g_own[None], g_tok).astype(BF16)
 
-    g_vec = jnp.stack(
-        [
-            col(g_q), col(g_v), col(g_br), col(g_cq), col(g_cv), col(g_cb), col(g_ffn),
-            g_shift7, g_shift8, g_shift9, g_gain1, g_gain2, g_gain3,
-        ]
-    )
+    g_vec = sums[:n_vec]
     g_small = jnp.concatenate(
         [
             g_vec.reshape(n_vec, devices, piece).transpose(1, 0, 2).reshape(devices, -1),
@@ -1361,7 +1555,7 @@
         o_tok[None],
         o_enc[None],
         jnp.concatenate([o_qkv, o_in]),
-        o_out,
+        jnp.concatenate([o_o0, o_o1]),
         o_w1[0],
         o_w2[0],
         o_vec[:n_shift],

time: 597 us -> 493 us (0.83)
  matrix products: 74.1 us -> 17.1 us
  local copies, waits for them, and re-layouts: 58.6 us -> 15.8 us
  other arithmetic: 28.2 us -> 14.9 us
  Pallas kernels: 426 us -> 438 us
    dot_general x25 -> x6, matrix products: 74.1 us -> 17.1 us  [dot(): lax.dot_general(x, y, (contract, ((), ())), preferred_element_type=F32)]
    unnamed x102 -> x39, local copies, waits for them, and re-layouts: 28.1 us -> 7.35 us
    another operation x14 -> x0, local copies, waits for them, and re-layouts: 14.6 us -> none  [body(): jnp.stack([col(g_q), col(g_v), col(g_br), col(g_cq), col(g_cv), col(g_cb)...]
    reduce_sum x14 -> x0, other arithmetic: 14.6 us -> none  [the longest x7 7.16 us: col(): return jnp.sum(x.astype(F32), axis=0)]
    pallas_call x6 -> x7, Pallas kernels: 426 us -> 438 us  [kernel_call(): pl.pallas_call(kernel, out_shape=outs, in_specs=in_specs, out_specs=out_s...]
    slice x13 -> x0, local copies, waits for them, and re-layouts: 6.28 us -> none  [the longest x1 3.97 us: body(): w_in[2]]
where the time goes in v3:
time: 493 us; the launch traced here: 487 us
  Pallas kernels  438 us (89%)
  matrix products  17.1 us (3%)
  local copies, waits for them, and re-layouts  15.8 us (3%)
  other arithmetic  14.9 us (3%)
    pallas_call x7, Pallas kernels, kernel_call(): pl.pallas_call(kernel, out_shape=outs, in_specs=in_specs, out_specs=out_s...  438 us
    dot_general x6, matrix products, dot(): lax.dot_general(x, y, (contract, ((), ())), preferred_element_type=F32)  17.1 us

profile of v3, /device:TPU:0, one launch (start us, length us, event | category | flops | bytes accessed | tf_op | source)
XLA Modules:
  0.0 487.1 jit_solution(990272771114316696)
XLA Ops:
  2.8 0.8 reshape.120
  4.9 56.8 %opening.1 = (bf16[4,512,768]{2,1,0:T(8,128)(2,1)}, bf16[1,8,4,16,256]{4,3,2,1,0:T(8,128)(2,1)}, bf16[3,8,4,24,768]{4,3,2,1,0:T(8,128)(2,1)}, bf16[512,2048]{1,0:T(8,128)(2,1)}) custom-call(bf16[512,768]{1,0:T(8,128)(2,1)} %bitcast.87, bf16[1,16,256]{2,1,0:T(8,128)(2,1)} %reshape.121.small, bf16[6,24,768]{2,1,0:T(8,128)(2,1)} %attn_in.3, ...), custom_call_target="tpu_custom_call" | custom-call | tf_op jit(solution)/shard_map/opening/pallas_call | solution.py:792
  61.7 1.0 copy.33
  63.8 86.1 %self_attention.1 = (bf16[512,768]{1,0:T(8,128)(2,1)}, bf16[2048,768]{1,0:T(8,128)(2,1)}, bf16[2048,768]{1,0:T(8,128)(2,1)}, bf16[512,768]{1,0:T(8,128)(2,1)}, f...) custom-call(bf16[4,512,768]{2,1,0:T(8,128)(2,1)} %get-tuple-element., ...), custom_call_target="tpu_custom_call" | custom-call | tf_op jit(solution)/shard_map/self_attention/pallas_call | solution.py:792
  149.8 53.2 %cross_attention.1 = (f32[512,768]{1,0:T(8,128)}, f32[512,128]{1,0:T(8,128)}, bf16[512,768]{1,0:T(8,128)(2,1)}, bf16[512,768]{1,0:T(8,128)(2,1)}, bf16[1024,768]...) custom-call(bf16[512,768]{1,0:T(8,128)(2,1)} %get-tuple-element.67.a, ...), custom_call_target="tpu_custom_call" | custom-call | tf_op jit(solution)/shard_map/cross_attention/pallas_call | solution.py:792
  203.8 35.4 %feed_forward.1 = (bf16[512,768]{1,0:T(8,128)(2,1)}, bf16[768,3072]{1,0:T(8,128)(2,1)}, bf16[3072,768]{1,0:T(8,128)(2,1)}, bf16[768,768]{1,0:T(8,128)(2,1)}, bf1...) custom-call(f32[512,768]{1,0:T(8,128)} %get-tuple-element.75.hat1, ...), custom_call_target="tpu_custom_call" | custom-call | tf_op jit(solution)/shard_map/feed_forward/pallas_call | solution.py:792
  239.2 56.0 %cross_back.1 = (bf16[3,768,768]{2,1,0:T(8,128)(2,1)}, bf16[768,768]{1,0:T(8,128)(2,1)}, bf16[4,256,768]{2,1,0:T(8,128)(2,1)}, bf16[512,768]{1,0:T(8,128)(2,1)},...) custom-call(bf16[512,768]{1,0:T(8,128)(2,1)} %get-tuple-element.72.cq, ...), custom_call_target="tpu_custom_call" | custom-call | tf_op jit(solution)/shard_map/cross_back/pallas_call | solution.py:792
  295.2 93.1 %self_back.1 = (bf16[512,768]{1,0:T(8,128)(2,1)}, bf16[2048,768]{1,0:T(8,128)(2,1)}, bf16[2048,768]{1,0:T(8,128)(2,1)}, f32[1,24,3072]{2,1,0:T(8,128)}, f32[1,96...) custom-call(bf16[512,768]{1,0:T(8,128)(2,1)} %get-tuple-element.89.q, ...), custom_call_target="tpu_custom_call" | custom-call | tf_op jit(solution)/shard_map/self_back/pallas_call | solution.py:792
  388.3 1.6 pad_maximum_fusion.2
  389.9 2.4 fusion.10
  392.6 2.0 convolution_add_fusion.1
  394.5 2.8 fusion.11
  397.3 4.8 convolution_add_fusion
  402.2 5.9 %fusion.p_tok = bf16[4,512,768]{2,1,0:T(8,128)(2,1)} fusion(f32[4,512,768]{2,1,0:T(8,128)} %bitcast.66, f32[512,768]{1,0:T(8,128)} %convolution_add_fusion.1, pred[4]{0:T(512)(128)(4,1)S(1)} %iota_compare_fusion.5), kind=kLoop, calls=%fused_computation.1 | loop fusion | flops 4718592 | bytes 11010052 | tf_op jit(solution)/shard_map/convert_element_type | solution.py:1517
  409.9 0.8 copy.34
  410.7 2.1 convolution_convert_fusion.2
  412.8 2.7 convolution_convert_fusion.1
  415.6 2.7 convolution_convert_fusion
  418.3 2.0 pad_maximum_fusion.p_qkv
  420.3 57.6 %closing.1 = (f32[3,24,768]{2,1,0:T(8,128)}, f32[1,8,256]{2,1,0:T(8,128)}, f32[512,768]{1,0:T(8,128)}) custom-call(bf16[3,2,2,2,4,24,768]{6,5,4,3,2,1,0:T(8,128)(2,1)} %pad_maximum_fusion.p_qkv, f32[1,2,2,2,4,8,256]{6,5,4,3,2,1,0:T(8,128)} %bitcast.82, bf16[4,512,768]{2,1,0:T(8,128)(2,1)} %fusion.p_tok), custom_call_target="tpu_custom_call" | custom-call | tf_op jit(solution)/shard_map/closing/pallas_call | solution.py:792
  477.9 1.9 pad_maximum_fusion.1
  482.5 0.9 copy.41
  483.4 1.1 copy.42
  484.5 0.9 copy.43
  (58 shorter events, 11.5 us)
Async XLA Ops:
  389.9 2.5 copy-start.2
  389.9 2.7 copy-start.3
  392.2 2.3 copy-start.13
  394.5 2.8 copy-start.11
  402.2 6.0 %copy-start.9 = (f32[16,768]{1,0:T(8,128)S(1)}, f32[16,768]{1,0:T(8,128)}, u32[]{:S(2)}) copy-start(f32[16,768]{1,0:T(8,128)} %get-tuple-element.104) | copy-start | bytes 147460
  402.2 6.9 %copy-start.10 = (f32[1,3072]{1,0:T(1,128)S(1)}, f32[1,3072]{1,0:T(1,128)}, u32[]{:S(2)}) copy-start(f32[1,3072]{1,0:T(1,128)} %get-tuple-element.105) | copy-start | bytes 36868
  402.2 8.5 %copy-start = (bf16[4,512,768]{2,1,0:T(8,128)(2,1)S(1)}, bf16[4,512,768]{2,1,0:T(8,128)(2,1)}, u32[]{:S(2)}) copy-start(bf16[4,512,768]{2,1,0:T(8,128)(2,1)} %get-tuple-element.63.all_tok) | copy-start | bytes 9437188
  410.7 2.1 copy-start.14
  412.8 2.7 copy-start.12
  420.3 57.6 %copy-start.8 = (f32[3,24,768]{2,1,0:T(8,128)S(1)}, f32[3,24,768]{2,1,0:T(8,128)}, u32[]{:S(2)}) copy-start(f32[3,24,768]{2,1,0:T(8,128)} %get-tuple-element.110) | copy-start | bytes 663556
  420.3 62.2 %copy-start.4 = (bf16[512,768]{1,0:T(8,128)(2,1)S(1)}, bf16[512,768]{1,0:T(8,128)(2,1)}, u32[]{:S(2)}) copy-start(bf16[512,768]{1,0:T(8,128)(2,1)} %get-tuple-element.88) | copy-start | bytes 2359300
  477.8 5.5 %copy-start.1 = (f32[512,768]{1,0:T(8,128)S(1)}, f32[512,768]{1,0:T(8,128)}, u32[]{:S(2)}) copy-start(f32[512,768]{1,0:T(8,128)} %get-tuple-element.107) | copy-start | bytes 4718596
  477.9 6.6 %copy-start.5 = (f32[256,768]{1,0:T(8,128)S(1)}, f32[256,768]{1,0:T(8,128)}, u32[]{:S(2)}) copy-start(f32[256,768]{1,0:T(8,128)} %get-tuple-element.108) | copy-start | bytes 2359300
  482.5 2.9 copy-start.7
  482.5 3.6 copy-start.6

commit v4 on v3

--- a/solution.py
+++ b/solution.py
@@ -13,7 +13,7 @@
 MESH = pl.DeviceIdType.MESH
 F32 = jnp.float32
 BF16 = jnp.bfloat16
-VMEM_LIMIT = 62 * 1024 * 1024
+VMEM_OF = {"opening": 8}
 ANY = pl.BlockSpec(memory_space=pl.ANY)
 VMEM = pl.BlockSpec(memory_space=pltpu.VMEM)
 
@@ -368,24 +368,29 @@
     return chain(steps)
 
 
-def pair_gather_stages(mail, place, shard, whole):
+def pair_gather_stages(mail, place, shard, whole, pieces=1):
     n, h = place.paths, place.half
-    rows = shard.shape[0] // 2
-    half = lambda ref, u: ref.at[pl.ds(pl.multiple_of(u * rows, rows), rows)]
-    lands, core_lands = mail.new_recv(n), mail.new_recv(n)
+    rows = shard.shape[0] // (2 * pieces)
+    part = lambda ref, u, s: ref.at[pl.ds(pl.multiple_of((u * pieces + s) * rows, rows), rows)]
+    half = lambda ref, u: ref.at[pl.ds(pl.multiple_of(u * pieces * rows, rows), pieces * rows)]
+    lands = [mail.new_recv(n) for _ in range(pieces)]
+    core_lands = mail.new_recv(n)
     own = mail.local(place.primary, shard, whole.at[place.p])
     first = jnp.where(place.c == 0, 0, h)
     edge = jnp.where(place.c == 0, h - 1, h)
     starts = []
-    for u in range(2):
-        for q in range(h):
-            q = first + q
-            to = (place.leaf_at(place.a, place.b, u), q)
-            near = place.primary & jnp.logical_not((q == place.p) & (place.c == u))
-            away = near | (jnp.logical_not(place.primary) & (q == edge))
-            starts.append(
-                mail.send(away, half(shard, u), half(whole.at[place.p], u), to, lands + place.p)
-            )
+    for s in range(pieces):
+        for u in range(2):
+            for q in range(h):
+                q = first + q
+                to = (place.leaf_at(place.a, place.b, u), q)
+                near = place.primary & jnp.logical_not((q == place.p) & (place.c == u))
+                away = near | (jnp.logical_not(place.primary) & (q == edge))
+                starts.append(
+                    mail.send(
+                        away, part(shard, u, s), part(whole.at[place.p], u, s), to, lands[s] + place.p
+                    )
+                )
     k = mail.new_recv()
     mate = whole.at[place.p]
     starts.append(
@@ -394,17 +399,26 @@
     starts.append(own[0])
     stages = [functools.partial(run, starts)]
     outward = place.at_p(place.p - place.inward)
-    for r in range(n):
-        j = place.shard_of_rank(r)
-        item = half(whole.at[j], place.c)
-        got = jnp.logical_not(place.primary & (place.p == j))
-        actions = [mail.hear(got, item, place.at_core(), lands + j)]
-        if r >= h and h > 1:
-            actions.append(mail.send(place.pm > 0, item, item, outward, lands + j))
-        actions.append(
-            mail.send(jnp.logical_not(place.p == j), item, item, place.at_core(), core_lands + j)
-        )
-        stages.append(functools.partial(run, actions))
+    for s in range(pieces):
+        for r in list(range(h, n)) + list(range(h)):
+            j = place.shard_of_rank(r)
+            item = part(whole.at[j], place.c, s)
+            got = jnp.logical_not(place.primary & (place.p == j))
+            actions = [mail.hear(got, item, place.at_core(), lands[s] + j)]
+            if r >= h and h > 1:
+                actions.append(mail.send(place.pm > 0, item, item, outward, lands[s] + j))
+            if s == pieces - 1:
+                whole_half = half(whole.at[j], place.c)
+                actions.append(
+                    mail.send(
+                        jnp.logical_not(place.p == j),
+                        whole_half,
+                        whole_half,
+                        place.at_core(),
+                        core_lands + j,
+                    )
+                )
+            stages.append(functools.partial(run, actions))
     rest = [own[1]]
     rest.append(
         mail.hear(jnp.logical_not(place.primary), half(mate, 1 - place.c), place.at_core(), k)
@@ -798,10 +812,10 @@
         compiler_params=pltpu.CompilerParams(
             collective_id=collective_id,
             has_side_effects=True,
-            vmem_limit_bytes=VMEM_LIMIT,
+            vmem_limit_bytes=VMEM_OF.get(name, 62) * 1024 * 1024,
         )
         if collective_id is not None
-        else pltpu.CompilerParams(vmem_limit_bytes=VMEM_LIMIT),
+        else pltpu.CompilerParams(vmem_limit_bytes=62 * 1024 * 1024),
         name=name,
     )(*ins)
 
@@ -943,8 +957,8 @@
 
 
 def self_kernel(
-    shape, all_tok, w_qkv, vec, bias, enc, attn_in, attn_out, ffn_in, ffn_out,
-    q, k, v, att, lse, all_enc, g_in, g_out, g_1, z_2, *sems,
+    shape, all_tok, w_qkv, vec, bias, enc, attn_in, attn_out, ffn_in,
+    q, k, v, att, lse, all_enc, g_in, g_out, z_1, *sems,
 ):
     place, mail = open_kernel(shape, True, False, sems)
     n, rows, width = all_tok.shape
@@ -954,9 +968,7 @@
     wholes = [g_in, g_out]
     w = block_stages(mail, place, shards, lambda i: [g.at[:, place.leaf, i] for g in wholes])
     w += spread_stages(mail, place, wholes)
-    f = block_stages(mail, place, [ffn_in], lambda i: [g_1.at[:, place.leaf, i]])
-    f += spread_stages(mail, place, [g_1])
-    z = block_stages(mail, place, [ffn_out], lambda i: [z_2.at[:, i]])
+    f = block_stages(mail, place, [ffn_in], lambda i: [z_1.at[:, i]])
     w[0]()
     scale = HEAD**-0.5
     q[...] = ((mm(all_tok[place.block], w_qkv[0]) + vec[pl.ds(0, 1)]) * scale).astype(BF16)
@@ -971,14 +983,10 @@
     units = blocks * pairs
     t = lambda x: n + (x * units) // 12
     hooks, last = {}, n + units
-    at_units(hooks, w[1:3], [t(1)] * 2)
-    at_units(hooks, e[:1], [1])
-    at_units(hooks, f[:1], [2])
-    at_units(hooks, z[:1], [t(1)])
-    at_units(hooks, w[3:5] + w[5:-1], [t(4), t(6)] + [t(7)] * len(w[5:-1]))
-    at_units(hooks, e[1:-1], [t(3)] * len(e[1:3]) + [t(8)] * len(e[3:-1]))
-    at_units(hooks, f[1:5] + f[5:-1], [t(6), t(6), t(10), t(11)] + [last] * len(f[5:-1]))
-    at_units(hooks, e[-1:] + w[-1:] + f[-1:] + z[1:], [last] * 4)
+    at_units(hooks, f[:1], [t(2)])
+    at_units(hooks, w[1:5] + w[5:-1], [t(3), t(3), t(6), t(8)] + [t(11)] * len(w[5:-1]))
+    at_units(hooks, e[:1] + f[1:], [t(7), t(9)])
+    at_units(hooks, w[-1:] + e[1:], [last] * len(e))
     early = {at: stages for at, stages in hooks.items() if at < n}
     late = {at - n: stages for at, stages in hooks.items() if at >= n}
     hooked(n, project, early)
@@ -1022,18 +1030,20 @@
 
 
 def cross_kernel(
-    shape, shifts, att, all_tok, all_enc, w_in, w_out, vec, z_2, cot,
-    hat1, inv1, first_low, cq, ck, cv, crossed, lse, g_2, my_cot, toks, *sems,
+    shape, shifts, att, all_tok, all_enc, w_in, w_out, vec, z_1, ffn_out, cot,
+    hat1, inv1, first_low, cq, ck, cv, crossed, lse, g_1, g_2, my_cot, toks, *sems,
 ):
-    place, mail = open_kernel(shape, False, True, sems)
+    place, mail = open_kernel(shape, True, True, sems)
     rows, width = cq.shape
     n, enc_rows, _ = all_enc.shape
-    w = spread_stages(mail, place, [g_2], [z_2])
+    f = spread_stages(mail, place, [g_1], [z_1])
+    w = block_stages(mail, place, [ffn_out], lambda i: [g_2.at[:, place.leaf, i]])
+    w += spread_stages(mail, place, [g_2])
     c = mirror_stages(mail, place, cot, my_cot)
     mine = mail.local(None, all_tok.at[place.block], toks)
     mine[0]()
     w[0]()
-    c[0]()
+    f[0]()
 
     def project(i):
         x = all_enc[i]
@@ -1042,6 +1052,8 @@
         cv[at] = (mm(x, w_in[2]) + vec[pl.ds(4, 1)]).astype(BF16)
 
     hooked(n, project, {})
+    f[1]()
+    c[0]()
     mine[1]()
     scale = HEAD**-0.5
 
@@ -1059,7 +1071,8 @@
     total = blocks * pairs
     t = lambda x: (x * total) // 12
     late = {}
-    at_units(late, w[1:], [t(1), t(4), t(5)] + [total] * (len(w) - 4))
+    at_units(late, f[2:], [t(4)] + [t(6)] * (len(f) - 4) + [total])
+    at_units(late, w[1:], [t(4), t(4), t(10)] + [total] * (len(w) - 4))
     at_units(late, c[1:], [total])
 
     def unit(i):
@@ -1147,21 +1160,27 @@
 
 
 def cross_back_kernel(
-    shape, shifts, cq, ck, cv, do, o, lse, first_low, hat1, inv1, all_enc, w_in, w_out, att, g_pre2, vec, sums_in, p_2, out_rows,
-    g_in, g_wo, g_enc, g_att, g_pre1, sums, s_2, my_out, dq, dk, dv, g_br, dk_acc, dv_acc, *scratch,
+    shape, shifts, cq, ck, cv, do, o, lse, first_low, hat1, inv1, all_enc, w_in, w_out, att, g_pre2, vec, sums_in, p_1, p_2, out_rows,
+    g_in, g_wo, g_enc, g_att, g_pre1, sums, s_1, o_2, my_out, dq, dk, dv, g_br, dk_acc, dv_acc, *scratch,
 ):
     sems, scratch = scratch[:3], scratch[3:]
-    place, mail = open_kernel(shape, False, True, sems)
+    place, mail = open_kernel(shape, True, True, sems)
     rows, width = cq.shape
-    f, sum_2 = fold_stages(mail, place, p_2, scratch[:N_FOLD])
+    f_2, sum_2 = fold_stages(mail, place, p_2, scratch[:N_FOLD])
+    f_1, sum_1 = fold_stages(mail, place, p_1, scratch[N_FOLD : 2 * N_FOLD])
+    l_2 = line_stages(mail, place, sum_2, scratch[2 * N_FOLD], o_2)
     c = mirror_stages(mail, place, out_rows, my_out)
-    f[0]()
+    f_2[0]()
+    c[0]()
     blocks, step, pairs = attend_units(rows, width)
     total = blocks * pairs
     t = lambda x: (x * total) // 12
     hooks = {}
-    at_units(hooks, f[1:5] + f[5:], [t(1), t(5), t(7), t(10)] + [total] * len(f[5:]))
-    at_units(hooks, c, [0, total])
+    more = len(f_1) - 5
+    at_units(hooks, f_2[1:], [t(2), t(6), t(7), t(11)] + [t(11)] * more)
+    at_units(hooks, l_2, [t(11), total + 6])
+    at_units(hooks, f_1, [t(3), t(7), total, total + 2, total + 6] + [total + 6] * more)
+    at_units(hooks, c[1:], [total + 6])
 
     def unit(i):
         first = i % blocks == 0
@@ -1180,23 +1199,27 @@
             dk[:, cols] = dk_acc[...].astype(BF16)
             dv[:, cols] = dv_acc[...].astype(BF16)
 
-    last = hooks.pop(total)
+    late = {at: hooks.pop(at) for at in list(hooks) if at >= total}
     hooked(total, unit, hooks)
-    sums[...] = sums_in[...]
     n, enc_rows, _ = all_enc.shape
-    g_in[0] = t_mm(first_low[...], dq[...]).astype(BF16)
     flat = all_enc.reshape(n * enc_rows, width)
-    g_in[1] = t_mm(flat[...], dk[...]).astype(BF16)
-    g_in[2] = t_mm(flat[...], dv[...]).astype(BF16)
-    sums[pl.ds(3, 1)] = row_sum(dq[...].astype(F32))
-    sums[pl.ds(4, 1)] = row_sum(dv[...].astype(F32))
+
+    def query_grads():
+        sums[...] = sums_in[...]
+        sums[pl.ds(3, 1)] = row_sum(dq[...].astype(F32))
+        sums[pl.ds(4, 1)] = row_sum(dv[...].astype(F32))
+        g_in[0] = t_mm(first_low[...], dq[...]).astype(BF16)
+
+    def key_grads():
+        g_in[1] = t_mm(flat[...], dk[...]).astype(BF16)
+
+    def value_grads():
+        g_in[2] = t_mm(flat[...], dv[...]).astype(BF16)
 
     def encoder(i, _):
         at = pl.ds(pl.multiple_of(i * enc_rows, enc_rows), enc_rows)
         g_enc[i] = (mm_t(dk[at], w_in[1]) + mm_t(dv[at], w_in[2])).astype(BF16)
         return 0
-
-    lax.fori_loop(0, n, encoder, 0)
 
     def back_one(at):
         g = g_pre2[at] + mm_t(dq[at], w_in[0])
@@ -1210,47 +1233,55 @@
         sums[pl.ds(2, 1)] += row_sum(low.astype(F32))
         g_att[at] = mm_t(low, w_out[0]).astype(BF16)
 
-    by_rows(rows, back_one)
-    g_wo[...] = t_mm(att[...], g_br[...]).astype(BF16)
-    run(last)
-    s_2[...] = sum_2[...]
+    def out_grads():
+        g_wo[...] = t_mm(att[...], g_br[...]).astype(BF16)
+
+    steps = [
+        query_grads,
+        key_grads,
+        value_grads,
+        lambda: lax.fori_loop(0, n, encoder, 0),
+        lambda: by_rows(rows, back_one),
+        out_grads,
+    ]
+    for at, step_of in enumerate(steps):
+        run(late.get(total + at, []))
+        step_of()
+    run(late[total + len(steps)])
+    s_1[...] = sum_1[...]
     mail.finish()
 
 
 def self_back_kernel(
-    shape, q, k, v, bias, do, o, lse, z_2, sums_in, p_1, p_in, p_o0, p_o1, p_enc,
-    dq, dk, dv, o_1, o_2, o_in, o_o0, o_o1, o_enc, sums, dk_acc, dv_acc, *scratch,
+    shape, q, k, v, bias, do, o, lse, z_1, sums_in, all_tok, p_in, p_o0, p_o1, p_enc,
+    dq, dk, dv, g_qkv, o_1, o_in, o_o0, o_o1, o_enc, sums, dk_acc, dv_acc, *scratch,
 ):
     sems, scratch = scratch[:3], scratch[3:]
     place, mail = open_kernel(shape, True, False, sems)
     rows, width = q.shape
-    l_2 = line_stages(mail, place, z_2, scratch[0], o_2)
-    f_1, sum_1 = fold_stages(mail, place, p_1, scratch[1 : 1 + N_FOLD])
-    rest = scratch[1 + N_FOLD :]
+    l_1 = line_stages(mail, place, z_1, scratch[0], o_1)
+    rest = scratch[1:]
     f_in, sum_in = fold_stages(mail, place, p_in, rest[:N_FOLD])
     f_o0, sum_o0 = fold_stages(mail, place, p_o0, rest[N_FOLD : 2 * N_FOLD])
     f_o1, sum_o1 = fold_stages(mail, place, p_o1, rest[2 * N_FOLD : 3 * N_FOLD])
     rest = rest[3 * N_FOLD :]
-    l_1 = line_stages(mail, place, sum_1, rest[0], o_1)
-    l_in = line_stages(mail, place, sum_in, rest[1], o_in)
-    l_o0 = line_stages(mail, place, sum_o0, rest[2], o_o0)
-    l_o1 = line_stages(mail, place, sum_o1, rest[3], o_o1)
-    e = pair_sum_stages(mail, place, p_enc, rest[4:], o_enc)
+    l_in = line_stages(mail, place, sum_in, rest[0], o_in)
+    l_o0 = line_stages(mail, place, sum_o0, rest[1], o_o0)
+    l_o1 = line_stages(mail, place, sum_o1, rest[2], o_o1)
+    e = pair_sum_stages(mail, place, p_enc, rest[3:], o_enc)
     f_w = [functools.partial(run, three) for three in zip(f_in, f_o0, f_o1)]
     l_w = [functools.partial(run, three) for three in zip(l_in, l_o0, l_o1)]
-    f_1[0]()
-    l_2[0]()
-    e[0]()
+    f_w[0]()
+    l_1[0]()
     blocks, step, pairs = attend_units(rows, width)
     total = blocks * pairs
     t = lambda x: (x * total) // 12
     hooks = {}
-    more = len(f_1) - 5
-    at_units(hooks, f_1[1:], [t(1), t(4), t(5), t(6)] + [t(6)] * more)
-    at_units(hooks, f_w, [t(1), t(3), t(8), t(9), t(11)] + [t(11)] * more)
-    at_units(hooks, e[1:-1], [t(2)] * 2 + [t(4)] * (len(e) - 4))
-    at_units(hooks, l_2[1:] + l_1[:1] + l_w[:1], [t(4), t(6), t(11)])
-    at_units(hooks, l_1[1:] + e[-1:] + l_w[1:], [total] * 3)
+    more = len(f_w) - 5
+    at_units(hooks, f_w[1:], [t(1), t(4), t(5), t(7)] + [t(7)] * more)
+    at_units(hooks, e[:-1], [t(2)] + [t(3)] * 2 + [t(4)] * (len(e) - 4))
+    at_units(hooks, l_1[1:] + l_w[:1], [t(5), t(7)])
+    at_units(hooks, e[-1:] + l_w[1:], [total] * 2)
 
     def unit(i):
         @pl.when(i % blocks == 0)
@@ -1272,11 +1303,15 @@
     sums[...] = sums_in[...]
     sums[pl.ds(0, 1)] = row_sum(dq[...].astype(F32))
     sums[pl.ds(1, 1)] = row_sum(dv[...].astype(F32))
+    flat = all_tok.reshape(k.shape[0], width)
+    g_qkv[0] = t_mm(all_tok[place.block], dq[...]).astype(BF16)
+    g_qkv[1] = t_mm(flat[...], dk[...]).astype(BF16)
+    g_qkv[2] = t_mm(flat[...], dv[...]).astype(BF16)
     run(last)
     mail.finish()
 
 
-def closing_kernel(shape, p_qkv, p_small, p_tok, o_qkv, o_small, o_tok, *scratch):
+def closing_kernel(shape, p_qkv, p_small, dq, dk, dv, w_qkv, g_pre1, o_qkv, o_small, o_tok, p_tok, *scratch):
     sems, scratch = scratch[:3], scratch[3:]
     place, mail = open_kernel(shape, True, False, sems)
     f_q, sum_q = fold_stages(mail, place, p_qkv, scratch[:N_FOLD])
@@ -1287,15 +1322,40 @@
     t = pair_sum_stages(mail, place, p_tok, rest[2:], o_tok)
     a = [functools.partial(run, two) for two in zip(f_q, f_s)]
     b = [functools.partial(run, two) for two in zip(l_q, l_s)]
+    n, rows, width = p_tok.shape
+    step = min(128, rows)
+
+    def terms(r):
+        j = place.shard_of_rank(r)
+
+        def some(i, _):
+            at = pl.ds(pl.multiple_of(i * step, step), step)
+            far = pl.ds(pl.multiple_of(j * rows + i * step, step), step)
+            total = mm_t(dk[far], w_qkv[1]) + mm_t(dv[far], w_qkv[2])
+            p_tok[j, at] = total.astype(BF16)
+
+            @pl.when(j == place.block)
+            def _():
+                own = g_pre1[at] + mm_t(dq[at], w_qkv[0])
+                p_tok[j, at] = (total + own).astype(BF16)
+
+            return 0
+
+        lax.fori_loop(0, rows // step, some, 0)
+
     a[0]()
+    terms(n - 1)
     t[0]()
-    tracks = [a[1:], t[1:]]
-    for k in range(max(len(x) for x in tracks)):
-        for x in tracks:
-            if k < len(x) and x[k] is not t[-1]:
-                x[k]()
-    run(b)
+    for k in range(1, n):
+        terms(n - 1 - k)
+        t[k]()
+        if k < len(a):
+            a[k]()
+    run(a[n:])
+    run(b[:1])
+    run(t[n:-1])
     t[-1]()
+    run(b[1:])
     mail.finish()
 
 
@@ -1356,12 +1416,12 @@
     w_qkv = w_qkv.reshape(three, width, width)
 
     rest_in = attn_in.shape[0] - three
-    q, k, v, attended, self_mass, all_enc, w_in, w_out, w1, z_2 = kernel_call(
+    q, k, v, attended, self_mass, all_enc, w_in, w_out, z_1 = kernel_call(
         functools.partial(self_kernel, shape),
         "self_attention",
         1,
-        [all_tok, w_qkv, vec, bias, encoded, attn_in, attn_out, ffn_in, ffn_out],
-        [VMEM] * 4 + [ANY] * 5,
+        [all_tok, w_qkv, vec, bias, encoded, attn_in, attn_out, ffn_in],
+        [VMEM] * 4 + [ANY] * 4,
         [
             sds((rows, width)),
             sds((tree_rows, width)),
@@ -1371,26 +1431,20 @@
             sds((paths, enc_rows, width)),
             sds((rest_in, leafs, paths) + attn_in.shape[1:]),
             sds((attn_out.shape[0], leafs, paths) + attn_out.shape[1:]),
-            sds((1, leafs, paths) + ffn_in.shape[1:]),
-            sds((1, paths) + ffn_out.shape[1:]),
+            sds((1, paths) + ffn_in.shape[1:]),
         ],
-        [VMEM] * 5 + [ANY] * 5,
+        [VMEM] * 5 + [ANY] * 4,
         mail_scratch(),
     )
     w_in = w_in.reshape(rest_in, width, width)
     w_out = w_out.reshape(attn_out.shape[0], width, width)
 
-    p = lax.axis_index("path")
-    upper = p >= shape.half
-    primary = (lax.axis_index("leaf") % 2 == 1) == upper
-    block = jnp.where(primary, p, paths - 1 - p)
-    my_tokens = lax.dynamic_index_in_dim(all_tok, block, 0, False)
-    hat1, inv1, first_low, cq, ck, cv, crossed, cross_mass, w2, my_cot = kernel_call(
+    hat1, inv1, first_low, cq, ck, cv, crossed, cross_mass, w1, w2, my_cot = kernel_call(
         functools.partial(cross_kernel, shape, n_shift),
         "cross_attention",
         2,
-        [attended, all_tok, all_enc, w_in, w_out, vec, z_2, cotangent],
-        [VMEM, ANY] + [VMEM] * 4 + [ANY] * 2,
+        [attended, all_tok, all_enc, w_in, w_out, vec, z_1, ffn_out, cotangent],
+        [VMEM, ANY] + [VMEM] * 4 + [ANY] * 3,
         [
             sds((rows, width), F32),
             sds((rows, 128), F32),
@@ -1400,10 +1454,11 @@
             sds((tree_enc, width)),
             sds((rows, width)),
             sds((rows, width), F32),
+            sds((1, leafs, paths) + ffn_in.shape[1:]),
             sds((1, leafs, paths) + ffn_out.shape[1:]),
             sds((rows, width)),
         ],
-        [VMEM] * 8 + [ANY] * 2,
+        [VMEM] * 8 + [ANY] * 3,
         [pltpu.VMEM((rows, width), BF16)] + mail_scratch(),
     )
     w1 = w1.reshape(width, hidden_width)
@@ -1446,15 +1501,15 @@
         )
 
     r1, r2 = ffn_in.shape[1:], ffn_out.shape[1:]
-    g_rest, g_wo0, g_enc, g_att, g_pre1, sums, s_2, output = kernel_call(
+    g_rest, g_wo0, g_enc, g_att, g_pre1, sums, s_1, o_w2, output = kernel_call(
         functools.partial(cross_back_kernel, shape, n_shift),
         "cross_back",
         3,
         [
             cq, ck, cv, g_crossed, crossed, cross_mass, first_low, hat1, inv1, all_enc, w_in, w_out, attended,
-            g_pre2, vec, sums, spread(g_w2[None]), output,
+            g_pre2, vec, sums, spread(g_w1[None]), spread(g_w2[None]), output,
         ],
-        [VMEM] * 16 + [ANY] * 2,
+        [VMEM] * 16 + [ANY] * 3,
         [
             sds((rest_in, width, width)),
             sds((width, width)),
@@ -1462,31 +1517,34 @@
             sds((rows, width)),
             sds((rows, width), F32),
             sds(vec.shape, F32),
-            sds((1, paths) + r2),
+            sds((1, paths) + r1),
+            sds((1,) + r2, F32),
             sds((rows, width)),
         ],
-        [VMEM] * 7 + [ANY],
+        [VMEM] * 8 + [ANY],
         [vm((rows, width)), vm((tree_enc, width)), vm((tree_enc, width)), vm((rows, width))]
         + [pltpu.VMEM((tree_enc, PAIR), F32)] * 2
         + mail_scratch()
-        + fold_scratch(shape, 1, *r2, BF16),
+        + fold_scratch(shape, 1, *r2, BF16)
+        + fold_scratch(shape, 1, *r1, BF16)
+        + line_scratch(shape, 1, *r2, BF16),
     )
     ri = attn_in.shape[1:]
-    g_q, g_k, g_v, o_w1, o_w2, o_in, o_o0, o_o1, o_enc, sums = kernel_call(
+    g_q, g_k, g_v, g_qkv, o_w1, o_in, o_o0, o_o1, o_enc, sums = kernel_call(
         functools.partial(self_back_kernel, shape),
         "self_back",
         4,
         [
-            q, k, v, bias, g_att, attended, self_mass, s_2, sums, spread(g_w1[None]), spread(g_rest),
+            q, k, v, bias, g_att, attended, self_mass, s_1, sums, all_tok, spread(g_rest),
             spread(g_wo0[None]), spread(g_wo1[None]), g_enc,
         ],
-        [VMEM] * 9 + [ANY] * 4 + [VMEM],
+        [VMEM] * 10 + [ANY] * 3 + [VMEM],
         [
             sds((rows, width)),
             sds((tree_rows, width)),
             sds((tree_rows, width)),
+            sds((three, width, width)),
             sds((1,) + r1, F32),
-            sds((1,) + r2, F32),
             sds((rest_in,) + ri, F32),
             sds((1,) + ri, F32),
             sds((1,) + ri, F32),
@@ -1496,26 +1554,15 @@
         [VMEM] * 10,
         [pltpu.VMEM((tree_rows, PAIR), F32)] * 2
         + mail_scratch()
-        + line_scratch(shape, 1, *r2, BF16)
-        + fold_scratch(shape, 1, *r1, BF16)
+        + line_scratch(shape, 1, *r1, BF16)
         + fold_scratch(shape, rest_in, *ri, BF16)
         + fold_scratch(shape, 1, *ri, BF16)
         + fold_scratch(shape, 1, *ri, BF16)
-        + line_scratch(shape, 1, *r1, BF16)
         + line_scratch(shape, rest_in, *ri, BF16)
         + line_scratch(shape, 1, *ri, BF16)
         + line_scratch(shape, 1, *ri, BF16)
         + pair_sum_scratch(shape, enc_rows, width),
     )
-    flat_tok = all_tok.reshape(tree_rows, width)
-    g_in0 = t_mm(my_tokens, g_q).astype(BF16)
-    g_in1 = t_mm(flat_tok, g_k).astype(BF16)
-    g_in2 = t_mm(flat_tok, g_v).astype(BF16)
-    g_tok = (mm_t(g_k, w_qkv[1]) + mm_t(g_v, w_qkv[2])).reshape(paths, rows, width)
-    g_own = g_pre1 + mm_t(g_q, w_qkv[0])
-    mine = (jnp.arange(paths) == block)[:, None, None]
-    g_tok = jnp.where(mine, g_tok + g_own[None], g_tok).astype(BF16)
-
     g_vec = sums[:n_vec]
     g_small = jnp.concatenate(
         [
@@ -1528,20 +1575,20 @@
     g_small_rows = -(-small_count // 2048) * 8
     g_small = jnp.pad(g_small, ((0, 0), (0, g_small_rows * 256 - small_count)))
     p_small = g_small.reshape(1, shape.A, shape.B, 2, paths, g_small_rows, 256)
-    p_qkv = spread(jnp.stack([g_in0, g_in1, g_in2]))
     o_qkv, o_small, o_tok = kernel_call(
         functools.partial(closing_kernel, shape),
         "closing",
         5,
-        [p_qkv, p_small, g_tok],
-        [ANY, ANY, VMEM],
+        [spread(g_qkv), p_small, g_q, g_k, g_v, w_qkv, g_pre1],
+        [ANY, ANY] + [VMEM] * 5,
         [
             sds((three,) + ri, F32),
             sds((1, g_small_rows, 256), F32),
             sds((rows, width), F32),
         ],
         [VMEM] * 3,
-        mail_scratch()
+        [vm((paths, rows, width))]
+        + mail_scratch()
         + fold_scratch(shape, three, *ri, BF16)
         + fold_scratch(shape, 1, g_small_rows, 256, F32)
         + line_scratch(shape, three, *ri, BF16)

time: 493 us -> 471 us (0.955)
  matrix products: 17.1 us -> 0 us
  other arithmetic: 14.9 us -> 6.39 us
    dot_general x6 -> x0, matrix products: 17.1 us -> none  [dot(): lax.dot_general(x, y, (contract, ((), ())), preferred_element_type=F32)]
    convert_element_type x1 -> x0, other arithmetic: 5.93 us -> none  [body(): g_tok = jnp.where(mine, g_tok + g_own[None], g_tok).astype(BF16)]
    unnamed x39 -> x33, local copies, waits for them, and re-layouts: 7.35 us -> 12.9 us
where the time goes in v4:
time: 471 us; the launch traced here: 462 us
  Pallas kernels  435 us (92%)
  local copies, waits for them, and re-layouts  19.2 us (4%)
  other arithmetic  6.39 us (1%)
    pallas_call x7, Pallas kernels, kernel_call(): pl.pallas_call(kernel, out_shape=outs, in_specs=in_specs, out_specs=out_s...  435 us
    unnamed x33, local copies, waits for them, and re-layouts  12.9 us

profile of v4, /device:TPU:0, one launch (start us, length us, event | category | flops | bytes accessed | tf_op | source)
XLA Modules:
  0.0 461.8 jit_solution(13658556330452785468)
XLA Ops:
  0.6 0.7 iota_compare_fusion.2
  1.4 0.8 reshape.98
  2.2 0.8 reshape.99
  2.9 0.7 fusion.4
  3.7 0.9 copy-done.3
  4.6 1.1 copy-done.4
  5.8 54.7 %opening.1 = (bf16[4,512,768]{2,1,0:T(8,128)(2,1)S(1)}, bf16[1,8,4,16,256]{4,3,2,1,0:T(8,128)(2,1)S(1)}, bf16[3,8,4,24,768]{4,3,2,1,0:T(8,128)(2,1)S(1)}, bf16[512,2048]{1,0:T(8,128)(2,1)S(1)}) custom-call(bf16[512,768]{1,0:T(8,128)(2,1)S(1)} %bitcast.39, bf16[1,16,256]{2,1,0:T(8,128)(2,1)S(1)} %reshape.100.small, bf16[6,24,768]{2,1,0:T(8,128)(2,1)S(1)} %copy-done.3, ...), custom_call_target="tpu_custom_call" | custom-call | tf_op jit(solution)/shard_map/opening/pallas_call | solution.py:806
  60.4 1.6 copy-done
  62.1 1.8 copy-done.1
  63.9 1.3 copy-done.2
  66.3 78.4 %self_attention.1 = (bf16[512,768]{1,0:T(8,128)(2,1)}, bf16[2048,768]{1,0:T(8,128)(2,1)}, bf16[2048,768]{1,0:T(8,128)(2,1)}, bf16[512,768]{1,0:T(8,128)(2,1)}, f...) custom-call(bf16[4,512,768]{2,1,0:T(8,128)(2,1)} %copy-done, ...), custom_call_target="tpu_custom_call" | custom-call | tf_op jit(solution)/shard_map/self_attention/pallas_call | solution.py:806
  144.8 58.3 %cross_attention.1 = (f32[512,768]{1,0:T(8,128)}, f32[512,128]{1,0:T(8,128)}, bf16[512,768]{1,0:T(8,128)(2,1)}, bf16[512,768]{1,0:T(8,128)(2,1)}, bf16[1024,768]...) custom-call(bf16[512,768]{1,0:T(8,128)(2,1)} %get-tuple-element.68.a, ...), custom_call_target="tpu_custom_call" | custom-call | tf_op jit(solution)/shard_map/cross_attention/pallas_call | solution.py:806
  203.9 35.5 %feed_forward.1 = (bf16[512,768]{1,0:T(8,128)(2,1)}, bf16[768,3072]{1,0:T(8,128)(2,1)}, bf16[3072,768]{1,0:T(8,128)(2,1)}, bf16[768,768]{1,0:T(8,128)(2,1)}, bf1...) custom-call(f32[512,768]{1,0:T(8,128)} %get-tuple-element.76.hat1, ...), custom_call_target="tpu_custom_call" | custom-call | tf_op jit(solution)/shard_map/feed_forward/pallas_call | solution.py:806
  239.4 65.7 %cross_back.1 = (bf16[3,768,768]{2,1,0:T(8,128)(2,1)}, bf16[768,768]{1,0:T(8,128)(2,1)}, bf16[4,256,768]{2,1,0:T(8,128)(2,1)}, bf16[512,768]{1,0:T(8,128)(2,1)},...) custom-call(bf16[512,768]{1,0:T(8,128)(2,1)} %get-tuple-element.73.c, ...), custom_call_target="tpu_custom_call" | custom-call | tf_op jit(solution)/shard_map/cross_back/pallas_call | solution.py:806
  305.1 72.4 %self_back.1 = (bf16[512,768]{1,0:T(8,128)(2,1)}, bf16[2048,768]{1,0:T(8,128)(2,1)}, bf16[2048,768]{1,0:T(8,128)(2,1)}, bf16[3,768,768]{2,1,0:T(8,128)(2,1)}, f3...) custom-call(bf16[512,768]{1,0:T(8,128)(2,1)} %get-tuple-element.91.q, ...), custom_call_target="tpu_custom_call" | custom-call | tf_op jit(solution)/shard_map/self_back/pallas_call | solution.py:806
  377.6 1.6 pad_maximum_fusion.1
  379.1 1.0 reshape.109
  381.7 0.8 copy.34
  382.5 69.9 %closing.1 = (f32[3,24,768]{2,1,0:T(8,128)}, f32[1,8,256]{2,1,0:T(8,128)}, f32[512,768]{1,0:T(8,128)}) custom-call(bf16[3,2,2,2,4,24,768]{6,5,4,3,2,1,0:T(8,128)(2,1)} %bitcast.51, f32[1,2,2,2,4,8,256]{6,5,4,3,2,1,0:T(8,128)} %bitcast.55, bf16[512,768]{1,0:T(8,128)(2,1)} %get-tuple-element.105.dq, bf16[2048,768]{1,0:T(8,128)(2,1)} %get-tuple-element.106.dk, ...), custom_call_target="tpu_custom_call" | custom-call | tf_op jit(solution)/shard_map/closing/pallas_call | solution.py:806
  452.4 1.8 pad_maximum_fusion
  457.0 0.9 copy.41
  457.9 1.1 copy.42
  459.0 0.9 copy.43
  459.9 0.7 copy.44
  (42 shorter events, 7.0 us)
Async XLA Ops:
  3.7 0.9 copy-start.3
  4.6 1.1 copy-start.4
  60.4 1.6 copy-start
  62.1 1.8 copy-start.1
  63.9 1.3 copy-start.2
  305.1 75.8 %copy-start.11 = (f32[1,3072]{1,0:T(1,128)S(1)}, f32[1,3072]{1,0:T(1,128)}, u32[]{:S(2)}) copy-start(f32[1,3072]{1,0:T(1,128)} %get-tuple-element.104) | copy-start | bytes 36868
  382.5 69.9 %copy-start.10 = (f32[3,24,768]{2,1,0:T(8,128)S(1)}, f32[3,24,768]{2,1,0:T(8,128)}, u32[]{:S(2)}) copy-start(f32[3,24,768]{2,1,0:T(8,128)} %get-tuple-element.112) | copy-start | bytes 663556
  382.5 74.5 %copy-start.6 = (bf16[512,768]{1,0:T(8,128)(2,1)S(1)}, bf16[512,768]{1,0:T(8,128)(2,1)}, u32[]{:S(2)}) copy-start(bf16[512,768]{1,0:T(8,128)(2,1)} %get-tuple-element.90) | copy-start | bytes 2359300
  452.4 5.5 %copy-start.5 = (f32[512,768]{1,0:T(8,128)S(1)}, f32[512,768]{1,0:T(8,128)}, u32[]{:S(2)}) copy-start(f32[512,768]{1,0:T(8,128)} %get-tuple-element.109) | copy-start | bytes 4718596
  457.0 2.0 copy-start.7
  457.9 2.0 copy-start.9
  457.9 2.7 copy-start.8
